TPU v7x, 256 devices: a whole 4x4x8 slice. The times are simulated.
256 devices in a mesh: ctx: 32 (over z_hi, y, x), tp: 8 (over z_lo, core).
Axes of the slice: x: 4, y: 4, z: 8 (z_hi: 2, z_lo: 4; z = z_hi * 4 + z_lo), core: 2. Of those that a mesh axis runs over, the one named last changes fastest.
Arguments:
- query_window: bfloat16 [512, 8192], P(None, 'tp'), may hold values from -200 to 200
- key_cache: bfloat16 [16384, 512], P('ctx'), may hold values from -8 to 8
- value_cache: bfloat16 [16384, 512], P('ctx'), may hold values from -6 to 6
- out_weight: bfloat16 [8192, 4096], P('tp'), may hold values from -0.09375 to 0.09375
- grad_routed: bfloat16 [512, 4096], P('ctx', 'tp'), may hold values from -6 to 6
- token_route: int32 [512], replicated, may hold values from 0 to 511, each once
- window_start: int32 [1], replicated, may hold values from 8192 to 15872
Outputs:
- grad_query: bfloat16 [512, 8192], P('ctx', 'tp')
- grad_keys: bfloat16 [16384, 512], P(('ctx', 'tp'))
- grad_values: bfloat16 [16384, 512], P(('ctx', 'tp'))
Inputs may be any that keep to these rules, and one draw needn't show every extreme that they name: `token_route`: each window token appears once.
All inputs are finite; a program needn't handle non-finite values.
Results may differ from a plain program's by a relative error of at most 0.012.
Values may be sent and summed in bfloat16 or wider, within the bound.
No kernel may reach another device: no remote copies, remote signals or barrier semaphores. Data moves between devices by JAX's collectives and lax.ppermute only.
A program may use at most 320 MiB of HBM per device.

v0:
```python
import math

import jax
import jax.numpy as jnp
from jax import lax
from jax.sharding import PartitionSpec as P

HQ = 64
KVH = 4
HD = 128


NEG_FILL = -1e30


def joined(value, axis, join):
    pieces = jax.tree.map(lambda part: lax.all_gather(part, axis), value)
    head = jax.tree.map(lambda part: part[0], pieces)
    tail = jax.tree.map(lambda part: part[1:], pieces)
    so_far, _ = lax.scan(lambda so_far, slab: (join(so_far, slab), None), head, tail)
    return so_far


def combine_stats(earlier, later_part):
    row_peak = jnp.maximum(earlier[0], later_part[0])
    return (
        row_peak,
        earlier[1] * jnp.exp(earlier[0] - row_peak)
        + later_part[1] * jnp.exp(later_part[0] - row_peak),
    )


def on_device(
    query_window, key_cache, value_cache, out_weight, grad_routed, token_route, window_start
):
    head_size = HD
    group_size = HQ // KVH
    local_heads = query_window.shape[1] // head_size
    kv_local = max(1, local_heads // group_size)
    per_kv = local_heads // kv_local
    window = query_window.shape[0]
    key_span = key_cache.shape[0]
    scale_factor = 1.0 / math.sqrt(head_size)
    tp_index = lax.axis_index("tp")
    ctx_index = lax.axis_index("ctx")
    first_kv = tp_index * local_heads // group_size
    contract = (((1,), (1,)), ((), ()))
    feature_rows = lax.all_gather(grad_routed, "tp", axis=1, tiled=True)
    all_rows = lax.all_gather(feature_rows, "ctx", axis=0, tiled=True)
    routed_heads = lax.dot_general(
        all_rows, out_weight, contract, preferred_element_type=jnp.float32
    ).astype(jnp.bfloat16)
    inverse = (
        jnp.zeros((window,), jnp.int32).at[token_route].set(jnp.arange(window, dtype=jnp.int32))
    )
    token_heads = jnp.take(routed_heads, inverse, axis=0)
    key_heads = lax.dynamic_slice_in_dim(
        key_cache, first_kv * head_size, kv_local * head_size, 1
    ).reshape(key_span, kv_local, head_size)
    value_heads = lax.dynamic_slice_in_dim(
        value_cache, first_kv * head_size, kv_local * head_size, 1
    ).reshape(key_span, kv_local, head_size)
    queries = query_window.reshape(window, kv_local, per_kv, head_size)
    grad_heads = token_heads.reshape(window, kv_local, per_kv, head_size)
    query_pos = window_start[0] + jnp.arange(window, dtype=jnp.int32)
    key_pos = ctx_index * key_span + jnp.arange(key_span, dtype=jnp.int32)
    visible = key_pos[None, :] <= query_pos[:, None]
    scores = (
        jnp.einsum("qgpd,kgd->gpqk", queries, key_heads, preferred_element_type=jnp.float32)
        * scale_factor
    )
    scores = jnp.where(visible, scores, NEG_FILL)
    local_peak = jnp.max(scores, axis=-1)
    weights_local = jnp.where(visible, jnp.exp(scores - local_peak[..., None]), 0.0)
    local_total = jnp.sum(weights_local, axis=-1)
    row_peak, row_total = joined((local_peak, local_total), "ctx", combine_stats)
    attn_probs = (
        jnp.where(visible, jnp.exp(scores - row_peak[..., None]), 0.0) / row_total[..., None]
    )
    grad_probs = jnp.einsum(
        "qgpd,kgd->gpqk", grad_heads, value_heads, preferred_element_type=jnp.float32
    )
    row_delta = lax.psum(jnp.sum(attn_probs * grad_probs, axis=-1), "ctx")
    score_grad = (attn_probs * (grad_probs - row_delta[..., None])).astype(jnp.bfloat16)
    probs_half = attn_probs.astype(jnp.bfloat16)
    query_part = jnp.einsum(
        "gpqk,kgd->qgpd", score_grad, key_heads, preferred_element_type=jnp.float32
    ).reshape(window, local_heads * head_size)
    query_sum = lax.psum_scatter(query_part, "ctx", scatter_dimension=0, tiled=True)
    grad_query = (scale_factor * query_sum).astype(jnp.bfloat16)
    key_part = scale_factor * jnp.einsum(
        "gpqk,qgpd->kgd", score_grad, queries, preferred_element_type=jnp.float32
    ).reshape(key_span, kv_local * head_size)
    value_part = jnp.einsum(
        "gpqk,qgpd->kgd", probs_half, grad_heads, preferred_element_type=jnp.float32
    ).reshape(key_span, kv_local * head_size)
    zero_block = jnp.zeros((key_span, KVH * head_size), jnp.float32)
    key_full = lax.dynamic_update_slice_in_dim(zero_block, key_part, first_kv * head_size, 1)
    value_full = lax.dynamic_update_slice_in_dim(zero_block, value_part, first_kv * head_size, 1)
    key_sum, value_sum = (
        lax.psum_scatter(key_full, "tp", scatter_dimension=0, tiled=True),
        lax.psum_scatter(value_full, "tp", scatter_dimension=0, tiled=True),
    )
    return (grad_query, key_sum.astype(jnp.bfloat16), value_sum.astype(jnp.bfloat16))


def solution(mesh):
    in_specs = (
        P(None, "tp"),
        P("ctx", None),
        P("ctx", None),
        P("tp", None),
        P("ctx", "tp"),
        P(),
        P(),
    )
    out_specs = (P("ctx", "tp"), P(("ctx", "tp"), None), P(("ctx", "tp"), None))
    return jax.shard_map(
        on_device, mesh=mesh, in_specs=in_specs, out_specs=out_specs, check_vma=False
    )
```

profile of v0, /device:TPU:0, one launch (start us, length us, event | category | flops | bytes accessed | tf_op | source)
XLA Modules:
  0.0 798.8 jit_solution(7164521539488544346)
XLA Ops:
  7.2 15.5 %all_gather.22 = bf16[16,4096]{1,0:T(8,128)(2,1)} all-gather(bf16[16,512]{1,0:T(8,128)(2,1)} %param.13), channel_id=1, replica_groups=mesh['ctx'=32,'tp'=8] {'tp'}, dimensions={1}, use_global_device_ids=true | all-gather | bytes 147456 | tf_op jit(solution)/shard_map/all_gather | solution.py:48
  23.7 2.5 fusion.5
  26.2 3.2 copy-done.1
  29.4 2.0 select_reduce_fusion
  31.4 124.3 %all-gather.1 = f32[256,512]{1,0:T(8,128)S(1)} all-gather(f32[8,512]{1,0:T(8,128)S(1)} %select_reduce_fusion), channel_id=3, replica_groups=mesh['ctx'=32,'tp'=8] {'ctx'}, dimensions={0}, use_global_device_ids=true | all-gather | bytes 540672 | tf_op jit(solution)/shard_map/all_gather | solution.py:17
  155.7 2.4 scatter_custom_fusion
  158.2 109.3 %all-gather = f32[256,512]{1,0:T(8,128)S(1)} all-gather(f32[8,512]{1,0:T(8,128)S(1)} %get-tuple-element.45), channel_id=2, replica_groups=mesh['ctx'=32,'tp'=8] {'ctx'}, dimensions={0}, use_global_device_ids=true | all-gather | bytes 540672 | tf_op jit(solution)/shard_map/all_gather | solution.py:17
  267.6 1.4 while.12
  269.1 9.2 %convolution_convert_fusion = bf16[512,1024]{1,0:T(8,128)(2,1)S(1)} fusion(bf16[512,4096]{1,0:T(8,128)(2,1)} %all-gather.4.cloned.1.call-done, bf16[1024,4096]{1,0:T(8,128)(2,1)} %param.12), kind=kOutput, calls=%fused_computation.20 | convolution fusion | flops 4295491584 | bytes 13631488 | tf_op jit(solution)/shard_map/dot_general | solution.py:50
  278.2 2.1 gather_fusion
  280.9 5.4 fusion.10
  286.6 1.0 copy-done.3
  287.9 10.2 %fusion.2 = (f32[8,512]{1,0:T(8,128)S(1)}, f32[512,512,8]{1,0,2:T(8,128)}) fusion(f32[8,512]{1,0:T(8,128)S(1)} %bitcast.119, f32[8,512]{1,0:T(8,128)S(1)} %bitcast.122, f32[512,512,8]{1,0,2:T(8,128)} %copy-done.1, pred[512,512]{0,1:T(8,128)(4,1)S(1)} %broadcast_compare_fusion, bf16[512,8,128]{0,2,1:T(8,128)(2,1)} %bitcast.117, ...), kind=kOutput, calls=%fused_computation.10 | convolution fusion | flops 552071168 | bytes 18268676 | tf_op jit(solution)/shard_map/qgpd,kgd->gpqk/dot_general | solution.py:80
  298.0 216.8 %psum.7 = f32[8,512]{1,0:T(8,128)S(1)} all-reduce(f32[8,512]{1,0:T(8,128)S(1)} %get-tuple-element.47), channel_id=1, replica_groups=mesh['ctx'=32,'tp'=8] {'ctx'}, use_global_device_ids=true, to_apply=%region_6.7 | all-reduce | flops 4096 | bytes 32768 | tf_op jit(solution)/shard_map/psum | solution.py:83
  514.8 7.3 fusion.6
  522.2 1.8 copy-done.2
  524.1 1.2 fusion.14
  526.3 3.0 fusion.25
  529.4 1.9 copy.15
  531.3 1.5 convert_element_type.23
  532.8 27.3 %reduce-scatter.6.cloned.1.call-done = f32[64,512]{1,0:T(8,128)} async-done(((f32[512,512]{1,0:T(8,128)}), f32[64,512]{1,0:T(8,128)}) %reduce-scatter.6.cloned.1.call-update) | async-done | bytes 131088 | tf_op jit(solution)/shard_map/reduce_scatter | solution.py:101
  560.1 1.5 convert_element_type.21
  561.6 229.2 %reduce-scatter.4.cloned.1.call-done = f32[16,1024]{1,0:T(8,128)} async-done(((f32[512,1024]{1,0:T(8,128)}), f32[16,1024]{1,0:T(8,128)}) %reduce-scatter.4.cloned.1.call-update) | async-done | bytes 65552 | tf_op jit(solution)/shard_map/reduce_scatter | solution.py:89
  790.8 1.5 multiply_convert_fusion
  (68 shorter events, 3.4 us)
Async XLA Ops:
  7.2 16.5 %copy-start = (bf16[512,1024]{1,0:T(8,128)(2,1)S(1)}, bf16[512,1024]{1,0:T(8,128)(2,1)}, u32[]{:S(2)}) copy-start(bf16[512,1024]{1,0:T(8,128)(2,1)} %param.9) | copy-start | bytes 3145732
  7.2 261.9 %all-gather.4.cloned.1.call-start = ((), (), s32[]{:S(2)}) async-start(), calls=%async_computation.3 | async-start | bytes 4325376 | tf_op jit(solution)/shard_map/all_gather | solution.py:49
  22.7 508.5 %reduce-scatter.8.cloned.1.call-start = ((), (), s32[]{:S(2)}) async-start(), calls=%async_computation.6 | async-start | bytes 1179648 | tf_op jit(solution)/shard_map/reduce_scatter | solution.py:102
  23.7 132.0 %copy-start.6 = (s32[512]{0:T(512)S(1)}, s32[512]{0:T(512)}, u32[]{:S(2)}) copy-start(s32[512]{0:T(512)} %param.14) | copy-start | bytes 6148
  26.2 3.2 copy-start.1
  280.9 5.5 copy-start.5
  286.6 1.0 copy-start.3
  287.6 272.5 %reduce-scatter.6.cloned.1.call-start = ((), (), s32[]{:S(2)}) async-start(), calls=%async_computation.5 | async-start | bytes 1179648 | tf_op jit(solution)/shard_map/reduce_scatter | solution.py:101
  522.1 1.9 copy-start.2
  525.3 1.0 copy-start.4
  526.3 264.5 %reduce-scatter.4.cloned.1.call-start = ((), (), s32[]{:S(2)}) async-start(), calls=%async_computation.4 | async-start | bytes 2162688 | tf_op jit(solution)/shard_map/reduce_scatter | solution.py:89
Sparse Core Ops, SparseCore 0:
  22.9 113.1 all-gather.3
  287.8 35.7 reduce-scatter.7
  526.4 33.6 reduce-scatter.5
  562.5 228.2 reduce-scatter.3
where the time goes:
time: 799 us
  blocking collectives  466 us (58%)
  waiting for transfers between devices  257 us (32%)
  matrix products  31.5 us (4%)
  other arithmetic  14.8 us (2%)
  between operations  14.7 us (2%)
  local copies, waits for them, and re-layouts  14.3 us (2%)
    all_gather x2, blocking collectives, joined(): pieces = jax.tree.map(lambda part: lax.all_gather(part, axis), value)  234 us
    reduce_scatter x1, waiting for transfers between devices, on_device(): lax.psum_scatter(query_part, 'ctx', scatter_dimension=0, tiled=True)  229 us
    psum x1, blocking collectives, on_device(): row_delta = lax.psum(jnp.sum(attn_probs * grad_probs, axis=-1), 'ctx')  217 us
    reduce_scatter x1, waiting for transfers between devices, on_device(): lax.psum_scatter(key_full, 'tp', scatter_dimension=0, tiled=True)  27.3 us
  transfers between devices with their start and end apart: 4, of which 2 were waited for; matrix products, arithmetic and copies ran while one was open for 4% of the time, Pallas kernels for 0%

commit v1 on v0

v1 whole, which is shorter than its diff:
```python
import functools
import math

import jax
import jax.numpy as jnp
from jax import lax
from jax.experimental import pallas as pl
from jax.experimental.pallas import tpu as pltpu
from jax.sharding import Mesh
from jax.sharding import PartitionSpec as P

HQ = 64
KVH = 4
HD = 128
GROUP = HQ // KVH
SCALE = 1.0 / math.sqrt(HD)
NEG = -1e30
FLOOR = -1e29
LINE = ("zh", "tp")

BF = jnp.bfloat16
F32 = jnp.float32
ROWS = (((1,), (1,)), ((), ()))


def dot(a, b, dims=None):
    if dims is None:
        return jnp.dot(a, b, preferred_element_type=F32)
    return lax.dot_general(a, b, dims, preferred_element_type=F32)


def params(mib):
    return pltpu.CompilerParams(
        vmem_limit_bytes=mib * 1024 * 1024, dimension_semantics=("arbitrary",)
    )


def project_kernel(grad_ref, weight_ref, out_ref, total):
    step = pl.program_id(0)

    @pl.when(step == 0)
    def _():
        total[...] = jnp.zeros_like(total)

    rows = grad_ref.shape[0] * grad_ref.shape[2]
    total[...] += dot(grad_ref[...].reshape(rows, grad_ref.shape[3]), weight_ref[...], ROWS)

    @pl.when(step == pl.num_programs(0) - 1)
    def _():
        out_ref[...] = total[...].astype(BF)


def project(grads, weight):
    lines, parts, rows, width = grads.shape
    heads = weight.shape[0]
    return pl.pallas_call(
        project_kernel,
        grid=(parts,),
        in_specs=[
            pl.BlockSpec((lines, 1, rows, width), lambda i: (0, i, 0, 0)),
            pl.BlockSpec((heads, width), lambda i: (0, i)),
        ],
        out_specs=pl.BlockSpec((lines * rows, heads), lambda i: (0, 0)),
        out_shape=jax.ShapeDtypeStruct((lines * rows, heads), BF),
        scratch_shapes=[pltpu.VMEM((lines * rows, heads), F32)],
        compiler_params=params(24),
        name="project",
    )(grads, weight)


def scores_kernel(place, query_ref, own_ref, other_ref, expo_ref, peak_ref, total_ref):
    head = pl.program_id(0)
    query = query_ref[...]
    span, window = own_ref.shape[0], query.shape[0]
    query_pos = (
        place[3] + place[0] * window + lax.broadcasted_iota(jnp.int32, (1, window), 1)
    )
    scored = []
    for slot, keys in enumerate((own_ref, other_ref)):
        key_pos = place[1 + slot] + lax.broadcasted_iota(jnp.int32, (span, 1), 0)
        raw = dot(keys[...], query, ROWS) * (SCALE * math.log2(math.e))
        scored.append(jnp.where(key_pos <= query_pos, raw, NEG))
    peak = jnp.maximum(
        jnp.max(scored[0], axis=0, keepdims=True), jnp.max(scored[1], axis=0, keepdims=True)
    )
    peak = jnp.maximum(peak, FLOOR)
    total = jnp.zeros_like(peak)
    for slot in range(2):
        expo = jnp.exp2(scored[slot] - peak)
        expo_ref[0, slot] = expo
        total += jnp.sum(expo, axis=0, keepdims=True)
    peak_ref[pl.ds(head, 1), :] = peak
    total_ref[pl.ds(head, 1), :] = total


def scores(place, queries, key_cache, others, half, local_heads):
    span = key_cache.shape[0]
    return pl.pallas_call(
        scores_kernel,
        grid_spec=pltpu.PrefetchScalarGridSpec(
            num_scalar_prefetch=1,
            grid=(local_heads,),
            in_specs=[
                pl.BlockSpec((half, HD), lambda h, p: (p[0], h)),
                pl.BlockSpec((span, HD), lambda h, p: (0, p[4])),
                pl.BlockSpec((span, HD), lambda h, p: (0, 0)),
            ],
            out_specs=[
                pl.BlockSpec((1, 2, span, half), lambda h, p: (h, 0, 0, 0)),
                pl.BlockSpec((local_heads, half), lambda h, p: (0, 0)),
                pl.BlockSpec((local_heads, half), lambda h, p: (0, 0)),
            ],
        ),
        out_shape=[
            jax.ShapeDtypeStruct((local_heads, 2, span, half), F32),
            jax.ShapeDtypeStruct((local_heads, half), F32),
            jax.ShapeDtypeStruct((local_heads, half), F32),
        ],
        compiler_params=params(24),
        cost_estimate=pl.CostEstimate(
            flops=2 * local_heads * 2 * span * half * HD,
            bytes_accessed=4 * local_heads * 2 * span * half,
            transcendentals=local_heads * 2 * span * half,
        ),
        name="scores",
    )(place, queries, key_cache, others)


def delta_kernel(place, route_ref, grad_ref, own_ref, other_ref, expo_ref, out_ref, delta_ref):
    head = pl.program_id(0)
    half, window = out_ref.shape[0], grad_ref.shape[0] * grad_ref.shape[1]
    token = place[0] * half + lax.broadcasted_iota(jnp.int32, (half, window), 0)
    pick = jnp.where(route_ref[...] == token, 1.0, 0.0).astype(BF)
    grad = dot(pick, grad_ref[...].reshape(window, HD)).astype(BF)
    out_ref[...] = grad
    delta = jnp.zeros((1, half), F32)
    for slot, values in enumerate((own_ref, other_ref)):
        delta += jnp.sum(expo_ref[0, slot] * dot(values[...], grad, ROWS), axis=0, keepdims=True)
    delta_ref[pl.ds(head, 1), :] = delta


def deltas(place, route, grads, value_cache, others, expo):
    local_heads, _, span, half = expo.shape
    groups, rows, width = grads.shape
    return pl.pallas_call(
        delta_kernel,
        grid_spec=pltpu.PrefetchScalarGridSpec(
            num_scalar_prefetch=1,
            grid=(local_heads,),
            in_specs=[
                pl.BlockSpec((1, groups * rows), lambda h, p: (0, 0)),
                pl.BlockSpec((groups, rows, HD), lambda h, p: (0, 0, h)),
                pl.BlockSpec((span, HD), lambda h, p: (0, p[4])),
                pl.BlockSpec((span, HD), lambda h, p: (0, 1)),
                pl.BlockSpec((1, 2, span, half), lambda h, p: (h, 0, 0, 0)),
            ],
            out_specs=[
                pl.BlockSpec((half, HD), lambda h, p: (0, h)),
                pl.BlockSpec((local_heads, half), lambda h, p: (0, 0)),
            ],
        ),
        out_shape=[
            jax.ShapeDtypeStruct((half, width), BF),
            jax.ShapeDtypeStruct((local_heads, half), F32),
        ],
        compiler_params=params(24),
        name="deltas",
    )(place, route, grads, value_cache, others, expo)


def grads_kernel(
    place,
    stats_ref,
    peak_ref,
    query_ref,
    grad_ref,
    key_own,
    key_other,
    value_own,
    value_other,
    expo_ref,
    query_out,
    cache_out,
    factor,
    delta,
    keys_turned,
    key_total,
    value_total,
):
    head = pl.program_id(0)

    @pl.when(head == 0)
    def _():
        peaks = stats_ref[:, 0]
        peak = jnp.max(peaks, axis=0)
        weight = jnp.exp2(peaks - peak[None])
        total = jnp.sum(weight * stats_ref[:, 1], axis=0)
        factor[...] = jnp.exp2(peak_ref[...] - peak) / total
        delta[...] = jnp.sum(weight * stats_ref[:, 2], axis=0) / total
        for slot, keys in enumerate((key_own, key_other)):
            keys_turned[slot] = keys[...].astype(F32).T.astype(BF)
        key_total[...] = jnp.zeros_like(key_total)
        value_total[...] = jnp.zeros_like(value_total)

    query, grad = query_ref[...], grad_ref[...]
    row_factor, row_delta = factor[pl.ds(head, 1), :], delta[pl.ds(head, 1), :]
    turned = jnp.zeros((HD, query.shape[0]), F32)
    for slot, values in enumerate((value_own, value_other)):
        probs = expo_ref[0, slot] * row_factor
        score_grad = (probs * (dot(values[...], grad, ROWS) - row_delta)).astype(BF)
        value_total[slot] += dot(probs.astype(BF), grad)
        key_total[slot] += dot(score_grad, query)
        turned += dot(keys_turned[slot], score_grad)
    query_out[...] = (SCALE * turned).T.astype(BF)

    @pl.when(head == pl.num_programs(0) - 1)
    def _():
        parts, rows = cache_out.shape[0] // 2, cache_out.shape[1]
        for slot in range(2):
            line = place[0] if slot == 0 else 1 - place[0]
            where = pl.ds(line * parts, parts)
            cache_out[where, :, :HD] = (
                (SCALE * key_total[slot]).astype(BF).reshape(parts, rows, HD)
            )
            cache_out[where, :, HD:] = value_total[slot].astype(BF).reshape(parts, rows, HD)


def gradients(place, stats, peak, queries, grads, key_cache, value_cache, others, expo, parts):
    local_heads, _, span, half = expo.shape
    groups = stats.shape[0]
    return pl.pallas_call(
        grads_kernel,
        grid_spec=pltpu.PrefetchScalarGridSpec(
            num_scalar_prefetch=1,
            grid=(local_heads,),
            in_specs=[
                pl.BlockSpec((groups, 3, local_heads, half), lambda h, p: (0, 0, 0, 0)),
                pl.BlockSpec((local_heads, half), lambda h, p: (0, 0)),
                pl.BlockSpec((half, HD), lambda h, p: (p[0], h)),
                pl.BlockSpec((half, HD), lambda h, p: (0, h)),
                pl.BlockSpec((span, HD), lambda h, p: (0, p[4])),
                pl.BlockSpec((span, HD), lambda h, p: (0, 0)),
                pl.BlockSpec((span, HD), lambda h, p: (0, p[4])),
                pl.BlockSpec((span, HD), lambda h, p: (0, 1)),
                pl.BlockSpec((1, 2, span, half), lambda h, p: (h, 0, 0, 0)),
            ],
            out_specs=[
                pl.BlockSpec((half, HD), lambda h, p: (0, h)),
                pl.BlockSpec((2 * parts, span // parts, 2 * HD), lambda h, p: (0, 0, 0)),
            ],
            scratch_shapes=[
                pltpu.VMEM((local_heads, half), F32),
                pltpu.VMEM((local_heads, half), F32),
                pltpu.VMEM((2, HD, span), BF),
                pltpu.VMEM((2, span, HD), F32),
                pltpu.VMEM((2, span, HD), F32),
            ],
        ),
        out_shape=[
            jax.ShapeDtypeStruct((half, local_heads * HD), BF),
            jax.ShapeDtypeStruct((2 * parts, span // parts, 2 * HD), BF),
        ],
        compiler_params=params(32),
        name="gradients",
    )(
        place,
        stats,
        peak,
        queries,
        grads,
        key_cache,
        others,
        value_cache,
        others,
        expo,
    )


def to_all(value, axis, count):
    return lax.all_to_all(jnp.broadcast_to(value[None], (count,) + value.shape), axis, 0, 0)


def on_device(
    lines,
    groups,
    parts,
    query_window,
    key_cache,
    value_cache,
    out_weight,
    grad_routed,
    token_route,
    window_start,
):
    window, local_heads = query_window.shape[0], query_window.shape[1] // HD
    half, span, rows = window // lines, key_cache.shape[0], grad_routed.shape[0]
    line, group, part = lax.axis_index("zh"), lax.axis_index("xy"), lax.axis_index("tp")
    kv_head = part * local_heads // GROUP
    first = (line * groups + group) * span
    first_other = ((1 - line) * groups + group) * span
    place = jnp.stack([line, first, first_other, window_start[0], kv_head]).astype(jnp.int32)

    with jax.named_scope("gradient_rows"):
        rows_in = to_all(grad_routed, LINE, lines * parts)
        rows_in = rows_in.reshape(lines, parts, rows, grad_routed.shape[1])
    with jax.named_scope("cache_pair"):
        mine = jnp.concatenate(
            [
                lax.dynamic_slice_in_dim(key_cache, kv_head * HD, HD, 1),
                lax.dynamic_slice_in_dim(value_cache, kv_head * HD, HD, 1),
            ],
            axis=1,
        )
        others = lax.ppermute(mine, "zh", [(0, 1), (1, 0)])
    head_grad = project(rows_in, out_weight)
    with jax.named_scope("head_gradients"):
        gathered = to_all(head_grad, "xy", groups)
    expo, peak, total = scores(place, query_window, key_cache, others, half, local_heads)
    route = token_route.reshape(lines, groups, rows).transpose(1, 0, 2).reshape(1, window)
    grads, delta = deltas(place, route, gathered, value_cache, others, expo)
    with jax.named_scope("row_stats"):
        stats = to_all(jnp.stack([peak, total, delta]), "xy", groups)
    query_part, cache_part = gradients(
        place, stats, peak, query_window, grads, key_cache, value_cache, others, expo, parts
    )
    with jax.named_scope("query_terms"):
        query_terms = lax.all_to_all(
            query_part.reshape(groups, half // groups, query_part.shape[1]), "xy", 0, 0
        )
        grad_query = jnp.sum(query_terms.astype(F32), axis=0).astype(BF)
    with jax.named_scope("cache_terms"):
        cache_terms = lax.all_to_all(cache_part, LINE, 0, 0)
        per_head = parts // KVH
        share = cache_terms.shape[1]
        cache_sum = jnp.sum(
            cache_terms.reshape(lines, KVH, per_head, share, 2, HD).astype(F32), axis=(0, 2)
        ).astype(BF)
        grad_keys = cache_sum[:, :, 0].transpose(1, 0, 2).reshape(share, KVH * HD)
        grad_values = cache_sum[:, :, 1].transpose(1, 0, 2).reshape(share, KVH * HD)
    return grad_query, grad_keys, grad_values


def solution(mesh):
    lines = 2
    groups, parts = mesh.shape["ctx"] // lines, mesh.shape["tp"]
    fine = Mesh(mesh.devices.reshape(lines, groups, parts), ("zh", "xy", "tp"))
    ctx = ("zh", "xy")
    in_specs = (
        P(None, "tp"),
        P(ctx, None),
        P(ctx, None),
        P("tp", None),
        P(ctx, "tp"),
        P(),
        P(),
    )
    out_specs = (P(ctx, "tp"), P(ctx + ("tp",), None), P(ctx + ("tp",), None))
    return jax.shard_map(
        functools.partial(on_device, lines, groups, parts),
        mesh=fine,
        in_specs=in_specs,
        out_specs=out_specs,
        check_vma=False,
    )
```

time: 799 us -> 136 us (0.17)
  the two profiles are of different devices: /device:TPU:0 before, /device:TPU:1 now
where the time goes in v1:
time: 136 us
  blocking collectives  47.9 us (35%)
  waiting for transfers between devices  29.8 us (22%)
  Pallas kernels  23.1 us (17%)
  starting transfers between devices  17.4 us (13%)
  local copies, waits for them, and re-layouts  13.9 us (10%)
  other arithmetic  2.15 us (2%)
  between operations  1.45 us (1%)
    all_to_all x2, blocking collectives, to_all(): lax.all_to_all(jnp.broadcast_to(value[None], (count,) + value.shape), axi...  36.3 us
    all_to_all x1, waiting for transfers between devices, on_device(): cache_terms = lax.all_to_all(cache_part, LINE, 0, 0)  16.6 us
    ppermute x1, waiting for transfers between devices, on_device(): others = lax.ppermute(mine, 'zh', [(0, 1), (1, 0)])  13.2 us
    all_to_all x1, blocking collectives, on_device(): lax.all_to_all(query_part.reshape(groups, half // groups, query_part.shap...  11.6 us
    unnamed x16, local copies, waits for them, and re-layouts  9.99 us
    all_to_all x1, starting transfers between devices, on_device(): cache_terms = lax.all_to_all(cache_part, LINE, 0, 0)  9.71 us
    pallas_call x1, Pallas kernels, gradients(): pl.pallas_call(grads_kernel, grid_spec=pltpu.PrefetchScalarGridSpec(num_s...  8.9 us
    all_to_all x1, starting transfers between devices, to_all(): lax.all_to_all(jnp.broadcast_to(value[None], (count,) + value.shape), axi...  6.75 us
  transfers between devices with their start and end apart: 3, of which 2 were waited for; matrix products, arithmetic and copies ran while one was open for 1% of the time, Pallas kernels for 4%

profile of v1, /device:TPU:1, one launch (start us, length us, event | category | flops | bytes accessed | tf_op | source)
XLA Modules:
  0.0 135.7 jit_solution(6887902957109736302)
XLA Ops:
  0.7 0.8 broadcast_in_dim.6
  1.4 21.5 %all_to_all.25 = bf16[16,16,512]{2,1,0:T(8,128)(2,1)S(1)} all-to-all(bf16[16,16,512]{2,1,0:T(8,128)(2,1)S(1)} %broadcast_in_dim.6), channel_id=1, replica_groups=mesh['zh'=2,'xy'=16,'tp'=8] {'zh','tp'}, dimensions={0} | all-to-all | bytes 524288 | tf_op jit(solution)/shard_map/gradient_rows/all_to_all | solution.py:280
  22.9 3.4 %copy-done.3 = bf16[1024,4096]{1,0:T(8,128)(2,1)S(1)} copy-done((bf16[1024,4096]{1,0:T(8,128)(2,1)S(1)}, bf16[1024,4096]{1,0:T(8,128)(2,1)}, u32[]{:S(2)}) %copy-start.3) | copy-done | bytes 8388632
  26.3 4.1 %project.1 = bf16[32,1024]{1,0:T(8,128)(2,1)S(1)} custom-call(bf16[2,8,16,512]{3,2,1,0:T(8,128)(2,1)S(1)} %bitcast.26, bf16[1024,4096]{1,0:T(8,128)(2,1)S(1)} %copy-done.3), custom_call_target="tpu_custom_call" | custom-call | tf_op jit(solution)/shard_map/project/pallas_call | solution.py:56
  30.4 1.2 broadcast_in_dim.7
  31.6 6.8 %all-to-all-start.1 = ((bf16[16,32,1024]{2,1,0:T(8,128)(2,1)}), bf16[16,32,1024]{2,1,0:T(8,128)(2,1)S(1)}, u32[]{:S(2)}, u32[]{:S(2)}) async-start(bf16[16,32,1024]{2,1,0:T(8,128)(2,1)} %broadcast_in_dim.7), calls=%async_computation.1 | async-start | bytes 2097152 | tf_op jit(solution)/shard_map/head_gradients/all_to_all | solution.py:280
  38.4 0.7 pad_maximum_fusion
  39.2 0.9 collective-permute-start
  41.0 13.2 %collective-permute-done.other_ref.key_other.value_other = bf16[512,256]{1,0:T(8,128)(2,1)S(1)} collective-permute-done((bf16[512,256]{1,0:T(8,128)(2,1)}, bf16[512,256]{1,0:T(8,128)(2,1)S(1)}, u32[]{:S(2)}, u32[]{:S(2)}) %collective-permute-start) | collective-permute-done | bytes 262176 | tf_op jit(solution)/shard_map/cache_pair/ppermute | solution.py:314
  54.2 5.1 %scores.1 = (f32[8,2,512,256]{3,2,1,0:T(8,128)S(1)}, f32[8,256]{1,0:T(8,128)S(1)}, f32[8,256]{1,0:T(8,128)S(1)}) custom-call(s32[5]{0:T(128)S(1)} %stack.31.place, bf16[512,1024]{1,0:T(8,128)(2,1)S(1)} %copy-done.5, bf16[512,512]{1,0:T(8,128)(2,1)S(1)} %copy-done.6, bf16[512,256]{1,0:T(8,128)(2,1)S(1)} %collective-permute-done.other_ref.key_other.value_other), custom_call_target="tpu_custom_call" | custom-call | flops 536870912 | bytes 8388608 | tf_op jit(solution)/shard_map/scores/pallas_call | solution.py:98
  59.3 3.2 %copy-done = f32[8,2,512,256]{3,2,1,0:T(8,128)} copy-done((f32[8,2,512,256]{3,2,1,0:T(8,128)}, f32[8,2,512,256]{3,2,1,0:T(8,128)S(1)}, u32[]{:S(2)}) %copy-start) | copy-done | bytes 8388632
  62.5 3.4 %copy-done.1 = f32[8,2,512,256]{3,2,1,0:T(8,128)S(1)} copy-done((f32[8,2,512,256]{3,2,1,0:T(8,128)S(1)}, f32[8,2,512,256]{3,2,1,0:T(8,128)}, u32[]{:S(2)}) %copy-start.1) | copy-done | bytes 8388632
  65.9 5.1 %deltas.1 = (bf16[256,1024]{1,0:T(8,128)(2,1)S(1)}, f32[8,256]{1,0:T(8,128)S(1)}) custom-call(s32[5]{0:T(128)S(1)} %stack.31.place, s32[1,512]{1,0:T(1,128)S(1)} %reshape.31.route_ref, bf16[16,32,1024]{2,1,0:T(8,128)(2,1)S(1)} %all-to-all-done.1.grad_ref, bf16[512,512]{1,0:T(8,128)(2,1)S(1)} %copy-done.4, ...), custom_call_target="tpu_custom_call" | custom-call | tf_op jit(solution)/shard_map/deltas/pallas_call | solution.py:145
  71.0 14.8 %all_to_all.26.stats_ref = f32[16,3,8,256]{3,2,1,0:T(8,128)S(1)} all-to-all(f32[16,3,8,256]{3,2,1,0:T(8,128)S(1)} %broadcast_in_dim.8), channel_id=1, replica_groups=mesh['zh'=2,'xy'=16,'tp'=8] {'xy'}, dimensions={0} | all-to-all | bytes 786432 | tf_op jit(solution)/shard_map/row_stats/all_to_all | solution.py:280
  85.9 8.9 %gradients.1 = (bf16[256,1024]{1,0:T(8,128)(2,1)S(1)}, bf16[16,64,256]{2,1,0:T(8,128)(2,1)}) custom-call(s32[5]{0:T(128)S(1)} %stack.31.place, f32[16,3,8,256]{3,2,1,0:T(8,128)S(1)} %all_to_all.26.stats_ref, f32[8,256]{1,0:T(8,128)S(1)} %get-tuple-element.10.peak_ref, bf16[512,1024]{1,0:T(8,128)(2,1)S(1)} %copy-done.5, ...), custom_call_target="tpu_custom_call" | custom-call | tf_op jit(solution)/shard_map/gradients/pallas_call | solution.py:231
  94.8 11.6 %all_to_all.27 = bf16[16,16,1024]{2,1,0:T(8,128)(2,1)S(1)} all-to-all(bf16[16,16,1024]{2,1,0:T(8,128)(2,1)S(1)} %bitcast.27), channel_id=1, replica_groups=mesh['zh'=2,'xy'=16,'tp'=8] {'xy'}, dimensions={0} | all-to-all | bytes 1048576 | tf_op jit(solution)/shard_map/query_terms/all_to_all | solution.py:327
  106.4 9.7 %all-to-all-start.4 = ((bf16[16,64,256]{2,1,0:T(8,128)(2,1)}), bf16[16,64,256]{2,1,0:T(8,128)(2,1)S(1)}, u32[]{:S(2)}, u32[]{:S(2)}) async-start(bf16[16,64,256]{2,1,0:T(8,128)(2,1)} %get-tuple-element.16), calls=%async_computation.4 | async-start | bytes 1048576 | tf_op jit(solution)/shard_map/cache_terms/all_to_all | solution.py:332
  116.1 0.7 reduce_sum.24
  116.8 16.6 %all-to-all-done.4 = bf16[16,64,256]{2,1,0:T(8,128)(2,1)S(1)} async-done(((bf16[16,64,256]{2,1,0:T(8,128)(2,1)}), bf16[16,64,256]{2,1,0:T(8,128)(2,1)S(1)}, u32[]{:S(2)}, u32[]{:S(2)}) %all-to-all-start.4) | async-done | bytes 524320 | tf_op jit(solution)/shard_map/cache_terms/all_to_all | solution.py:332
  133.4 0.1 reshape.34
  133.5 0.7 reduce_sum.25
  134.3 0.2 fusion
  134.5 0.6 copy_bitcast_fusion
  135.1 0.6 copy_bitcast_fusion.1
  (21 shorter events, 0.4 us)
Async XLA Ops:
  0.6 37.7 %copy-start.4 = (bf16[512,512]{1,0:T(8,128)(2,1)S(1)}, bf16[512,512]{1,0:T(8,128)(2,1)}, u32[]{:S(2)}) copy-start(bf16[512,512]{1,0:T(8,128)(2,1)} %value_own.1) | copy-start | bytes 1572868
  0.6 40.1 %copy-start.7 = (s32[512]{0:T(512)S(1)}, s32[512]{0:T(512)}, u32[]{:S(2)}) copy-start(s32[512]{0:T(512)} %param.12) | copy-start | bytes 6148
  22.9 3.4 %copy-start.3 = (bf16[1024,4096]{1,0:T(8,128)(2,1)S(1)}, bf16[1024,4096]{1,0:T(8,128)(2,1)}, u32[]{:S(2)}) copy-start(bf16[1024,4096]{1,0:T(8,128)(2,1)} %weight_ref.1) | copy-start | bytes 25165828
  26.3 12.1 %copy-start.6 = (bf16[512,512]{1,0:T(8,128)(2,1)S(1)}, bf16[512,512]{1,0:T(8,128)(2,1)}, u32[]{:S(2)}) copy-start(bf16[512,512]{1,0:T(8,128)(2,1)} %key_own.1) | copy-start | bytes 1572868
  26.3 27.9 %copy-start.5 = (bf16[512,1024]{1,0:T(8,128)(2,1)S(1)}, bf16[512,1024]{1,0:T(8,128)(2,1)}, u32[]{:S(2)}) copy-start(bf16[512,1024]{1,0:T(8,128)(2,1)} %query_ref.3) | copy-start | bytes 3145732
  31.6 31.0 %all-to-all-start.1 = ((bf16[16,32,1024]{2,1,0:T(8,128)(2,1)}), bf16[16,32,1024]{2,1,0:T(8,128)(2,1)S(1)}, u32[]{:S(2)}, u32[]{:S(2)}) async-start(bf16[16,32,1024]{2,1,0:T(8,128)(2,1)} %broadcast_in_dim.7), calls=%async_computation.1 | async-start | bytes 2097152 | tf_op jit(solution)/shard_map/head_gradients/all_to_all | solution.py:280
  39.2 15.1 %collective-permute-start = (bf16[512,256]{1,0:T(8,128)(2,1)}, bf16[512,256]{1,0:T(8,128)(2,1)S(1)}, u32[]{:S(2)}, u32[]{:S(2)}) collective-permute-start(bf16[512,256]{1,0:T(8,128)(2,1)} %pad_maximum_fusion), channel_id=1, source_target_pairs={{0,128},{128,0},{1,129},{129,1},{2,130},{130,2},{3,131},{131,3},{4... | collective-permute-start | bytes 786440 | tf_op jit(solution)/shard_map/cache_pair/ppermute | solution.py:314
  59.3 3.2 %copy-start = (f32[8,2,512,256]{3,2,1,0:T(8,128)}, f32[8,2,512,256]{3,2,1,0:T(8,128)S(1)}, u32[]{:S(2)}) copy-start(f32[8,2,512,256]{3,2,1,0:T(8,128)S(1)} %get-tuple-element.12.expo_ref) | copy-start | bytes 25165828
  62.5 3.4 %copy-start.1 = (f32[8,2,512,256]{3,2,1,0:T(8,128)S(1)}, f32[8,2,512,256]{3,2,1,0:T(8,128)}, u32[]{:S(2)}) copy-start(f32[8,2,512,256]{3,2,1,0:T(8,128)} %copy-done) | copy-start | bytes 25165828
  65.9 19.9 %copy-start.2 = (f32[8,2,512,256]{3,2,1,0:T(8,128)S(1)}, f32[8,2,512,256]{3,2,1,0:T(8,128)}, u32[]{:S(2)}) copy-start(f32[8,2,512,256]{3,2,1,0:T(8,128)} %copy-done) | copy-start | bytes 25165828
  106.4 27.0 %all-to-all-start.4 = ((bf16[16,64,256]{2,1,0:T(8,128)(2,1)}), bf16[16,64,256]{2,1,0:T(8,128)(2,1)S(1)}, u32[]{:S(2)}, u32[]{:S(2)}) async-start(bf16[16,64,256]{2,1,0:T(8,128)(2,1)} %get-tuple-element.16), calls=%async_computation.4 | async-start | bytes 1048576 | tf_op jit(solution)/shard_map/cache_terms/all_to_all | solution.py:332

commit v2 on v0

v2 whole, which is shorter than its diff:
```python
import functools
import math

import jax
import jax.numpy as jnp
from jax import lax
from jax.experimental import pallas as pl
from jax.experimental.pallas import tpu as pltpu
from jax.sharding import Mesh
from jax.sharding import PartitionSpec as P

HQ = 64
KVH = 4
HD = 128
GROUP = HQ // KVH
SCALE = 1.0 / math.sqrt(HD)
NEG = -1e30
FLOOR = -1e29
VMEM_MIB = 16
LOG2E = math.log2(math.e)

BF = jnp.bfloat16
F32 = jnp.float32
ROWS = (((1,), (1,)), ((), ()))


def dot(a, b, dims=None):
    if dims is None:
        return jnp.dot(a, b, preferred_element_type=F32)
    return lax.dot_general(a, b, dims, preferred_element_type=F32)


VMEM = pl.BlockSpec(memory_space=pltpu.VMEM)
SMEM = pl.BlockSpec(memory_space=pltpu.SMEM)


HBM = pl.BlockSpec(memory_space=pltpu.HBM)


def call(kernel, name, args, outs, scratch=(), cost=None, streamed=(), held=()):
    return pl.pallas_call(
        kernel,
        in_specs=[SMEM] + [HBM if i in streamed else VMEM for i in range(1, len(args))],
        out_specs=[VMEM] * len(outs),
        out_shape=[
            pltpu.VMEM(*out) if i in held else jax.ShapeDtypeStruct(*out)
            for i, out in enumerate(outs)
        ],
        scratch_shapes=list(scratch),
        compiler_params=pltpu.CompilerParams(vmem_limit_bytes=VMEM_MIB * 1024 * 1024),
        cost_estimate=cost,
        name=name,
    )(*args)


def in_hbm(array):
    return pltpu.with_memory_space_constraint(array, pltpu.HBM)


def in_vmem(array):
    return pltpu.with_memory_space_constraint(array, pltpu.VMEM)


LINE, FIRST, FIRST_OTHER, START, KV_HEAD, CORE, BLOCKS = range(7)


def columns(index, width=HD):
    return pl.ds(pl.multiple_of(index * width, width), width)


def project_kernel(place, *refs):
    pieces, weight_ref, out_ref = refs[:-2], refs[-2], refs[-1]
    cores, lines, rows, width = pieces[0].shape
    total = None
    for index in range(len(pieces) * cores):
        piece = pieces[index // cores][index % cores].reshape(lines * rows, width)
        term = dot(weight_ref[:, columns(place[BLOCKS + index], width)], piece, ROWS)
        total = term if total is None else total + term
    result = total.T.astype(BF)
    for copy in range(out_ref.shape[0]):
        out_ref[copy] = result


def other_pair(place, straight, crossed):
    swap = place[CORE] == 1
    first, second = straight[...], crossed[...]
    return jnp.where(swap, second, first), jnp.where(swap, first, second)


def score_heads(place, slot, query_ref, keys, expo_ref, peak_ref, total_ref):
    heads, span, window = expo_ref.shape
    query_pos = place[START] + place[LINE] * window + lax.broadcasted_iota(jnp.int32, (1, window), 1)
    key_pos = place[FIRST + slot] + lax.broadcasted_iota(jnp.int32, (span, 1), 0)

    def one_head(head, _):
        query = query_ref[pl.ds(place[LINE] * window, window), columns(head)]
        scored = dot(keys, query, ROWS) * (SCALE * LOG2E)
        scored = jnp.where(key_pos <= query_pos, scored, NEG)
        peak = jnp.maximum(jnp.max(scored, axis=0, keepdims=True), FLOOR)
        expo = jnp.exp2(scored - peak)
        expo_ref[head] = expo
        peak_ref[pl.ds(head, 1), :] = peak
        total_ref[pl.ds(head, 1), :] = jnp.sum(expo, axis=0, keepdims=True)
        return 0

    lax.fori_loop(0, heads, one_head, 0)


def own_kernel(place, query_ref, key_ref, weight_in, expo_ref, peak_ref, total_ref, weight_out, done):
    copy = pltpu.make_async_copy(weight_in, weight_out, done)
    copy.start()
    keys = key_ref[:, columns(place[KV_HEAD])]
    score_heads(place, 0, query_ref, keys, expo_ref, peak_ref, total_ref)
    copy.wait()


def other_kernel(place, query_ref, straight, crossed, expo_ref, peak_ref, total_ref):
    keys = other_pair(place, straight, crossed)[0]
    score_heads(place, 1, query_ref, keys, expo_ref, peak_ref, total_ref)


def delta_kernel(
    place,
    route_ref,
    gathered_ref,
    value_ref,
    straight,
    crossed,
    expo_own,
    peak_own,
    total_own,
    expo_other,
    peak_other,
    total_other,
    grad_ref,
    stats_ref,
):
    heads, span, half = expo_own.shape
    window = route_ref.shape[1]
    token = place[LINE] * half + lax.broadcasted_iota(jnp.int32, (half, window), 0)
    pick = jnp.where(route_ref[...] == token, 1.0, 0.0).astype(BF)
    values = (value_ref[:, columns(place[KV_HEAD])], other_pair(place, straight, crossed)[1])
    grad_ref[...] = dot(pick, gathered_ref[...].reshape(window, heads * HD)).astype(BF)
    peak = jnp.maximum(peak_own[...], peak_other[...])
    factors = (jnp.exp2(peak_own[...] - peak), jnp.exp2(peak_other[...] - peak))
    stats_ref[0, 0] = peak
    stats_ref[0, 1] = total_own[...] * factors[0] + total_other[...] * factors[1]

    def one_head(head, _):
        grad = grad_ref[:, columns(head)]
        for slot, expo_ref in enumerate((expo_own, expo_other)):
            stats_ref[1 + slot, 2, pl.ds(head, 1), :] = jnp.sum(
                expo_ref[head] * dot(values[slot], grad, ROWS), axis=0, keepdims=True
            )
        return 0

    lax.fori_loop(0, heads, one_head, 0)
    stats_ref[0, 2] = stats_ref[1, 2] * factors[0] + stats_ref[2, 2] * factors[1]
    for copy in range(1, stats_ref.shape[0]):
        stats_ref[copy] = stats_ref[0]


def grads_kernel(
    place,
    stats_ref,
    query_ref,
    grad_ref,
    key_ref,
    value_ref,
    straight,
    crossed,
    expo_own,
    peak_own,
    expo_other,
    peak_other,
    query_out,
    keep_out,
    send_out,
    factor,
    delta,
    keys_turned,
    key_total,
    value_total,
):
    heads, span, half = expo_own.shape
    peaks = stats_ref[:, 0]
    peak = jnp.max(peaks, axis=0)
    weight = jnp.exp2(peaks - peak[None])
    total = jnp.sum(weight * stats_ref[:, 1], axis=0)
    for slot, own_peak in enumerate((peak_own, peak_other)):
        factor[slot] = jnp.exp2(own_peak[...] - peak) / total
    delta[...] = jnp.sum(weight * stats_ref[:, 2], axis=0) / total
    key_other, value_other = other_pair(place, straight, crossed)
    keys = (key_ref[:, columns(place[KV_HEAD])], key_other)
    values = (value_ref[:, columns(place[KV_HEAD])], value_other)
    for slot in range(2):
        keys_turned[slot] = keys[slot].astype(F32).T.astype(BF)
    key_total[...] = jnp.zeros_like(key_total)
    value_total[...] = jnp.zeros_like(value_total)

    def one_head(head, _):
        query = query_ref[pl.ds(place[LINE] * half, half), columns(head)]
        grad = grad_ref[:, columns(head)]
        row_delta = delta[pl.ds(head, 1), :]
        turned = jnp.zeros((HD, half), F32)
        for slot in range(2):
            expo_ref = (expo_own, expo_other)[slot]
            probs = expo_ref[head] * factor[slot, pl.ds(head, 1), :]
            score_grad = (probs * (dot(values[slot], grad, ROWS) - row_delta)).astype(BF)
            value_total[slot] += dot(probs.astype(BF), grad)
            key_total[slot] += dot(score_grad, query)
            turned += dot(keys_turned[slot], score_grad)
        result = (SCALE * turned).T.astype(BF)
        query_out[:, :, columns(head)] = result.reshape(query_out.shape[0], query_out.shape[1], HD)
        return 0

    lax.fori_loop(0, heads, one_head, 0)
    slots, chips, share, _ = keep_out.shape
    for slot in range(2):
        for chip in range(chips):
            for part, sums, scale in ((0, key_total, SCALE), (1, value_total, 1.0)):
                where = slice(part * HD, (part + 1) * HD)
                mine = pl.multiple_of((2 * chip + place[CORE]) * share, share)
                theirs = pl.multiple_of((2 * chip + 1 - place[CORE]) * share, share)
                keep_out[slot, chip, :, where] = scale * sums[slot, pl.ds(mine, share), :]
                send_out[slot, chip, :, where] = (
                    scale * sums[slot, pl.ds(theirs, share), :]
                ).astype(BF)


def on_device(
    lines,
    groups,
    parts,
    query_window,
    key_cache,
    value_cache,
    out_weight,
    grad_routed,
    token_route,
    window_start,
):
    window, local_heads = query_window.shape[0], query_window.shape[1] // HD
    half, span, rows = window // lines, key_cache.shape[0], grad_routed.shape[0]
    chips = parts // 2
    line, group, part = lax.axis_index("zh"), lax.axis_index("xy"), lax.axis_index("tp")
    chip, core = part // 2, part % 2
    kv_head = part * local_heads // GROUP
    pieces = [
        ((chip - step + chips) % chips) * 2 + (core + other) % 2
        for step in range(chips)
        for other in range(2)
    ]
    place = jnp.stack(
        [
            line,
            (line * groups + group) * span,
            ((1 - line) * groups + group) * span,
            window_start[0],
            kv_head,
            core,
        ]
        + pieces
    ).astype(jnp.int32)

    route = token_route.reshape(lines, groups, rows)
    route = jnp.where(line == 0, route, route[::-1]).transpose(1, 0, 2).reshape(1, window)
    out_weight, place, route = lax.optimization_barrier((out_weight, place, route))

    def to_pair(value):
        return lax.ppermute(value, "zh", [(0, 1), (1, 0)])

    def to_core(value):
        return lax.ppermute(value, "tp", [(i, i ^ 1) for i in range(parts)])

    def to_chip(value, step):
        return lax.ppermute(value, "tp", [(i, (i + 2 * step) % parts) for i in range(parts)])

    score_cost = pl.CostEstimate(
        flops=2 * local_heads * span * half * HD,
        bytes_accessed=4 * local_heads * span * half,
        transcendentals=local_heads * span * half,
    )
    score_outs = [
        ((local_heads, span, half), F32),
        ((local_heads, half), F32),
        ((local_heads, half), F32),
    ]
    expo_own, peak_own, total_own, weight = call(
        own_kernel,
        "own_scores",
        (place, query_window, key_cache, in_hbm(out_weight)),
        score_outs + [(out_weight.shape, BF)],
        scratch=[pltpu.SemaphoreType.DMA],
        cost=score_cost,
        streamed=(3,),
        held=(0, 3),
    )
    with jax.named_scope("gradient_rows"):
        other_rows = to_pair(grad_routed)
        other_rows, weight = lax.optimization_barrier((other_rows, weight))
        pair = jnp.stack([grad_routed, other_rows])
        chip_rows = jnp.stack([pair, to_core(pair)])
        all_rows = [chip_rows] + [to_chip(chip_rows, step) for step in range(1, chips)]
    with jax.named_scope("cache_pair"):
        mine = jnp.where(
            core == 0,
            lax.dynamic_slice_in_dim(key_cache, kv_head * HD, HD, 1),
            lax.dynamic_slice_in_dim(value_cache, kv_head * HD, HD, 1),
        )
        straight = to_pair(mine)
        crossed = to_core(straight)
    expo_other, peak_other, total_other = call(
        other_kernel,
        "other_scores",
        (place, query_window, straight, crossed),
        score_outs,
        cost=score_cost,
        held=(0,),
    )
    all_rows, straight, crossed, expo_other, peak_other, total_other = lax.optimization_barrier(
        (all_rows, straight, crossed, expo_other, peak_other, total_other)
    )
    (gathered,) = call(
        project_kernel,
        "project",
        (place, *all_rows, in_vmem(weight)),
        [((groups, lines * rows, local_heads * HD), BF)],
    )
    with jax.named_scope("head_gradients"):
        gathered = lax.all_to_all(gathered, "xy", 0, 0)
    own = (in_vmem(expo_own), peak_own)
    other = (in_vmem(expo_other), peak_other)
    grads, stats = call(
        delta_kernel,
        "deltas",
        (place, route, gathered, value_cache, straight, crossed)
        + own
        + (total_own,)
        + other
        + (total_other,),
        [((half, local_heads * HD), BF), ((groups, 3, local_heads, half), F32)],
    )
    with jax.named_scope("row_stats"):
        stats = lax.all_to_all(stats, "xy", 0, 0)
    share = span // parts
    query_part, keep, send = call(
        grads_kernel,
        "gradients",
        (place, stats, query_window, grads, key_cache, value_cache, straight, crossed) + own + other,
        [
            ((groups, half // groups, local_heads * HD), BF),
            ((2, chips, share, 2 * HD), F32),
            ((2, chips, share, 2 * HD), BF),
        ],
        scratch=[
            pltpu.VMEM((2, local_heads, half), F32),
            pltpu.VMEM((local_heads, half), F32),
            pltpu.VMEM((2, HD, span), BF),
            pltpu.VMEM((2, span, HD), F32),
            pltpu.VMEM((2, span, HD), F32),
        ],
    )
    query_terms = lax.all_to_all(query_part, "xy", 0, 0)
    with jax.named_scope("cache_terms"):
        chip_sum = keep + to_core(send).astype(F32)
        line_sum = chip_sum[0] + to_pair(chip_sum[1].astype(BF)).astype(F32)
        line_sum = line_sum.astype(BF)
        own = lax.dynamic_index_in_dim(line_sum, chip, 0, False)
        arrived = jnp.stack(
            [own]
            + [
                to_chip(lax.dynamic_index_in_dim(line_sum, (chip + step) % chips, 0, False), step)
                for step in range(1, chips)
            ]
        )
        arrived, query_terms = lax.optimization_barrier((arrived, query_terms))
        in_order = [
            lax.dynamic_index_in_dim(arrived, (chip - head + chips) % chips, 0, False)
            for head in range(chips)
        ]
        grad_keys = jnp.concatenate([piece[:, :HD] for piece in in_order], axis=1)
        grad_values = jnp.concatenate([piece[:, HD:] for piece in in_order], axis=1)
    with jax.named_scope("query_terms"):
        grad_query = jnp.sum(query_terms.astype(F32), axis=0).astype(BF)
    return grad_query, grad_keys, grad_values


def solution(mesh):
    lines = 2
    groups, parts = mesh.shape["ctx"] // lines, mesh.shape["tp"]
    fine = Mesh(mesh.devices.reshape(lines, groups, parts), ("zh", "xy", "tp"))
    ctx = ("zh", "xy")
    in_specs = (
        P(None, "tp"),
        P(ctx, None),
        P(ctx, None),
        P("tp", None),
        P(ctx, "tp"),
        P(),
        P(),
    )
    out_specs = (P(ctx, "tp"), P(ctx + ("tp",), None), P(ctx + ("tp",), None))
    return jax.shard_map(
        functools.partial(on_device, lines, groups, parts),
        mesh=fine,
        in_specs=in_specs,
        out_specs=out_specs,
        check_vma=False,
    )
```

time: 799 us -> 104 us (0.13)
  the two profiles are of different devices: /device:TPU:0 before, /device:TPU:1 now
where the time goes in v2:
time: 104 us
  blocking collectives  34.2 us (33%)
  starting transfers between devices  30.3 us (29%)
  Pallas kernels  22.3 us (21%)
  waiting for transfers between devices  8.8 us (8%)
  local copies, waits for them, and re-layouts  3.31 us (3%)
  other arithmetic  3.1 us (3%)
  between operations  1.54 us (1%)
    all_to_all x1, blocking collectives, on_device(): gathered = lax.all_to_all(gathered, 'xy', 0, 0)  22.9 us
    pallas_call x5, Pallas kernels, call(): pl.pallas_call(kernel, in_specs=[SMEM] + [HBM if i in streamed else VMEM...  22.3 us
    ppermute x3, starting transfers between devices, to_pair(): return lax.ppermute(value, 'zh', [(0, 1), (1, 0)])  11.4 us
    all_to_all x1, blocking collectives, on_device(): stats = lax.all_to_all(stats, 'xy', 0, 0)  11.3 us
    ppermute x6, starting transfers between devices, to_chip(): lax.ppermute(value, 'tp', [(i, (i + 2 * step) % parts) for i in range(par...  10.5 us
    ppermute x6, waiting for transfers between devices, to_chip(): lax.ppermute(value, 'tp', [(i, (i + 2 * step) % parts) for i in range(par...  5.45 us
    ppermute x3, starting transfers between devices, to_core(): return lax.ppermute(value, 'tp', [(i, i ^ 1) for i in range(parts)])  4.89 us
    all_to_all x1, starting transfers between devices, on_device(): query_terms = lax.all_to_all(query_part, 'xy', 0, 0)  3.57 us
  transfers between devices with their start and end apart: 13, of which 7 were waited for; matrix products, arithmetic and copies ran while one was open for 2% of the time, Pallas kernels for 7%

profile of v2, /device:TPU:1, one launch (start us, length us, event | category | flops | bytes accessed | tf_op | source)
XLA Modules:
  0.0 103.5 jit_solution(10096525931876076737)
XLA Ops:
  0.6 7.8 %collective-permute-start = (bf16[16,512]{1,0:T(8,128)(2,1)}, bf16[16,512]{1,0:T(8,128)(2,1)S(1)}, u32[]{:S(2)}, u32[]{:S(2)}) collective-permute-start(bf16[16,512]{1,0:T(8,128)(2,1)} %param.11), channel_id=1, source_target_pairs={{0,128},{128,0},{1,129},{129,1},{2,130},{130,2},{3,131},{131,3},{4... | collective-permute-start | bytes 49160 | tf_op jit(solution)/shard_map/gradient_rows/ppermute | solution.py:271
  8.5 1.0 dynamic-slice_select_fusion
  11.3 1.2 %copy-done = bf16[512,1024]{1,0:T(8,128)(2,1)S(1)} copy-done((bf16[512,1024]{1,0:T(8,128)(2,1)S(1)}, bf16[512,1024]{1,0:T(8,128)(2,1)}, u32[]{:S(2)}) %copy-start) | copy-done | bytes 1048600
  12.6 1.0 %copy-done.1 = bf16[512,512]{1,0:T(8,128)(2,1)S(1)} copy-done((bf16[512,512]{1,0:T(8,128)(2,1)S(1)}, bf16[512,512]{1,0:T(8,128)(2,1)}, u32[]{:S(2)}) %copy-start.1) | copy-done | bytes 524312
  13.6 3.9 %own_scores.1 = (f32[8,512,256]{2,1,0:T(8,128)S(1)}, f32[8,256]{1,0:T(8,128)S(1)}, f32[8,256]{1,0:T(8,128)S(1)}, bf16[1024,4096]{1,0:T(8,128)(2,1)S(1)}) custom-call(s32[14]{0:T(128)S(1)} %stack.86.place, bf16[512,1024]{1,0:T(8,128)(2,1)S(1)} %copy-done, bf16[512,512]{1,0:T(8,128)(2,1)S(1)} %copy-done.1, bf16[1024,4096]{1,0:T(8,128)(2,1)} %weight_in), custom_call_target="tpu_custom_call" | custom-call | flops 268435456 | bytes 4194304 | tf_op jit(solution)/shard_map/own_scores/pallas_call | solution.py:41
  17.6 1.4 %collective-permute-start.1 = (bf16[2,16,512]{2,1,0:T(8,128)(2,1)S(1)}, bf16[2,16,512]{2,1,0:T(8,128)(2,1)S(1)}, u32[]{:S(2)}, u32[]{:S(2)}) collective-permute-start(bf16[2,16,512]{2,1,0:T(8,128)(2,1)S(1)} %get-tuple-element.76), channel_id=1, source_target_pairs={{0,1},{1,0},{2,3},{3,2},{4,5},{5,4},{6,7},{7,6},{8,9},{9,8},{10,11... | collective-permute-start | bytes 98312 | tf_op jit(solution)/shard_map/gradient_rows/ppermute | solution.py:274
  19.8 2.6 %collective-permute-start.4 = (bf16[2,2,16,512]{3,2,1,0:T(8,128)(2,1)S(1)}, bf16[2,2,16,512]{3,2,1,0:T(8,128)(2,1)S(1)}, u32[]{:S(2)}, u32[]{:S(2)}) collective-permute-start(bf16[2,2,16,512]{3,2,1,0:T(8,128)(2,1)S(1)} %pad_maximum_fusion.1.refs_0_), channel_id=1, source_target_pairs={{0,6},{1,7},{2,0},{3,1},{4,2},{5,3},{6,4},{7,5},{8,14},{9,15},{10,... | collective-permute-start | bytes 196616 | tf_op jit(solution)/shard_map/gradient_rows/ppermute | solution.py:277
  22.5 1.7 %collective-permute-start.3 = (bf16[2,2,16,512]{3,2,1,0:T(8,128)(2,1)S(1)}, bf16[2,2,16,512]{3,2,1,0:T(8,128)(2,1)S(1)}, u32[]{:S(2)}, u32[]{:S(2)}) collective-permute-start(bf16[2,2,16,512]{3,2,1,0:T(8,128)(2,1)S(1)} %pad_maximum_fusion.1.refs_0_), channel_id=1, source_target_pairs={{0,4},{1,5},{2,6},{3,7},{4,0},{5,1},{6,2},{7,3},{8,12},{9,13},{10,... | collective-permute-start | bytes 196616 | tf_op jit(solution)/shard_map/gradient_rows/ppermute | solution.py:277
  24.9 3.6 %other_scores.1 = (f32[8,512,256]{2,1,0:T(8,128)S(1)}, f32[8,256]{1,0:T(8,128)S(1)}, f32[8,256]{1,0:T(8,128)S(1)}) custom-call(s32[14]{0:T(128)S(1)} %stack.86.place, bf16[512,1024]{1,0:T(8,128)(2,1)S(1)} %copy-done, bf16[512,128]{1,0:T(8,128)(2,1)S(1)} %collective-permute-done.5.straight, bf16[512,128]{1,0:T(8,128)(2,1)S(1)} %collective-permute-done.6.crossed), custom_call_target="tpu_custom_call" | custom-call | flops 268435456 | bytes 4194304 | tf_op jit(solution)/shard_map/other_scores/pallas_call | solution.py:41
  28.6 2.1 %collective-permute-done.3.refs_2_ = bf16[2,2,16,512]{3,2,1,0:T(8,128)(2,1)S(1)} collective-permute-done((bf16[2,2,16,512]{3,2,1,0:T(8,128)(2,1)S(1)}, bf16[2,2,16,512]{3,2,1,0:T(8,128)(2,1)S(1)}, u32[]{:S(2)}, u32[]{:S(2)}) %collective-permute-start.3) | collective-permute-done | bytes 65568 | tf_op jit(solution)/shard_map/gradient_rows/ppermute | solution.py:277
  30.7 2.9 %project.1 = bf16[16,32,1024]{2,1,0:T(8,128)(2,1)S(1)} custom-call(s32[14]{0:T(128)S(1)} %stack.86.place, bf16[2,2,16,512]{3,2,1,0:T(8,128)(2,1)S(1)} %pad_maximum_fusion.1.refs_0_, bf16[2,2,16,512]{3,2,1,0:T(8,128)(2,1)S(1)} %collective-permute-done.2.refs_1_, bf16[2,2,16,512]{3,2,1,0:T(8,128)(2,1)S(1)} %collective-permute-done.3.refs_2_, ...), custom_call_target="tpu_custom_call" | custom-call | tf_op jit(solution)/shard_map/project/pallas_call | solution.py:41
  33.6 22.9 %all_to_all.15.gathered_ref = bf16[16,32,1024]{2,1,0:T(8,128)(2,1)S(1)} all-to-all(bf16[16,32,1024]{2,1,0:T(8,128)(2,1)S(1)} %project.1), channel_id=1, replica_groups=mesh['zh'=2,'xy'=16,'tp'=8] {'xy'}, dimensions={0} | all-to-all | bytes 2097152 | tf_op jit(solution)/shard_map/head_gradients/all_to_all | solution.py:331
  56.5 3.6 %deltas.1 = (bf16[256,1024]{1,0:T(8,128)(2,1)S(1)}, f32[16,3,8,256]{3,2,1,0:T(8,128)S(1)}) custom-call(s32[14]{0:T(128)S(1)} %stack.86.place, s32[1,512]{1,0:T(1,128)S(1)} %reshape.14.route_ref, bf16[16,32,1024]{2,1,0:T(8,128)(2,1)S(1)} %all_to_all.15.gathered_ref, bf16[512,512]{1,0:T(8,128)(2,1)S(1)} %copy-done.3, ...), custom_call_target="tpu_custom_call" | custom-call | tf_op jit(solution)/shard_map/deltas/pallas_call | solution.py:41
  60.1 11.3 %all_to_all.16.stats_ref = f32[16,3,8,256]{3,2,1,0:T(8,128)S(1)} all-to-all(f32[16,3,8,256]{3,2,1,0:T(8,128)S(1)} %get-tuple-element.52), channel_id=1, replica_groups=mesh['zh'=2,'xy'=16,'tp'=8] {'xy'}, dimensions={0} | all-to-all | bytes 786432 | tf_op jit(solution)/shard_map/row_stats/all_to_all | solution.py:345
  71.4 8.1 %gradients.1 = (bf16[16,16,1024]{2,1,0:T(8,128)(2,1)}, f32[2,4,64,256]{3,2,1,0:T(8,128)S(1)}, bf16[2,4,64,256]{3,2,1,0:T(8,128)(2,1)S(1)}) custom-call(s32[14]{0:T(128)S(1)} %stack.86.place, f32[16,3,8,256]{3,2,1,0:T(8,128)S(1)} %all_to_all.16.stats_ref, bf16[512,1024]{1,0:T(8,128)(2,1)S(1)} %copy-done, bf16[256,1024]{1,0:T(8,128)(2,1)S(1)} %get-tuple-element.53.grad_ref, ...), custom_call_target="tpu_custom_call" | custom-call | tf_op jit(solution)/shard_map/gradients/pallas_call | solution.py:41
  79.5 3.0 %collective-permute-start.7 = (bf16[2,4,64,256]{3,2,1,0:T(8,128)(2,1)S(1)}, bf16[2,4,64,256]{3,2,1,0:T(8,128)(2,1)S(1)}, u32[]{:S(2)}, u32[]{:S(2)}) collective-permute-start(bf16[2,4,64,256]{3,2,1,0:T(8,128)(2,1)S(1)} %get-tuple-element.55), channel_id=1, source_target_pairs={{0,1},{1,0},{2,3},{3,2},{4,5},{5,4},{6,7},{7,6},{8,9},{9,8},{10,11... | collective-permute-start | bytes 786440 | tf_op jit(solution)/shard_map/cache_terms/ppermute | solution.py:274
  82.5 1.2 %collective-permute-done.7 = bf16[2,4,64,256]{3,2,1,0:T(8,128)(2,1)S(1)} collective-permute-done((bf16[2,4,64,256]{3,2,1,0:T(8,128)(2,1)S(1)}, bf16[2,4,64,256]{3,2,1,0:T(8,128)(2,1)S(1)}, u32[]{:S(2)}, u32[]{:S(2)}) %collective-permute-start.7) | collective-permute-done | bytes 262176 | tf_op jit(solution)/shard_map/cache_terms/ppermute | solution.py:274
  83.8 3.4 %collective-permute-start.8 = (bf16[4,64,256]{2,1,0:T(8,128)(2,1)S(1)}, bf16[4,64,256]{2,1,0:T(8,128)(2,1)S(1)}, u32[]{:S(2)}, u32[]{:S(2)}) collective-permute-start(bf16[4,64,256]{2,1,0:T(8,128)(2,1)S(1)} %fusion.2), channel_id=1, source_target_pairs={{0,128},{128,0},{1,129},{129,1},{2,130},{130,2},{3,131},{131,3},{4... | collective-permute-start | bytes 393224 | tf_op jit(solution)/shard_map/cache_terms/ppermute | solution.py:271
  87.2 3.6 %all-to-all-start.2 = ((bf16[16,16,1024]{2,1,0:T(8,128)(2,1)}), bf16[16,16,1024]{2,1,0:T(8,128)(2,1)S(1)}, u32[]{:S(2)}, u32[]{:S(2)}) async-start(bf16[16,16,1024]{2,1,0:T(8,128)(2,1)} %get-tuple-element.56), calls=%async_computation.2 | async-start | bytes 1048576 | tf_op jit(solution)/shard_map/all_to_all | solution.py:364
  90.8 1.7 %collective-permute-done.8 = bf16[4,64,256]{2,1,0:T(8,128)(2,1)S(1)} collective-permute-done((bf16[4,64,256]{2,1,0:T(8,128)(2,1)S(1)}, bf16[4,64,256]{2,1,0:T(8,128)(2,1)S(1)}, u32[]{:S(2)}, u32[]{:S(2)}) %collective-permute-start.8) | collective-permute-done | bytes 131104 | tf_op jit(solution)/shard_map/cache_terms/ppermute | solution.py:271
  92.6 1.5 %collective-permute-start.11 = (bf16[64,256]{1,0:T(8,128)(2,1)S(1)}, bf16[64,256]{1,0:T(8,128)(2,1)S(1)}, u32[]{:S(2)}, u32[]{:S(2)}) collective-permute-start(bf16[64,256]{1,0:T(8,128)(2,1)S(1)} %get-tuple-element.64), channel_id=1, source_target_pairs={{0,6},{1,7},{2,0},{3,1},{4,2},{5,3},{6,4},{7,5},{8,14},{9,15},{10,... | collective-permute-start | bytes 98312 | tf_op jit(solution)/shard_map/cache_terms/ppermute | solution.py:277
  94.1 2.5 %collective-permute-start.10 = (bf16[64,256]{1,0:T(8,128)(2,1)S(1)}, bf16[64,256]{1,0:T(8,128)(2,1)S(1)}, u32[]{:S(2)}, u32[]{:S(2)}) collective-permute-start(bf16[64,256]{1,0:T(8,128)(2,1)S(1)} %get-tuple-element.65), channel_id=1, source_target_pairs={{0,4},{1,5},{2,6},{3,7},{4,0},{5,1},{6,2},{7,3},{8,12},{9,13},{10,... | collective-permute-start | bytes 98312 | tf_op jit(solution)/shard_map/cache_terms/ppermute | solution.py:277
  96.6 1.4 %collective-permute-start.9 = (bf16[64,256]{1,0:T(8,128)(2,1)S(1)}, bf16[64,256]{1,0:T(8,128)(2,1)S(1)}, u32[]{:S(2)}, u32[]{:S(2)}) collective-permute-start(bf16[64,256]{1,0:T(8,128)(2,1)S(1)} %get-tuple-element.66), channel_id=1, source_target_pairs={{0,2},{1,3},{2,4},{3,5},{4,6},{5,7},{6,0},{7,1},{8,10},{9,11},{10,... | collective-permute-start | bytes 98312 | tf_op jit(solution)/shard_map/cache_terms/ppermute | solution.py:277
  98.4 2.9 %collective-permute-done.9 = bf16[64,256]{1,0:T(8,128)(2,1)S(1)} collective-permute-done((bf16[64,256]{1,0:T(8,128)(2,1)S(1)}, bf16[64,256]{1,0:T(8,128)(2,1)S(1)}, u32[]{:S(2)}, u32[]{:S(2)}) %collective-permute-start.9) | collective-permute-done | bytes 32800 | tf_op jit(solution)/shard_map/cache_terms/ppermute | solution.py:277
  (38 shorter events, 5.5 us)
Async XLA Ops:
  0.6 16.9 %copy-start.4 = (bf16[16,512]{1,0:T(8,128)(2,1)S(1)}, bf16[16,512]{1,0:T(8,128)(2,1)}, u32[]{:S(2)}) copy-start(bf16[16,512]{1,0:T(8,128)(2,1)} %param.11) | copy-start | bytes 49156
  0.6 16.9 %collective-permute-start = (bf16[16,512]{1,0:T(8,128)(2,1)}, bf16[16,512]{1,0:T(8,128)(2,1)S(1)}, u32[]{:S(2)}, u32[]{:S(2)}) collective-permute-start(bf16[16,512]{1,0:T(8,128)(2,1)} %param.11), channel_id=1, source_target_pairs={{0,128},{128,0},{1,129},{129,1},{2,130},{130,2},{3,131},{131,3},{4... | collective-permute-start | bytes 49160 | tf_op jit(solution)/shard_map/gradient_rows/ppermute | solution.py:271
  9.5 9.5 %collective-permute-start.5 = (bf16[512,128]{1,0:T(8,128)(2,1)S(1)}, bf16[512,128]{1,0:T(8,128)(2,1)S(1)}, u32[]{:S(2)}, u32[]{:S(2)}) collective-permute-start(bf16[512,128]{1,0:T(8,128)(2,1)S(1)} %dynamic-slice_select_fusion), channel_id=1, source_target_pairs={{0,128},{128,0},{1,129},{129,1},{2,130},{130,2},{3,131},{131,3},{4... | collective-permute-start | bytes 393224 | tf_op jit(solution)/shard_map/cache_pair/ppermute | solution.py:271
  11.3 1.2 %copy-start = (bf16[512,1024]{1,0:T(8,128)(2,1)S(1)}, bf16[512,1024]{1,0:T(8,128)(2,1)}, u32[]{:S(2)}) copy-start(bf16[512,1024]{1,0:T(8,128)(2,1)} %query_ref.5) | copy-start | bytes 3145732
  12.6 1.0 %copy-start.1 = (bf16[512,512]{1,0:T(8,128)(2,1)S(1)}, bf16[512,512]{1,0:T(8,128)(2,1)}, u32[]{:S(2)}) copy-start(bf16[512,512]{1,0:T(8,128)(2,1)} %key_ref.3) | copy-start | bytes 1572868
  17.5 39.0 %copy-start.3 = (bf16[512,512]{1,0:T(8,128)(2,1)S(1)}, bf16[512,512]{1,0:T(8,128)(2,1)}, u32[]{:S(2)}) copy-start(bf16[512,512]{1,0:T(8,128)(2,1)} %value_ref.3) | copy-start | bytes 1572868
  17.6 2.2 %collective-permute-start.1 = (bf16[2,16,512]{2,1,0:T(8,128)(2,1)S(1)}, bf16[2,16,512]{2,1,0:T(8,128)(2,1)S(1)}, u32[]{:S(2)}, u32[]{:S(2)}) collective-permute-start(bf16[2,16,512]{2,1,0:T(8,128)(2,1)S(1)} %get-tuple-element.76), channel_id=1, source_target_pairs={{0,1},{1,0},{2,3},{3,2},{4,5},{5,4},{6,7},{7,6},{8,9},{9,8},{10,11... | collective-permute-start | bytes 98312 | tf_op jit(solution)/shard_map/gradient_rows/ppermute | solution.py:274
  19.0 6.0 %collective-permute-start.6 = (bf16[512,128]{1,0:T(8,128)(2,1)S(1)}, bf16[512,128]{1,0:T(8,128)(2,1)S(1)}, u32[]{:S(2)}, u32[]{:S(2)}) collective-permute-start(bf16[512,128]{1,0:T(8,128)(2,1)S(1)} %collective-permute-done.5.straight), channel_id=1, source_target_pairs={{0,1},{1,0},{2,3},{3,2},{4,5},{5,4},{6,7},{7,6},{8,9},{9,8},{10,11... | collective-permute-start | bytes 393224 | tf_op jit(solution)/shard_map/cache_pair/ppermute | solution.py:274
  19.8 8.8 %collective-permute-start.4 = (bf16[2,2,16,512]{3,2,1,0:T(8,128)(2,1)S(1)}, bf16[2,2,16,512]{3,2,1,0:T(8,128)(2,1)S(1)}, u32[]{:S(2)}, u32[]{:S(2)}) collective-permute-start(bf16[2,2,16,512]{3,2,1,0:T(8,128)(2,1)S(1)} %pad_maximum_fusion.1.refs_0_), channel_id=1, source_target_pairs={{0,6},{1,7},{2,0},{3,1},{4,2},{5,3},{6,4},{7,5},{8,14},{9,15},{10,... | collective-permute-start | bytes 196616 | tf_op jit(solution)/shard_map/gradient_rows/ppermute | solution.py:277
  22.5 8.2 %collective-permute-start.3 = (bf16[2,2,16,512]{3,2,1,0:T(8,128)(2,1)S(1)}, bf16[2,2,16,512]{3,2,1,0:T(8,128)(2,1)S(1)}, u32[]{:S(2)}, u32[]{:S(2)}) collective-permute-start(bf16[2,2,16,512]{3,2,1,0:T(8,128)(2,1)S(1)} %pad_maximum_fusion.1.refs_0_), channel_id=1, source_target_pairs={{0,4},{1,5},{2,6},{3,7},{4,0},{5,1},{6,2},{7,3},{8,12},{9,13},{10,... | collective-permute-start | bytes 196616 | tf_op jit(solution)/shard_map/gradient_rows/ppermute | solution.py:277
  24.2 6.5 %collective-permute-start.2 = (bf16[2,2,16,512]{3,2,1,0:T(8,128)(2,1)S(1)}, bf16[2,2,16,512]{3,2,1,0:T(8,128)(2,1)S(1)}, u32[]{:S(2)}, u32[]{:S(2)}) collective-permute-start(bf16[2,2,16,512]{3,2,1,0:T(8,128)(2,1)S(1)} %pad_maximum_fusion.1.refs_0_), channel_id=1, source_target_pairs={{0,2},{1,3},{2,4},{3,5},{4,6},{5,7},{6,0},{7,1},{8,10},{9,11},{10,... | collective-permute-start | bytes 196616 | tf_op jit(solution)/shard_map/gradient_rows/ppermute | solution.py:277
  33.6 37.8 %copy-start.2 = (bf16[512,512]{1,0:T(8,128)(2,1)S(1)}, bf16[512,512]{1,0:T(8,128)(2,1)}, u32[]{:S(2)}) copy-start(bf16[512,512]{1,0:T(8,128)(2,1)} %key_ref.3) | copy-start | bytes 1572868
  79.5 4.2 %collective-permute-start.7 = (bf16[2,4,64,256]{3,2,1,0:T(8,128)(2,1)S(1)}, bf16[2,4,64,256]{3,2,1,0:T(8,128)(2,1)S(1)}, u32[]{:S(2)}, u32[]{:S(2)}) collective-permute-start(bf16[2,4,64,256]{3,2,1,0:T(8,128)(2,1)S(1)} %get-tuple-element.55), channel_id=1, source_target_pairs={{0,1},{1,0},{2,3},{3,2},{4,5},{5,4},{6,7},{7,6},{8,9},{9,8},{10,11... | collective-permute-start | bytes 786440 | tf_op jit(solution)/shard_map/cache_terms/ppermute | solution.py:274
  83.8 8.7 %collective-permute-start.8 = (bf16[4,64,256]{2,1,0:T(8,128)(2,1)S(1)}, bf16[4,64,256]{2,1,0:T(8,128)(2,1)S(1)}, u32[]{:S(2)}, u32[]{:S(2)}) collective-permute-start(bf16[4,64,256]{2,1,0:T(8,128)(2,1)S(1)} %fusion.2), channel_id=1, source_target_pairs={{0,128},{128,0},{1,129},{129,1},{2,130},{130,2},{3,131},{131,3},{4... | collective-permute-start | bytes 393224 | tf_op jit(solution)/shard_map/cache_terms/ppermute | solution.py:271
  87.2 14.3 %all-to-all-start.2 = ((bf16[16,16,1024]{2,1,0:T(8,128)(2,1)}), bf16[16,16,1024]{2,1,0:T(8,128)(2,1)S(1)}, u32[]{:S(2)}, u32[]{:S(2)}) async-start(bf16[16,16,1024]{2,1,0:T(8,128)(2,1)} %get-tuple-element.56), calls=%async_computation.2 | async-start | bytes 1048576 | tf_op jit(solution)/shard_map/all_to_all | solution.py:364
  92.6 5.4 %collective-permute-start.11 = (bf16[64,256]{1,0:T(8,128)(2,1)S(1)}, bf16[64,256]{1,0:T(8,128)(2,1)S(1)}, u32[]{:S(2)}, u32[]{:S(2)}) collective-permute-start(bf16[64,256]{1,0:T(8,128)(2,1)S(1)} %get-tuple-element.64), channel_id=1, source_target_pairs={{0,6},{1,7},{2,0},{3,1},{4,2},{5,3},{6,4},{7,5},{8,14},{9,15},{10,... | collective-permute-start | bytes 98312 | tf_op jit(solution)/shard_map/cache_terms/ppermute | solution.py:277
  94.1 4.3 %collective-permute-start.10 = (bf16[64,256]{1,0:T(8,128)(2,1)S(1)}, bf16[64,256]{1,0:T(8,128)(2,1)S(1)}, u32[]{:S(2)}, u32[]{:S(2)}) collective-permute-start(bf16[64,256]{1,0:T(8,128)(2,1)S(1)} %get-tuple-element.65), channel_id=1, source_target_pairs={{0,4},{1,5},{2,6},{3,7},{4,0},{5,1},{6,2},{7,3},{8,12},{9,13},{10,... | collective-permute-start | bytes 98312 | tf_op jit(solution)/shard_map/cache_terms/ppermute | solution.py:277
  96.6 4.7 %collective-permute-start.9 = (bf16[64,256]{1,0:T(8,128)(2,1)S(1)}, bf16[64,256]{1,0:T(8,128)(2,1)S(1)}, u32[]{:S(2)}, u32[]{:S(2)}) collective-permute-start(bf16[64,256]{1,0:T(8,128)(2,1)S(1)} %get-tuple-element.66), channel_id=1, source_target_pairs={{0,2},{1,3},{2,4},{3,5},{4,6},{5,7},{6,0},{7,1},{8,10},{9,11},{10,... | collective-permute-start | bytes 98312 | tf_op jit(solution)/shard_map/cache_terms/ppermute | solution.py:277

commit v3 on v2

--- a/solution.py
+++ b/solution.py
@@ -87,13 +87,13 @@
     return jnp.where(swap, second, first), jnp.where(swap, first, second)
 
 
-def score_heads(place, slot, query_ref, keys, expo_ref, peak_ref, total_ref):
+def score_heads(place, slot, first_row, query_ref, keys, expo_ref, peak_ref, total_ref):
     heads, span, window = expo_ref.shape
     query_pos = place[START] + place[LINE] * window + lax.broadcasted_iota(jnp.int32, (1, window), 1)
     key_pos = place[FIRST + slot] + lax.broadcasted_iota(jnp.int32, (span, 1), 0)
 
     def one_head(head, _):
-        query = query_ref[pl.ds(place[LINE] * window, window), columns(head)]
+        query = query_ref[pl.ds(first_row, window), columns(head)]
         scored = dot(keys, query, ROWS) * (SCALE * LOG2E)
         scored = jnp.where(key_pos <= query_pos, scored, NEG)
         peak = jnp.maximum(jnp.max(scored, axis=0, keepdims=True), FLOOR)
@@ -106,17 +106,39 @@
     lax.fori_loop(0, heads, one_head, 0)
 
 
-def own_kernel(place, query_ref, key_ref, weight_in, expo_ref, peak_ref, total_ref, weight_out, done):
-    copy = pltpu.make_async_copy(weight_in, weight_out, done)
-    copy.start()
-    keys = key_ref[:, columns(place[KV_HEAD])]
-    score_heads(place, 0, query_ref, keys, expo_ref, peak_ref, total_ref)
-    copy.wait()
+def own_kernel(
+    place,
+    query_in,
+    key_in,
+    weight_in,
+    expo_ref,
+    peak_ref,
+    total_ref,
+    weight_out,
+    query_ref,
+    key_ref,
+    loaded,
+):
+    window = query_ref.shape[0]
+    rows = pl.ds(pl.multiple_of(place[LINE] * window, window), window)
+    copies = [
+        pltpu.make_async_copy(query_in.at[rows], query_ref, loaded.at[0]),
+        pltpu.make_async_copy(key_in.at[:, columns(place[KV_HEAD])], key_ref, loaded.at[1]),
+        pltpu.make_async_copy(weight_in, weight_out, loaded.at[2]),
+    ]
+    for copy in copies:
+        copy.start()
+    copies[0].wait()
+    copies[1].wait()
+    score_heads(place, 0, 0, query_ref, key_ref[...], expo_ref, peak_ref, total_ref)
+    copies[2].wait()
 
 
 def other_kernel(place, query_ref, straight, crossed, expo_ref, peak_ref, total_ref):
     keys = other_pair(place, straight, crossed)[0]
-    score_heads(place, 1, query_ref, keys, expo_ref, peak_ref, total_ref)
+    window = expo_ref.shape[2]
+    first_row = pl.multiple_of(place[LINE] * window, window)
+    score_heads(place, 1, first_row, query_ref, keys, expo_ref, peak_ref, total_ref)
 
 
 def delta_kernel(
@@ -228,6 +250,15 @@
                 ).astype(BF)
 
 
+def finish_kernel(place, terms_ref, *refs):
+    pieces, (query_out, key_out, value_out) = refs[:-3], refs[-3:]
+    query_out[...] = jnp.sum(terms_ref[...].astype(F32), axis=0).astype(BF)
+    for step, piece in enumerate(pieces):
+        where = columns(place[BLOCKS + 2 * step] // 2)
+        key_out[:, where] = piece[:, :HD]
+        value_out[:, where] = piece[:, HD:]
+
+
 def on_device(
     lines,
     groups,
@@ -265,8 +296,6 @@
 
     route = token_route.reshape(lines, groups, rows)
     route = jnp.where(line == 0, route, route[::-1]).transpose(1, 0, 2).reshape(1, window)
-    out_weight, place, route = lax.optimization_barrier((out_weight, place, route))
-
     def to_pair(value):
         return lax.ppermute(value, "zh", [(0, 1), (1, 0)])
 
@@ -289,16 +318,20 @@
     expo_own, peak_own, total_own, weight = call(
         own_kernel,
         "own_scores",
-        (place, query_window, key_cache, in_hbm(out_weight)),
+        (place, in_hbm(query_window), in_hbm(key_cache), in_hbm(out_weight)),
         score_outs + [(out_weight.shape, BF)],
-        scratch=[pltpu.SemaphoreType.DMA],
+        scratch=[
+            pltpu.VMEM((half, local_heads * HD), BF),
+            pltpu.VMEM((span, HD), BF),
+            pltpu.SemaphoreType.DMA((3,)),
+        ],
         cost=score_cost,
-        streamed=(3,),
+        streamed=(1, 2, 3),
         held=(0, 3),
     )
     with jax.named_scope("gradient_rows"):
         other_rows = to_pair(grad_routed)
-        other_rows, weight = lax.optimization_barrier((other_rows, weight))
+        other_rows, weight, route = lax.optimization_barrier((other_rows, weight, route))
         pair = jnp.stack([grad_routed, other_rows])
         chip_rows = jnp.stack([pair, to_core(pair)])
         all_rows = [chip_rows] + [to_chip(chip_rows, step) for step in range(1, chips)]
@@ -367,23 +400,22 @@
         line_sum = chip_sum[0] + to_pair(chip_sum[1].astype(BF)).astype(F32)
         line_sum = line_sum.astype(BF)
         own = lax.dynamic_index_in_dim(line_sum, chip, 0, False)
-        arrived = jnp.stack(
-            [own]
-            + [
-                to_chip(lax.dynamic_index_in_dim(line_sum, (chip + step) % chips, 0, False), step)
-                for step in range(1, chips)
-            ]
-        )
-        arrived, query_terms = lax.optimization_barrier((arrived, query_terms))
-        in_order = [
-            lax.dynamic_index_in_dim(arrived, (chip - head + chips) % chips, 0, False)
-            for head in range(chips)
+        arrived = [own] + [
+            to_chip(lax.dynamic_index_in_dim(line_sum, (chip + step) % chips, 0, False), step)
+            for step in range(1, chips)
         ]
-        grad_keys = jnp.concatenate([piece[:, :HD] for piece in in_order], axis=1)
-        grad_values = jnp.concatenate([piece[:, HD:] for piece in in_order], axis=1)
-    with jax.named_scope("query_terms"):
-        grad_query = jnp.sum(query_terms.astype(F32), axis=0).astype(BF)
-    return grad_query, grad_keys, grad_values
+    query_terms, *arrived = lax.optimization_barrier((query_terms, *arrived))
+    width = KVH * HD
+    return call(
+        finish_kernel,
+        "finish",
+        (place, query_terms, *arrived),
+        [
+            (query_terms.shape[1:], BF),
+            ((share, width), BF),
+            ((share, width), BF),
+        ],
+    )
 
 
 def solution(mesh):

time: 104 us -> 102 us (0.981)
  waiting for transfers between devices: 8.8 us -> 11.7 us
  local copies, waits for them, and re-layouts: 3.31 us -> 1.02 us
  other arithmetic: 3.1 us -> 1.12 us
  Pallas kernels: 22.3 us -> 24.2 us
  starting transfers between devices: 30.3 us -> 28.5 us
    unnamed x10 -> x8, local copies, waits for them, and re-layouts: 2.28 us -> 0.02 us
    ppermute x3, waiting for transfers between devices: 1.69 us -> 3.94 us  [to_pair(): return lax.ppermute(value, 'zh', [(0, 1), (1, 0)])]
    pallas_call x5 -> x6, Pallas kernels: 22.3 us -> 24.2 us  [call(): pl.pallas_call(kernel, in_specs=[SMEM] + [HBM if i in streamed else VMEM...]
    ppermute x6, starting transfers between devices: 10.5 us -> 8.55 us  [to_chip(): lax.ppermute(value, 'tp', [(i, (i + 2 * step) % parts) for i in range(par...]
    ppermute x3, starting transfers between devices: 4.89 us -> 6.46 us  [to_core(): return lax.ppermute(value, 'tp', [(i, i ^ 1) for i in range(parts)])]
    ppermute x3, starting transfers between devices: 11.4 us -> 9.89 us  [to_pair(): return lax.ppermute(value, 'zh', [(0, 1), (1, 0)])]
    concatenate x2 -> x0, other arithmetic: 1.28 us -> none  [the longest x1 0.64 us: on_device(): grad_values = jnp.concatenate([piece[:, HD:] for piece in in_order], axis=1)]
    ppermute x6, waiting for transfers between devices: 5.45 us -> 6.56 us  [to_chip(): lax.ppermute(value, 'tp', [(i, (i + 2 * step) % parts) for i in range(par...]
  transfers between devices with their start and end apart: 13 -> 13, of which waited for: 7 -> 6; matrix products, arithmetic and copies ran while one was open for 2% -> 2% of each run, Pallas kernels for 7% -> 8%
where the time goes in v3:
time: 102 us
  blocking collectives  34.2 us (34%)
  starting transfers between devices  28.5 us (28%)
  Pallas kernels  24.2 us (24%)
  waiting for transfers between devices  11.7 us (11%)
  between operations  1.48 us (1%)
  other arithmetic  1.12 us (1%)
  local copies, waits for them, and re-layouts  1.02 us (1%)
    pallas_call x6, Pallas kernels, call(): pl.pallas_call(kernel, in_specs=[SMEM] + [HBM if i in streamed else VMEM...  24.2 us
    all_to_all x1, blocking collectives, on_device(): gathered = lax.all_to_all(gathered, 'xy', 0, 0)  22.9 us
    all_to_all x1, blocking collectives, on_device(): stats = lax.all_to_all(stats, 'xy', 0, 0)  11.3 us
    ppermute x3, starting transfers between devices, to_pair(): return lax.ppermute(value, 'zh', [(0, 1), (1, 0)])  9.89 us
    ppermute x6, starting transfers between devices, to_chip(): lax.ppermute(value, 'tp', [(i, (i + 2 * step) % parts) for i in range(par...  8.55 us
    ppermute x6, waiting for transfers between devices, to_chip(): lax.ppermute(value, 'tp', [(i, (i + 2 * step) % parts) for i in range(par...  6.56 us
    ppermute x3, starting transfers between devices, to_core(): return lax.ppermute(value, 'tp', [(i, i ^ 1) for i in range(parts)])  6.46 us
    ppermute x3, waiting for transfers between devices, to_pair(): return lax.ppermute(value, 'zh', [(0, 1), (1, 0)])  3.94 us
  transfers between devices with their start and end apart: 13, of which 6 were waited for; matrix products, arithmetic and copies ran while one was open for 2% of the time, Pallas kernels for 8%

profile of v3, /device:TPU:1, one launch (start us, length us, event | category | flops | bytes accessed | tf_op | source)
XLA Modules:
  0.0 102.1 jit_solution(17092149033858848432)
XLA Ops:
  0.7 7.8 %collective-permute-start = (bf16[16,512]{1,0:T(8,128)(2,1)}, bf16[16,512]{1,0:T(8,128)(2,1)S(1)}, u32[]{:S(2)}, u32[]{:S(2)}) collective-permute-start(bf16[16,512]{1,0:T(8,128)(2,1)} %param.11), channel_id=1, source_target_pairs={{0,128},{128,0},{1,129},{129,1},{2,130},{130,2},{3,131},{131,3},{4... | collective-permute-start | bytes 49160 | tf_op jit(solution)/shard_map/gradient_rows/ppermute | solution.py:300
  8.5 1.0 dynamic-slice_select_fusion
  10.4 0.8 reshape.13
  11.3 4.6 %own_scores.1 = (f32[8,512,256]{2,1,0:T(8,128)S(1)}, f32[8,256]{1,0:T(8,128)S(1)}, f32[8,256]{1,0:T(8,128)S(1)}, bf16[1024,4096]{1,0:T(8,128)(2,1)S(1)}) custom-call(s32[14]{0:T(128)S(1)} %stack.73.place, bf16[512,1024]{1,0:T(8,128)(2,1)} %query_ref.3, bf16[512,512]{1,0:T(8,128)(2,1)} %key_ref.1, bf16[1024,4096]{1,0:T(8,128)(2,1)} %weight_in.1), custom_call_target="tpu_custom_call" | custom-call | flops 268435456 | bytes 4194304 | tf_op jit(solution)/shard_map/own_scores/pallas_call | solution.py:41
  16.0 1.4 %collective-permute-start.1 = (bf16[2,16,512]{2,1,0:T(8,128)(2,1)S(1)}, bf16[2,16,512]{2,1,0:T(8,128)(2,1)S(1)}, u32[]{:S(2)}, u32[]{:S(2)}) collective-permute-start(bf16[2,16,512]{2,1,0:T(8,128)(2,1)S(1)} %get-tuple-element.66), channel_id=1, source_target_pairs={{0,1},{1,0},{2,3},{3,2},{4,5},{5,4},{6,7},{7,6},{8,9},{9,8},{10,11... | collective-permute-start | bytes 98312 | tf_op jit(solution)/shard_map/gradient_rows/ppermute | solution.py:303
  17.4 2.1 %collective-permute-start.6 = (bf16[512,128]{1,0:T(8,128)(2,1)S(1)}, bf16[512,128]{1,0:T(8,128)(2,1)S(1)}, u32[]{:S(2)}, u32[]{:S(2)}) collective-permute-start(bf16[512,128]{1,0:T(8,128)(2,1)S(1)} %collective-permute-done.5.straight), channel_id=1, source_target_pairs={{0,1},{1,0},{2,3},{3,2},{4,5},{5,4},{6,7},{7,6},{8,9},{9,8},{10,11... | collective-permute-start | bytes 393224 | tf_op jit(solution)/shard_map/cache_pair/ppermute | solution.py:303
  19.5 2.4 %collective-permute-start.4 = (bf16[2,2,16,512]{3,2,1,0:T(8,128)(2,1)S(1)}, bf16[2,2,16,512]{3,2,1,0:T(8,128)(2,1)S(1)}, u32[]{:S(2)}, u32[]{:S(2)}) collective-permute-start(bf16[2,2,16,512]{3,2,1,0:T(8,128)(2,1)S(1)} %pad_maximum_fusion.refs_0_), channel_id=1, source_target_pairs={{0,6},{1,7},{2,0},{3,1},{4,2},{5,3},{6,4},{7,5},{8,14},{9,15},{10,... | collective-permute-start | bytes 196616 | tf_op jit(solution)/shard_map/gradient_rows/ppermute | solution.py:306
  22.0 2.3 %collective-permute-start.3 = (bf16[2,2,16,512]{3,2,1,0:T(8,128)(2,1)S(1)}, bf16[2,2,16,512]{3,2,1,0:T(8,128)(2,1)S(1)}, u32[]{:S(2)}, u32[]{:S(2)}) collective-permute-start(bf16[2,2,16,512]{3,2,1,0:T(8,128)(2,1)S(1)} %pad_maximum_fusion.refs_0_), channel_id=1, source_target_pairs={{0,4},{1,5},{2,6},{3,7},{4,0},{5,1},{6,2},{7,3},{8,12},{9,13},{10,... | collective-permute-start | bytes 196616 | tf_op jit(solution)/shard_map/gradient_rows/ppermute | solution.py:306
  25.0 3.6 %other_scores.1 = (f32[8,512,256]{2,1,0:T(8,128)S(1)}, f32[8,256]{1,0:T(8,128)S(1)}, f32[8,256]{1,0:T(8,128)S(1)}) custom-call(s32[14]{0:T(128)S(1)} %stack.73.place, bf16[512,1024]{1,0:T(8,128)(2,1)S(1)} %copy-done, bf16[512,128]{1,0:T(8,128)(2,1)S(1)} %collective-permute-done.5.straight, bf16[512,128]{1,0:T(8,128)(2,1)S(1)} %collective-permute-done.6.crossed), custom_call_target="tpu_custom_call" | custom-call | flops 268435456 | bytes 4194304 | tf_op jit(solution)/shard_map/other_scores/pallas_call | solution.py:41
  28.6 2.1 %collective-permute-done.3.refs_2_ = bf16[2,2,16,512]{3,2,1,0:T(8,128)(2,1)S(1)} collective-permute-done((bf16[2,2,16,512]{3,2,1,0:T(8,128)(2,1)S(1)}, bf16[2,2,16,512]{3,2,1,0:T(8,128)(2,1)S(1)}, u32[]{:S(2)}, u32[]{:S(2)}) %collective-permute-start.3) | collective-permute-done | bytes 65568 | tf_op jit(solution)/shard_map/gradient_rows/ppermute | solution.py:306
  30.7 2.9 %project.1 = bf16[16,32,1024]{2,1,0:T(8,128)(2,1)S(1)} custom-call(s32[14]{0:T(128)S(1)} %stack.73.place, bf16[2,2,16,512]{3,2,1,0:T(8,128)(2,1)S(1)} %pad_maximum_fusion.refs_0_, bf16[2,2,16,512]{3,2,1,0:T(8,128)(2,1)S(1)} %collective-permute-done.2.refs_1_, bf16[2,2,16,512]{3,2,1,0:T(8,128)(2,1)S(1)} %collective-permute-done.3.refs_2_, ...), custom_call_target="tpu_custom_call" | custom-call | tf_op jit(solution)/shard_map/project/pallas_call | solution.py:41
  33.6 22.9 %all_to_all.15.gathered_ref = bf16[16,32,1024]{2,1,0:T(8,128)(2,1)S(1)} all-to-all(bf16[16,32,1024]{2,1,0:T(8,128)(2,1)S(1)} %project.1), channel_id=1, replica_groups=mesh['zh'=2,'xy'=16,'tp'=8] {'xy'}, dimensions={0} | all-to-all | bytes 2097152 | tf_op jit(solution)/shard_map/head_gradients/all_to_all | solution.py:364
  56.5 3.6 %deltas.1 = (bf16[256,1024]{1,0:T(8,128)(2,1)S(1)}, f32[16,3,8,256]{3,2,1,0:T(8,128)S(1)}) custom-call(s32[14]{0:T(128)S(1)} %stack.73.place, s32[1,512]{1,0:T(1,128)S(1)} %reshape.14.route_ref, bf16[16,32,1024]{2,1,0:T(8,128)(2,1)S(1)} %all_to_all.15.gathered_ref, bf16[512,512]{1,0:T(8,128)(2,1)S(1)} %copy-done.2, ...), custom_call_target="tpu_custom_call" | custom-call | tf_op jit(solution)/shard_map/deltas/pallas_call | solution.py:41
  60.1 11.3 %all_to_all.16.stats_ref = f32[16,3,8,256]{3,2,1,0:T(8,128)S(1)} all-to-all(f32[16,3,8,256]{3,2,1,0:T(8,128)S(1)} %get-tuple-element.51), channel_id=1, replica_groups=mesh['zh'=2,'xy'=16,'tp'=8] {'xy'}, dimensions={0} | all-to-all | bytes 786432 | tf_op jit(solution)/shard_map/row_stats/all_to_all | solution.py:378
  71.4 8.1 %gradients.1 = (bf16[16,16,1024]{2,1,0:T(8,128)(2,1)}, f32[2,4,64,256]{3,2,1,0:T(8,128)S(1)}, bf16[2,4,64,256]{3,2,1,0:T(8,128)(2,1)S(1)}) custom-call(s32[14]{0:T(128)S(1)} %stack.73.place, f32[16,3,8,256]{3,2,1,0:T(8,128)S(1)} %all_to_all.16.stats_ref, bf16[512,1024]{1,0:T(8,128)(2,1)S(1)} %copy-done, bf16[256,1024]{1,0:T(8,128)(2,1)S(1)} %get-tuple-element.52.grad_ref, ...), custom_call_target="tpu_custom_call" | custom-call | tf_op jit(solution)/shard_map/gradients/pallas_call | solution.py:41
  79.6 3.0 %collective-permute-start.7 = (bf16[2,4,64,256]{3,2,1,0:T(8,128)(2,1)S(1)}, bf16[2,4,64,256]{3,2,1,0:T(8,128)(2,1)S(1)}, u32[]{:S(2)}, u32[]{:S(2)}) collective-permute-start(bf16[2,4,64,256]{3,2,1,0:T(8,128)(2,1)S(1)} %get-tuple-element.55), channel_id=1, source_target_pairs={{0,1},{1,0},{2,3},{3,2},{4,5},{5,4},{6,7},{7,6},{8,9},{9,8},{10,11... | collective-permute-start | bytes 786440 | tf_op jit(solution)/shard_map/cache_terms/ppermute | solution.py:303
  82.6 1.2 %collective-permute-done.7 = bf16[2,4,64,256]{3,2,1,0:T(8,128)(2,1)S(1)} collective-permute-done((bf16[2,4,64,256]{3,2,1,0:T(8,128)(2,1)S(1)}, bf16[2,4,64,256]{3,2,1,0:T(8,128)(2,1)S(1)}, u32[]{:S(2)}, u32[]{:S(2)}) %collective-permute-start.7) | collective-permute-done | bytes 262176 | tf_op jit(solution)/shard_map/cache_terms/ppermute | solution.py:303
  83.8 1.8 %collective-permute-start.8 = (bf16[4,64,256]{2,1,0:T(8,128)(2,1)S(1)}, bf16[4,64,256]{2,1,0:T(8,128)(2,1)S(1)}, u32[]{:S(2)}, u32[]{:S(2)}) collective-permute-start(bf16[4,64,256]{2,1,0:T(8,128)(2,1)S(1)} %fusion.2), channel_id=1, source_target_pairs={{0,128},{128,0},{1,129},{129,1},{2,130},{130,2},{3,131},{131,3},{4... | collective-permute-start | bytes 393224 | tf_op jit(solution)/shard_map/cache_terms/ppermute | solution.py:300
  85.6 3.6 %all-to-all-start.2 = ((bf16[16,16,1024]{2,1,0:T(8,128)(2,1)}), bf16[16,16,1024]{2,1,0:T(8,128)(2,1)S(1)}, u32[]{:S(2)}, u32[]{:S(2)}) async-start(bf16[16,16,1024]{2,1,0:T(8,128)(2,1)} %get-tuple-element.53), calls=%async_computation.2 | async-start | bytes 1048576 | tf_op jit(solution)/shard_map/all_to_all | solution.py:397
  89.3 3.9 %collective-permute-done.8 = bf16[4,64,256]{2,1,0:T(8,128)(2,1)S(1)} collective-permute-done((bf16[4,64,256]{2,1,0:T(8,128)(2,1)S(1)}, bf16[4,64,256]{2,1,0:T(8,128)(2,1)S(1)}, u32[]{:S(2)}, u32[]{:S(2)}) %collective-permute-start.8) | collective-permute-done | bytes 131104 | tf_op jit(solution)/shard_map/cache_terms/ppermute | solution.py:300
  93.3 2.7 %collective-permute-start.11 = (bf16[64,256]{1,0:T(8,128)(2,1)S(1)}, bf16[64,256]{1,0:T(8,128)(2,1)S(1)}, u32[]{:S(2)}, u32[]{:S(2)}) collective-permute-start(bf16[64,256]{1,0:T(8,128)(2,1)S(1)} %get-tuple-element.61), channel_id=1, source_target_pairs={{0,6},{1,7},{2,0},{3,1},{4,2},{5,3},{6,4},{7,5},{8,14},{9,15},{10,... | collective-permute-start | bytes 98312 | tf_op jit(solution)/shard_map/cache_terms/ppermute | solution.py:306
  97.0 2.9 %collective-permute-done.10.refs_2_ = bf16[64,256]{1,0:T(8,128)(2,1)S(1)} collective-permute-done((bf16[64,256]{1,0:T(8,128)(2,1)S(1)}, bf16[64,256]{1,0:T(8,128)(2,1)S(1)}, u32[]{:S(2)}, u32[]{:S(2)}) %collective-permute-start.10) | collective-permute-done | bytes 32800 | tf_op jit(solution)/shard_map/cache_terms/ppermute | solution.py:306
  100.0 0.9 collective-permute-done.9.refs_1_
  100.9 1.2 %finish.1 = (bf16[16,1024]{1,0:T(8,128)(2,1)}, bf16[64,512]{1,0:T(8,128)(2,1)}, bf16[64,512]{1,0:T(8,128)(2,1)}) custom-call(s32[14]{0:T(128)S(1)} %stack.73.place, bf16[16,16,1024]{2,1,0:T(8,128)(2,1)S(1)} %all-to-all-done.2.terms_ref, bf16[64,256]{1,0:T(8,128)(2,1)S(1)} %get-tuple-element.57.refs_0_, bf16[64,256]{1,0:T(8,128)(2,1)S(1)} %collective-permute-done.9.refs_1_, ...), custom_call_target="tpu_custom_call" | custom-call | tf_op jit(solution)/shard_map/finish/pallas_call | solution.py:41
  (30 shorter events, 2.4 us)
Async XLA Ops:
  0.6 15.4 %copy-start.3 = (bf16[16,512]{1,0:T(8,128)(2,1)S(1)}, bf16[16,512]{1,0:T(8,128)(2,1)}, u32[]{:S(2)}) copy-start(bf16[16,512]{1,0:T(8,128)(2,1)} %param.11) | copy-start | bytes 49156
  0.6 24.3 %copy-start = (bf16[512,1024]{1,0:T(8,128)(2,1)S(1)}, bf16[512,1024]{1,0:T(8,128)(2,1)}, u32[]{:S(2)}) copy-start(bf16[512,1024]{1,0:T(8,128)(2,1)} %query_ref.3) | copy-start | bytes 3145732
  0.7 15.3 %collective-permute-start = (bf16[16,512]{1,0:T(8,128)(2,1)}, bf16[16,512]{1,0:T(8,128)(2,1)S(1)}, u32[]{:S(2)}, u32[]{:S(2)}) collective-permute-start(bf16[16,512]{1,0:T(8,128)(2,1)} %param.11), channel_id=1, source_target_pairs={{0,128},{128,0},{1,129},{129,1},{2,130},{130,2},{3,131},{131,3},{4... | collective-permute-start | bytes 49160 | tf_op jit(solution)/shard_map/gradient_rows/ppermute | solution.py:300
  9.5 7.9 %collective-permute-start.5 = (bf16[512,128]{1,0:T(8,128)(2,1)S(1)}, bf16[512,128]{1,0:T(8,128)(2,1)S(1)}, u32[]{:S(2)}, u32[]{:S(2)}) collective-permute-start(bf16[512,128]{1,0:T(8,128)(2,1)S(1)} %dynamic-slice_select_fusion), channel_id=1, source_target_pairs={{0,128},{128,0},{1,129},{129,1},{2,130},{130,2},{3,131},{131,3},{4... | collective-permute-start | bytes 393224 | tf_op jit(solution)/shard_map/cache_pair/ppermute | solution.py:300
  16.0 40.5 %copy-start.2 = (bf16[512,512]{1,0:T(8,128)(2,1)S(1)}, bf16[512,512]{1,0:T(8,128)(2,1)}, u32[]{:S(2)}) copy-start(bf16[512,512]{1,0:T(8,128)(2,1)} %value_ref.3) | copy-start | bytes 1572868
  16.0 3.5 %collective-permute-start.1 = (bf16[2,16,512]{2,1,0:T(8,128)(2,1)S(1)}, bf16[2,16,512]{2,1,0:T(8,128)(2,1)S(1)}, u32[]{:S(2)}, u32[]{:S(2)}) collective-permute-start(bf16[2,16,512]{2,1,0:T(8,128)(2,1)S(1)} %get-tuple-element.66), channel_id=1, source_target_pairs={{0,1},{1,0},{2,3},{3,2},{4,5},{5,4},{6,7},{7,6},{8,9},{9,8},{10,11... | collective-permute-start | bytes 98312 | tf_op jit(solution)/shard_map/gradient_rows/ppermute | solution.py:303
  17.4 7.5 %collective-permute-start.6 = (bf16[512,128]{1,0:T(8,128)(2,1)S(1)}, bf16[512,128]{1,0:T(8,128)(2,1)S(1)}, u32[]{:S(2)}, u32[]{:S(2)}) collective-permute-start(bf16[512,128]{1,0:T(8,128)(2,1)S(1)} %collective-permute-done.5.straight), channel_id=1, source_target_pairs={{0,1},{1,0},{2,3},{3,2},{4,5},{5,4},{6,7},{7,6},{8,9},{9,8},{10,11... | collective-permute-start | bytes 393224 | tf_op jit(solution)/shard_map/cache_pair/ppermute | solution.py:303
  19.5 9.1 %collective-permute-start.4 = (bf16[2,2,16,512]{3,2,1,0:T(8,128)(2,1)S(1)}, bf16[2,2,16,512]{3,2,1,0:T(8,128)(2,1)S(1)}, u32[]{:S(2)}, u32[]{:S(2)}) collective-permute-start(bf16[2,2,16,512]{3,2,1,0:T(8,128)(2,1)S(1)} %pad_maximum_fusion.refs_0_), channel_id=1, source_target_pairs={{0,6},{1,7},{2,0},{3,1},{4,2},{5,3},{6,4},{7,5},{8,14},{9,15},{10,... | collective-permute-start | bytes 196616 | tf_op jit(solution)/shard_map/gradient_rows/ppermute | solution.py:306
  22.0 8.7 %collective-permute-start.3 = (bf16[2,2,16,512]{3,2,1,0:T(8,128)(2,1)S(1)}, bf16[2,2,16,512]{3,2,1,0:T(8,128)(2,1)S(1)}, u32[]{:S(2)}, u32[]{:S(2)}) collective-permute-start(bf16[2,2,16,512]{3,2,1,0:T(8,128)(2,1)S(1)} %pad_maximum_fusion.refs_0_), channel_id=1, source_target_pairs={{0,4},{1,5},{2,6},{3,7},{4,0},{5,1},{6,2},{7,3},{8,12},{9,13},{10,... | collective-permute-start | bytes 196616 | tf_op jit(solution)/shard_map/gradient_rows/ppermute | solution.py:306
  24.2 6.5 %collective-permute-start.2 = (bf16[2,2,16,512]{3,2,1,0:T(8,128)(2,1)S(1)}, bf16[2,2,16,512]{3,2,1,0:T(8,128)(2,1)S(1)}, u32[]{:S(2)}, u32[]{:S(2)}) collective-permute-start(bf16[2,2,16,512]{3,2,1,0:T(8,128)(2,1)S(1)} %pad_maximum_fusion.refs_0_), channel_id=1, source_target_pairs={{0,2},{1,3},{2,4},{3,5},{4,6},{5,7},{6,0},{7,1},{8,10},{9,11},{10,... | collective-permute-start | bytes 196616 | tf_op jit(solution)/shard_map/gradient_rows/ppermute | solution.py:306
  33.6 37.8 %copy-start.1 = (bf16[512,512]{1,0:T(8,128)(2,1)S(1)}, bf16[512,512]{1,0:T(8,128)(2,1)}, u32[]{:S(2)}) copy-start(bf16[512,512]{1,0:T(8,128)(2,1)} %key_ref.1) | copy-start | bytes 1572868
  79.6 4.2 %collective-permute-start.7 = (bf16[2,4,64,256]{3,2,1,0:T(8,128)(2,1)S(1)}, bf16[2,4,64,256]{3,2,1,0:T(8,128)(2,1)S(1)}, u32[]{:S(2)}, u32[]{:S(2)}) collective-permute-start(bf16[2,4,64,256]{3,2,1,0:T(8,128)(2,1)S(1)} %get-tuple-element.55), channel_id=1, source_target_pairs={{0,1},{1,0},{2,3},{3,2},{4,5},{5,4},{6,7},{7,6},{8,9},{9,8},{10,11... | collective-permute-start | bytes 786440 | tf_op jit(solution)/shard_map/cache_terms/ppermute | solution.py:303
  83.8 9.4 %collective-permute-start.8 = (bf16[4,64,256]{2,1,0:T(8,128)(2,1)S(1)}, bf16[4,64,256]{2,1,0:T(8,128)(2,1)S(1)}, u32[]{:S(2)}, u32[]{:S(2)}) collective-permute-start(bf16[4,64,256]{2,1,0:T(8,128)(2,1)S(1)} %fusion.2), channel_id=1, source_target_pairs={{0,128},{128,0},{1,129},{129,1},{2,130},{130,2},{3,131},{131,3},{4... | collective-permute-start | bytes 393224 | tf_op jit(solution)/shard_map/cache_terms/ppermute | solution.py:300
  85.6 15.2 %all-to-all-start.2 = ((bf16[16,16,1024]{2,1,0:T(8,128)(2,1)}), bf16[16,16,1024]{2,1,0:T(8,128)(2,1)S(1)}, u32[]{:S(2)}, u32[]{:S(2)}) async-start(bf16[16,16,1024]{2,1,0:T(8,128)(2,1)} %get-tuple-element.53), calls=%async_computation.2 | async-start | bytes 1048576 | tf_op jit(solution)/shard_map/all_to_all | solution.py:397
  93.3 3.8 %collective-permute-start.11 = (bf16[64,256]{1,0:T(8,128)(2,1)S(1)}, bf16[64,256]{1,0:T(8,128)(2,1)S(1)}, u32[]{:S(2)}, u32[]{:S(2)}) collective-permute-start(bf16[64,256]{1,0:T(8,128)(2,1)S(1)} %get-tuple-element.61), channel_id=1, source_target_pairs={{0,6},{1,7},{2,0},{3,1},{4,2},{5,3},{6,4},{7,5},{8,14},{9,15},{10,... | collective-permute-start | bytes 98312 | tf_op jit(solution)/shard_map/cache_terms/ppermute | solution.py:306
  96.0 4.0 %collective-permute-start.10 = (bf16[64,256]{1,0:T(8,128)(2,1)S(1)}, bf16[64,256]{1,0:T(8,128)(2,1)S(1)}, u32[]{:S(2)}, u32[]{:S(2)}) collective-permute-start(bf16[64,256]{1,0:T(8,128)(2,1)S(1)} %get-tuple-element.62), channel_id=1, source_target_pairs={{0,4},{1,5},{2,6},{3,7},{4,0},{5,1},{6,2},{7,3},{8,12},{9,13},{10,... | collective-permute-start | bytes 98312 | tf_op jit(solution)/shard_map/cache_terms/ppermute | solution.py:306
  96.0 4.9 %collective-permute-start.9 = (bf16[64,256]{1,0:T(8,128)(2,1)S(1)}, bf16[64,256]{1,0:T(8,128)(2,1)S(1)}, u32[]{:S(2)}, u32[]{:S(2)}) collective-permute-start(bf16[64,256]{1,0:T(8,128)(2,1)S(1)} %get-tuple-element.63), channel_id=1, source_target_pairs={{0,2},{1,3},{2,4},{3,5},{4,6},{5,7},{6,0},{7,1},{8,10},{9,11},{10,... | collective-permute-start | bytes 98312 | tf_op jit(solution)/shard_map/cache_terms/ppermute | solution.py:306

commit v4 on v3

--- a/solution.py
+++ b/solution.py
@@ -103,7 +103,7 @@
         total_ref[pl.ds(head, 1), :] = jnp.sum(expo, axis=0, keepdims=True)
         return 0
 
-    lax.fori_loop(0, heads, one_head, 0)
+    lax.fori_loop(0, heads, one_head, 0, unroll=True)
 
 
 def own_kernel(
@@ -156,6 +156,7 @@
     total_other,
     grad_ref,
     stats_ref,
+    probs_grad_ref,
 ):
     heads, span, half = expo_own.shape
     window = route_ref.shape[1]
@@ -171,12 +172,14 @@
     def one_head(head, _):
         grad = grad_ref[:, columns(head)]
         for slot, expo_ref in enumerate((expo_own, expo_other)):
+            grad_probs = dot(values[slot], grad, ROWS)
+            probs_grad_ref[head, slot] = grad_probs
             stats_ref[1 + slot, 2, pl.ds(head, 1), :] = jnp.sum(
-                expo_ref[head] * dot(values[slot], grad, ROWS), axis=0, keepdims=True
+                expo_ref[head] * grad_probs, axis=0, keepdims=True
             )
         return 0
 
-    lax.fori_loop(0, heads, one_head, 0)
+    lax.fori_loop(0, heads, one_head, 0, unroll=True)
     stats_ref[0, 2] = stats_ref[1, 2] * factors[0] + stats_ref[2, 2] * factors[1]
     for copy in range(1, stats_ref.shape[0]):
         stats_ref[copy] = stats_ref[0]
@@ -188,9 +191,9 @@
     query_ref,
     grad_ref,
     key_ref,
-    value_ref,
     straight,
     crossed,
+    probs_grad_ref,
     expo_own,
     peak_own,
     expo_other,
@@ -212,9 +215,7 @@
     for slot, own_peak in enumerate((peak_own, peak_other)):
         factor[slot] = jnp.exp2(own_peak[...] - peak) / total
     delta[...] = jnp.sum(weight * stats_ref[:, 2], axis=0) / total
-    key_other, value_other = other_pair(place, straight, crossed)
-    keys = (key_ref[:, columns(place[KV_HEAD])], key_other)
-    values = (value_ref[:, columns(place[KV_HEAD])], value_other)
+    keys = (key_ref[:, columns(place[KV_HEAD])], other_pair(place, straight, crossed)[0])
     for slot in range(2):
         keys_turned[slot] = keys[slot].astype(F32).T.astype(BF)
     key_total[...] = jnp.zeros_like(key_total)
@@ -228,7 +229,7 @@
         for slot in range(2):
             expo_ref = (expo_own, expo_other)[slot]
             probs = expo_ref[head] * factor[slot, pl.ds(head, 1), :]
-            score_grad = (probs * (dot(values[slot], grad, ROWS) - row_delta)).astype(BF)
+            score_grad = (probs * (probs_grad_ref[head, slot] - row_delta)).astype(BF)
             value_total[slot] += dot(probs.astype(BF), grad)
             key_total[slot] += dot(score_grad, query)
             turned += dot(keys_turned[slot], score_grad)
@@ -236,7 +237,7 @@
         query_out[:, :, columns(head)] = result.reshape(query_out.shape[0], query_out.shape[1], HD)
         return 0
 
-    lax.fori_loop(0, heads, one_head, 0)
+    lax.fori_loop(0, heads, one_head, 0, unroll=True)
     slots, chips, share, _ = keep_out.shape
     for slot in range(2):
         for chip in range(chips):
@@ -364,7 +365,7 @@
         gathered = lax.all_to_all(gathered, "xy", 0, 0)
     own = (in_vmem(expo_own), peak_own)
     other = (in_vmem(expo_other), peak_other)
-    grads, stats = call(
+    grads, stats, probs_grad = call(
         delta_kernel,
         "deltas",
         (place, route, gathered, value_cache, straight, crossed)
@@ -372,7 +373,12 @@
         + (total_own,)
         + other
         + (total_other,),
-        [((half, local_heads * HD), BF), ((groups, 3, local_heads, half), F32)],
+        [
+            ((half, local_heads * HD), BF),
+            ((groups, 3, local_heads, half), F32),
+            ((local_heads, 2, span, half), F32),
+        ],
+        held=(2,),
     )
     with jax.named_scope("row_stats"):
         stats = lax.all_to_all(stats, "xy", 0, 0)
@@ -380,7 +386,7 @@
     query_part, keep, send = call(
         grads_kernel,
         "gradients",
-        (place, stats, query_window, grads, key_cache, value_cache, straight, crossed) + own + other,
+        (place, stats, query_window, grads, key_cache, straight, crossed, in_vmem(probs_grad)) + own + other,
         [
             ((groups, half // groups, local_heads * HD), BF),
             ((2, chips, share, 2 * HD), F32),

time: 102 us -> 97.5 us (0.956); the launches traced: 102 us -> 95.8 us
  Pallas kernels: 24.2 us -> 17.3 us
  waiting for transfers between devices: 11.7 us -> 14.1 us
  starting transfers between devices: 28.5 us -> 26.7 us
    pallas_call x6, Pallas kernels: 24.2 us -> 17.3 us  [call(): pl.pallas_call(kernel, in_specs=[SMEM] + [HBM if i in streamed else VMEM...]
    ppermute x6, starting transfers between devices: 8.55 us -> 7.22 us  [to_chip(): lax.ppermute(value, 'tp', [(i, (i + 2 * step) % parts) for i in range(par...]
    ppermute x3, waiting for transfers between devices: 3.94 us -> 4.97 us  [to_pair(): return lax.ppermute(value, 'zh', [(0, 1), (1, 0)])]
  transfers between devices with their start and end apart: 13 -> 13, of which waited for: 6 -> 8; matrix products, arithmetic and copies ran while one was open for 2% -> 2% of each run, Pallas kernels for 8% -> 7%
where the time goes in v4:
time: 97.5 us; the launch traced here: 95.8 us
  blocking collectives  34.2 us (35%)
  starting transfers between devices  26.7 us (27%)
  Pallas kernels  17.3 us (18%)
  waiting for transfers between devices  14.1 us (14%)
  between operations  1.48 us (2%)
  other arithmetic  1.12 us (1%)
  local copies, waits for them, and re-layouts  1.02 us (1%)
    all_to_all x1, blocking collectives, on_device(): gathered = lax.all_to_all(gathered, 'xy', 0, 0)  22.8 us
    pallas_call x6, Pallas kernels, call(): pl.pallas_call(kernel, in_specs=[SMEM] + [HBM if i in streamed else VMEM...  17.3 us
    all_to_all x1, blocking collectives, on_device(): stats = lax.all_to_all(stats, 'xy', 0, 0)  11.3 us
    ppermute x3, starting transfers between devices, to_pair(): return lax.ppermute(value, 'zh', [(0, 1), (1, 0)])  9.47 us
    ppermute x6, waiting for transfers between devices, to_chip(): lax.ppermute(value, 'tp', [(i, (i + 2 * step) % parts) for i in range(par...  7.46 us
    ppermute x6, starting transfers between devices, to_chip(): lax.ppermute(value, 'tp', [(i, (i + 2 * step) % parts) for i in range(par...  7.22 us
    ppermute x3, starting transfers between devices, to_core(): return lax.ppermute(value, 'tp', [(i, i ^ 1) for i in range(parts)])  6.45 us
    ppermute x3, waiting for transfers between devices, to_pair(): return lax.ppermute(value, 'zh', [(0, 1), (1, 0)])  4.97 us
  transfers between devices with their start and end apart: 13, of which 8 were waited for; matrix products, arithmetic and copies ran while one was open for 2% of the time, Pallas kernels for 7%

profile of v4, /device:TPU:1, one launch (start us, length us, event | category | flops | bytes accessed | tf_op | source)
XLA Modules:
  0.0 95.8 jit_solution(5855470713626943980)
XLA Ops:
  0.7 7.8 %collective-permute-start = (bf16[16,512]{1,0:T(8,128)(2,1)}, bf16[16,512]{1,0:T(8,128)(2,1)S(1)}, u32[]{:S(2)}, u32[]{:S(2)}) collective-permute-start(bf16[16,512]{1,0:T(8,128)(2,1)} %param.11), channel_id=1, source_target_pairs={{0,128},{128,0},{1,129},{129,1},{2,130},{130,2},{3,131},{131,3},{4... | collective-permute-start | bytes 49160 | tf_op jit(solution)/shard_map/gradient_rows/ppermute | solution.py:301
  8.5 1.0 %dynamic-slice_select_fusion = bf16[512,128]{1,0:T(8,128)(2,1)S(1)} fusion(bf16[512,512]{1,0:T(8,128)(2,1)} %value_ref.1, s32[]{:T(128)S(6)} %select_n.109, bf16[512,512]{1,0:T(8,128)(2,1)} %key_ref.1, pred[]{:T(512)S(6)} %eq.28), kind=kLoop, calls=%fused_computation.6 | loop fusion | flops 65536 | bytes 393221 | tf_op jit(solution)/shard_map/cache_pair/jit(_where)/select_n | solution.py:340
  11.3 4.2 %own_scores.1 = (f32[8,512,256]{2,1,0:T(8,128)S(1)}, f32[8,256]{1,0:T(8,128)S(1)}, f32[8,256]{1,0:T(8,128)S(1)}, bf16[1024,4096]{1,0:T(8,128)(2,1)S(1)}) custom-call(s32[14]{0:T(128)S(1)} %stack.73.place, bf16[512,1024]{1,0:T(8,128)(2,1)} %query_ref.3, bf16[512,512]{1,0:T(8,128)(2,1)} %key_ref.1, bf16[1024,4096]{1,0:T(8,128)(2,1)} %weight_in.1), custom_call_target="tpu_custom_call" | custom-call | flops 268435456 | bytes 4194304 | tf_op jit(solution)/shard_map/own_scores/pallas_call | solution.py:41
  15.6 1.4 %collective-permute-start.1 = (bf16[2,16,512]{2,1,0:T(8,128)(2,1)S(1)}, bf16[2,16,512]{2,1,0:T(8,128)(2,1)S(1)}, u32[]{:S(2)}, u32[]{:S(2)}) collective-permute-start(bf16[2,16,512]{2,1,0:T(8,128)(2,1)S(1)} %get-tuple-element.68), channel_id=1, source_target_pairs={{0,1},{1,0},{2,3},{3,2},{4,5},{5,4},{6,7},{7,6},{8,9},{9,8},{10,11... | collective-permute-start | bytes 98312 | tf_op jit(solution)/shard_map/gradient_rows/ppermute | solution.py:304
  17.4 2.1 %collective-permute-start.6 = (bf16[512,128]{1,0:T(8,128)(2,1)S(1)}, bf16[512,128]{1,0:T(8,128)(2,1)S(1)}, u32[]{:S(2)}, u32[]{:S(2)}) collective-permute-start(bf16[512,128]{1,0:T(8,128)(2,1)S(1)} %collective-permute-done.5.straight), channel_id=1, source_target_pairs={{0,1},{1,0},{2,3},{3,2},{4,5},{5,4},{6,7},{7,6},{8,9},{9,8},{10,11... | collective-permute-start | bytes 393224 | tf_op jit(solution)/shard_map/cache_pair/ppermute | solution.py:304
  19.5 2.4 %collective-permute-start.4 = (bf16[2,2,16,512]{3,2,1,0:T(8,128)(2,1)S(1)}, bf16[2,2,16,512]{3,2,1,0:T(8,128)(2,1)S(1)}, u32[]{:S(2)}, u32[]{:S(2)}) collective-permute-start(bf16[2,2,16,512]{3,2,1,0:T(8,128)(2,1)S(1)} %pad_maximum_fusion.refs_0_), channel_id=1, source_target_pairs={{0,6},{1,7},{2,0},{3,1},{4,2},{5,3},{6,4},{7,5},{8,14},{9,15},{10,... | collective-permute-start | bytes 196616 | tf_op jit(solution)/shard_map/gradient_rows/ppermute | solution.py:307
  22.0 2.3 %collective-permute-start.3 = (bf16[2,2,16,512]{3,2,1,0:T(8,128)(2,1)S(1)}, bf16[2,2,16,512]{3,2,1,0:T(8,128)(2,1)S(1)}, u32[]{:S(2)}, u32[]{:S(2)}) collective-permute-start(bf16[2,2,16,512]{3,2,1,0:T(8,128)(2,1)S(1)} %pad_maximum_fusion.refs_0_), channel_id=1, source_target_pairs={{0,4},{1,5},{2,6},{3,7},{4,0},{5,1},{6,2},{7,3},{8,12},{9,13},{10,... | collective-permute-start | bytes 196616 | tf_op jit(solution)/shard_map/gradient_rows/ppermute | solution.py:307
  25.0 2.0 %other_scores.1 = (f32[8,512,256]{2,1,0:T(8,128)S(1)}, f32[8,256]{1,0:T(8,128)S(1)}, f32[8,256]{1,0:T(8,128)S(1)}) custom-call(s32[14]{0:T(128)S(1)} %stack.73.place, bf16[512,1024]{1,0:T(8,128)(2,1)S(1)} %copy-done, bf16[512,128]{1,0:T(8,128)(2,1)S(1)} %collective-permute-done.5.straight, bf16[512,128]{1,0:T(8,128)(2,1)S(1)} %collective-permute-done.6.crossed), custom_call_target="tpu_custom_call" | custom-call | flops 268435456 | bytes 4194304 | tf_op jit(solution)/shard_map/other_scores/pallas_call | solution.py:41
  27.0 3.7 %collective-permute-done.3.refs_2_ = bf16[2,2,16,512]{3,2,1,0:T(8,128)(2,1)S(1)} collective-permute-done((bf16[2,2,16,512]{3,2,1,0:T(8,128)(2,1)S(1)}, bf16[2,2,16,512]{3,2,1,0:T(8,128)(2,1)S(1)}, u32[]{:S(2)}, u32[]{:S(2)}) %collective-permute-start.3) | collective-permute-done | bytes 65568 | tf_op jit(solution)/shard_map/gradient_rows/ppermute | solution.py:307
  30.7 2.9 %project.1 = bf16[16,32,1024]{2,1,0:T(8,128)(2,1)S(1)} custom-call(s32[14]{0:T(128)S(1)} %stack.73.place, bf16[2,2,16,512]{3,2,1,0:T(8,128)(2,1)S(1)} %pad_maximum_fusion.refs_0_, bf16[2,2,16,512]{3,2,1,0:T(8,128)(2,1)S(1)} %collective-permute-done.2.refs_1_, bf16[2,2,16,512]{3,2,1,0:T(8,128)(2,1)S(1)} %collective-permute-done.3.refs_2_, ...), custom_call_target="tpu_custom_call" | custom-call | tf_op jit(solution)/shard_map/project/pallas_call | solution.py:41
  33.6 22.8 %all_to_all.15.gathered_ref = bf16[16,32,1024]{2,1,0:T(8,128)(2,1)S(1)} all-to-all(bf16[16,32,1024]{2,1,0:T(8,128)(2,1)S(1)} %project.1), channel_id=1, replica_groups=mesh['zh'=2,'xy'=16,'tp'=8] {'xy'}, dimensions={0} | all-to-all | bytes 2097152 | tf_op jit(solution)/shard_map/head_gradients/all_to_all | solution.py:365
  56.5 2.1 %deltas.1 = (bf16[256,1024]{1,0:T(8,128)(2,1)S(1)}, f32[16,3,8,256]{3,2,1,0:T(8,128)S(1)}, f32[8,2,512,256]{3,2,1,0:T(8,128)S(1)}) custom-call(s32[14]{0:T(128)S(1)} %stack.73.place, s32[1,512]{1,0:T(1,128)S(1)} %reshape.14.route_ref, bf16[16,32,1024]{2,1,0:T(8,128)(2,1)S(1)} %all_to_all.15.gathered_ref, bf16[512,512]{1,0:T(8,128)(2,1)S(1)} %copy-done.2, ...), custom_call_target="tpu_custom_call" | custom-call | tf_op jit(solution)/shard_map/deltas/pallas_call | solution.py:41
  58.6 11.3 %all_to_all.16.stats_ref = f32[16,3,8,256]{3,2,1,0:T(8,128)S(1)} all-to-all(f32[16,3,8,256]{3,2,1,0:T(8,128)S(1)} %get-tuple-element.52), channel_id=1, replica_groups=mesh['zh'=2,'xy'=16,'tp'=8] {'xy'}, dimensions={0} | all-to-all | bytes 786432 | tf_op jit(solution)/shard_map/row_stats/all_to_all | solution.py:384
  69.9 4.8 %gradients.1 = (bf16[16,16,1024]{2,1,0:T(8,128)(2,1)}, f32[2,4,64,256]{3,2,1,0:T(8,128)S(1)}, bf16[2,4,64,256]{3,2,1,0:T(8,128)(2,1)S(1)}) custom-call(s32[14]{0:T(128)S(1)} %stack.73.place, f32[16,3,8,256]{3,2,1,0:T(8,128)S(1)} %all_to_all.16.stats_ref, bf16[512,1024]{1,0:T(8,128)(2,1)S(1)} %copy-done, bf16[256,1024]{1,0:T(8,128)(2,1)S(1)} %get-tuple-element.53.grad_ref, ...), custom_call_target="tpu_custom_call" | custom-call | tf_op jit(solution)/shard_map/gradients/pallas_call | solution.py:41
  74.7 3.0 %collective-permute-start.7 = (bf16[2,4,64,256]{3,2,1,0:T(8,128)(2,1)S(1)}, bf16[2,4,64,256]{3,2,1,0:T(8,128)(2,1)S(1)}, u32[]{:S(2)}, u32[]{:S(2)}) collective-permute-start(bf16[2,4,64,256]{3,2,1,0:T(8,128)(2,1)S(1)} %get-tuple-element.57), channel_id=1, source_target_pairs={{0,1},{1,0},{2,3},{3,2},{4,5},{5,4},{6,7},{7,6},{8,9},{9,8},{10,11... | collective-permute-start | bytes 786440 | tf_op jit(solution)/shard_map/cache_terms/ppermute | solution.py:304
  77.7 1.2 %collective-permute-done.7 = bf16[2,4,64,256]{3,2,1,0:T(8,128)(2,1)S(1)} collective-permute-done((bf16[2,4,64,256]{3,2,1,0:T(8,128)(2,1)S(1)}, bf16[2,4,64,256]{3,2,1,0:T(8,128)(2,1)S(1)}, u32[]{:S(2)}, u32[]{:S(2)}) %collective-permute-start.7) | collective-permute-done | bytes 262176 | tf_op jit(solution)/shard_map/cache_terms/ppermute | solution.py:304
  78.9 1.4 %collective-permute-start.8 = (bf16[4,64,256]{2,1,0:T(8,128)(2,1)S(1)}, bf16[4,64,256]{2,1,0:T(8,128)(2,1)S(1)}, u32[]{:S(2)}, u32[]{:S(2)}) collective-permute-start(bf16[4,64,256]{2,1,0:T(8,128)(2,1)S(1)} %fusion.2), channel_id=1, source_target_pairs={{0,128},{128,0},{1,129},{129,1},{2,130},{130,2},{3,131},{131,3},{4... | collective-permute-start | bytes 393224 | tf_op jit(solution)/shard_map/cache_terms/ppermute | solution.py:301
  80.3 3.6 %all-to-all-start.2 = ((bf16[16,16,1024]{2,1,0:T(8,128)(2,1)}), bf16[16,16,1024]{2,1,0:T(8,128)(2,1)S(1)}, u32[]{:S(2)}, u32[]{:S(2)}) async-start(bf16[16,16,1024]{2,1,0:T(8,128)(2,1)} %get-tuple-element.55), calls=%async_computation.2 | async-start | bytes 1048576 | tf_op jit(solution)/shard_map/all_to_all | solution.py:403
  83.9 4.5 %collective-permute-done.8 = bf16[4,64,256]{2,1,0:T(8,128)(2,1)S(1)} collective-permute-done((bf16[4,64,256]{2,1,0:T(8,128)(2,1)S(1)}, bf16[4,64,256]{2,1,0:T(8,128)(2,1)S(1)}, u32[]{:S(2)}, u32[]{:S(2)}) %collective-permute-start.8) | collective-permute-done | bytes 131104 | tf_op jit(solution)/shard_map/cache_terms/ppermute | solution.py:301
  89.2 1.2 %collective-permute-start.9 = (bf16[64,256]{1,0:T(8,128)(2,1)S(1)}, bf16[64,256]{1,0:T(8,128)(2,1)S(1)}, u32[]{:S(2)}, u32[]{:S(2)}) collective-permute-start(bf16[64,256]{1,0:T(8,128)(2,1)S(1)} %get-tuple-element.65), channel_id=1, source_target_pairs={{0,2},{1,3},{2,4},{3,5},{4,6},{5,7},{6,0},{7,1},{8,10},{9,11},{10,... | collective-permute-start | bytes 98312 | tf_op jit(solution)/shard_map/cache_terms/ppermute | solution.py:307
  90.3 1.4 %collective-permute-done.11.refs_3_ = bf16[64,256]{1,0:T(8,128)(2,1)S(1)} collective-permute-done((bf16[64,256]{1,0:T(8,128)(2,1)S(1)}, bf16[64,256]{1,0:T(8,128)(2,1)S(1)}, u32[]{:S(2)}, u32[]{:S(2)}) %collective-permute-start.11) | collective-permute-done | bytes 32800 | tf_op jit(solution)/shard_map/cache_terms/ppermute | solution.py:307
  91.7 1.4 %collective-permute-done.10.refs_2_ = bf16[64,256]{1,0:T(8,128)(2,1)S(1)} collective-permute-done((bf16[64,256]{1,0:T(8,128)(2,1)S(1)}, bf16[64,256]{1,0:T(8,128)(2,1)S(1)}, u32[]{:S(2)}, u32[]{:S(2)}) %collective-permute-start.10) | collective-permute-done | bytes 32800 | tf_op jit(solution)/shard_map/cache_terms/ppermute | solution.py:307
  93.1 1.0 %collective-permute-done.9.refs_1_ = bf16[64,256]{1,0:T(8,128)(2,1)S(1)} collective-permute-done((bf16[64,256]{1,0:T(8,128)(2,1)S(1)}, bf16[64,256]{1,0:T(8,128)(2,1)S(1)}, u32[]{:S(2)}, u32[]{:S(2)}) %collective-permute-start.9) | collective-permute-done | bytes 32800 | tf_op jit(solution)/shard_map/cache_terms/ppermute | solution.py:307
  94.6 1.2 %finish.1 = (bf16[16,1024]{1,0:T(8,128)(2,1)}, bf16[64,512]{1,0:T(8,128)(2,1)}, bf16[64,512]{1,0:T(8,128)(2,1)}) custom-call(s32[14]{0:T(128)S(1)} %stack.73.place, bf16[16,16,1024]{2,1,0:T(8,128)(2,1)S(1)} %all-to-all-done.2.terms_ref, bf16[64,256]{1,0:T(8,128)(2,1)S(1)} %get-tuple-element.59.refs_0_, bf16[64,256]{1,0:T(8,128)(2,1)S(1)} %collective-permute-done.9.refs_1_, ...), custom_call_target="tpu_custom_call" | custom-call | tf_op jit(solution)/shard_map/finish/pallas_call | solution.py:41
  (30 shorter events, 3.6 us)
Async XLA Ops:
  0.6 14.9 %copy-start.3 = (bf16[16,512]{1,0:T(8,128)(2,1)S(1)}, bf16[16,512]{1,0:T(8,128)(2,1)}, u32[]{:S(2)}) copy-start(bf16[16,512]{1,0:T(8,128)(2,1)} %param.11) | copy-start | bytes 49156
  0.6 24.3 %copy-start = (bf16[512,1024]{1,0:T(8,128)(2,1)S(1)}, bf16[512,1024]{1,0:T(8,128)(2,1)}, u32[]{:S(2)}) copy-start(bf16[512,1024]{1,0:T(8,128)(2,1)} %query_ref.3) | copy-start | bytes 3145732
  0.7 14.9 %collective-permute-start = (bf16[16,512]{1,0:T(8,128)(2,1)}, bf16[16,512]{1,0:T(8,128)(2,1)S(1)}, u32[]{:S(2)}, u32[]{:S(2)}) collective-permute-start(bf16[16,512]{1,0:T(8,128)(2,1)} %param.11), channel_id=1, source_target_pairs={{0,128},{128,0},{1,129},{129,1},{2,130},{130,2},{3,131},{131,3},{4... | collective-permute-start | bytes 49160 | tf_op jit(solution)/shard_map/gradient_rows/ppermute | solution.py:301
  9.5 7.9 %collective-permute-start.5 = (bf16[512,128]{1,0:T(8,128)(2,1)S(1)}, bf16[512,128]{1,0:T(8,128)(2,1)S(1)}, u32[]{:S(2)}, u32[]{:S(2)}) collective-permute-start(bf16[512,128]{1,0:T(8,128)(2,1)S(1)} %dynamic-slice_select_fusion), channel_id=1, source_target_pairs={{0,128},{128,0},{1,129},{129,1},{2,130},{130,2},{3,131},{131,3},{4... | collective-permute-start | bytes 393224 | tf_op jit(solution)/shard_map/cache_pair/ppermute | solution.py:301
  15.5 41.0 %copy-start.2 = (bf16[512,512]{1,0:T(8,128)(2,1)S(1)}, bf16[512,512]{1,0:T(8,128)(2,1)}, u32[]{:S(2)}) copy-start(bf16[512,512]{1,0:T(8,128)(2,1)} %value_ref.1) | copy-start | bytes 1572868
  15.6 3.9 %collective-permute-start.1 = (bf16[2,16,512]{2,1,0:T(8,128)(2,1)S(1)}, bf16[2,16,512]{2,1,0:T(8,128)(2,1)S(1)}, u32[]{:S(2)}, u32[]{:S(2)}) collective-permute-start(bf16[2,16,512]{2,1,0:T(8,128)(2,1)S(1)} %get-tuple-element.68), channel_id=1, source_target_pairs={{0,1},{1,0},{2,3},{3,2},{4,5},{5,4},{6,7},{7,6},{8,9},{9,8},{10,11... | collective-permute-start | bytes 98312 | tf_op jit(solution)/shard_map/gradient_rows/ppermute | solution.py:304
  17.4 7.6 %collective-permute-start.6 = (bf16[512,128]{1,0:T(8,128)(2,1)S(1)}, bf16[512,128]{1,0:T(8,128)(2,1)S(1)}, u32[]{:S(2)}, u32[]{:S(2)}) collective-permute-start(bf16[512,128]{1,0:T(8,128)(2,1)S(1)} %collective-permute-done.5.straight), channel_id=1, source_target_pairs={{0,1},{1,0},{2,3},{3,2},{4,5},{5,4},{6,7},{7,6},{8,9},{9,8},{10,11... | collective-permute-start | bytes 393224 | tf_op jit(solution)/shard_map/cache_pair/ppermute | solution.py:304
  19.5 7.5 %collective-permute-start.4 = (bf16[2,2,16,512]{3,2,1,0:T(8,128)(2,1)S(1)}, bf16[2,2,16,512]{3,2,1,0:T(8,128)(2,1)S(1)}, u32[]{:S(2)}, u32[]{:S(2)}) collective-permute-start(bf16[2,2,16,512]{3,2,1,0:T(8,128)(2,1)S(1)} %pad_maximum_fusion.refs_0_), channel_id=1, source_target_pairs={{0,6},{1,7},{2,0},{3,1},{4,2},{5,3},{6,4},{7,5},{8,14},{9,15},{10,... | collective-permute-start | bytes 196616 | tf_op jit(solution)/shard_map/gradient_rows/ppermute | solution.py:307
  22.0 8.7 %collective-permute-start.3 = (bf16[2,2,16,512]{3,2,1,0:T(8,128)(2,1)S(1)}, bf16[2,2,16,512]{3,2,1,0:T(8,128)(2,1)S(1)}, u32[]{:S(2)}, u32[]{:S(2)}) collective-permute-start(bf16[2,2,16,512]{3,2,1,0:T(8,128)(2,1)S(1)} %pad_maximum_fusion.refs_0_), channel_id=1, source_target_pairs={{0,4},{1,5},{2,6},{3,7},{4,0},{5,1},{6,2},{7,3},{8,12},{9,13},{10,... | collective-permute-start | bytes 196616 | tf_op jit(solution)/shard_map/gradient_rows/ppermute | solution.py:307
  24.2 6.5 %collective-permute-start.2 = (bf16[2,2,16,512]{3,2,1,0:T(8,128)(2,1)S(1)}, bf16[2,2,16,512]{3,2,1,0:T(8,128)(2,1)S(1)}, u32[]{:S(2)}, u32[]{:S(2)}) collective-permute-start(bf16[2,2,16,512]{3,2,1,0:T(8,128)(2,1)S(1)} %pad_maximum_fusion.refs_0_), channel_id=1, source_target_pairs={{0,2},{1,3},{2,4},{3,5},{4,6},{5,7},{6,0},{7,1},{8,10},{9,11},{10,... | collective-permute-start | bytes 196616 | tf_op jit(solution)/shard_map/gradient_rows/ppermute | solution.py:307
  33.6 36.3 %copy-start.1 = (bf16[512,512]{1,0:T(8,128)(2,1)S(1)}, bf16[512,512]{1,0:T(8,128)(2,1)}, u32[]{:S(2)}) copy-start(bf16[512,512]{1,0:T(8,128)(2,1)} %key_ref.1) | copy-start | bytes 1572868
  74.7 4.1 %collective-permute-start.7 = (bf16[2,4,64,256]{3,2,1,0:T(8,128)(2,1)S(1)}, bf16[2,4,64,256]{3,2,1,0:T(8,128)(2,1)S(1)}, u32[]{:S(2)}, u32[]{:S(2)}) collective-permute-start(bf16[2,4,64,256]{3,2,1,0:T(8,128)(2,1)S(1)} %get-tuple-element.57), channel_id=1, source_target_pairs={{0,1},{1,0},{2,3},{3,2},{4,5},{5,4},{6,7},{7,6},{8,9},{9,8},{10,11... | collective-permute-start | bytes 786440 | tf_op jit(solution)/shard_map/cache_terms/ppermute | solution.py:304
  78.9 9.6 %collective-permute-start.8 = (bf16[4,64,256]{2,1,0:T(8,128)(2,1)S(1)}, bf16[4,64,256]{2,1,0:T(8,128)(2,1)S(1)}, u32[]{:S(2)}, u32[]{:S(2)}) collective-permute-start(bf16[4,64,256]{2,1,0:T(8,128)(2,1)S(1)} %fusion.2), channel_id=1, source_target_pairs={{0,128},{128,0},{1,129},{129,1},{2,130},{130,2},{3,131},{131,3},{4... | collective-permute-start | bytes 393224 | tf_op jit(solution)/shard_map/cache_terms/ppermute | solution.py:301
  80.3 14.3 %all-to-all-start.2 = ((bf16[16,16,1024]{2,1,0:T(8,128)(2,1)}), bf16[16,16,1024]{2,1,0:T(8,128)(2,1)S(1)}, u32[]{:S(2)}, u32[]{:S(2)}) async-start(bf16[16,16,1024]{2,1,0:T(8,128)(2,1)} %get-tuple-element.55), calls=%async_computation.2 | async-start | bytes 1048576 | tf_op jit(solution)/shard_map/all_to_all | solution.py:403
  88.5 3.1 %collective-permute-start.11 = (bf16[64,256]{1,0:T(8,128)(2,1)S(1)}, bf16[64,256]{1,0:T(8,128)(2,1)S(1)}, u32[]{:S(2)}, u32[]{:S(2)}) collective-permute-start(bf16[64,256]{1,0:T(8,128)(2,1)S(1)} %get-tuple-element.63), channel_id=1, source_target_pairs={{0,6},{1,7},{2,0},{3,1},{4,2},{5,3},{6,4},{7,5},{8,14},{9,15},{10,... | collective-permute-start | bytes 98312 | tf_op jit(solution)/shard_map/cache_terms/ppermute | solution.py:307
  89.2 4.0 %collective-permute-start.10 = (bf16[64,256]{1,0:T(8,128)(2,1)S(1)}, bf16[64,256]{1,0:T(8,128)(2,1)S(1)}, u32[]{:S(2)}, u32[]{:S(2)}) collective-permute-start(bf16[64,256]{1,0:T(8,128)(2,1)S(1)} %get-tuple-element.64), channel_id=1, source_target_pairs={{0,4},{1,5},{2,6},{3,7},{4,0},{5,1},{6,2},{7,3},{8,12},{9,13},{10,... | collective-permute-start | bytes 98312 | tf_op jit(solution)/shard_map/cache_terms/ppermute | solution.py:307
  89.2 5.0 %collective-permute-start.9 = (bf16[64,256]{1,0:T(8,128)(2,1)S(1)}, bf16[64,256]{1,0:T(8,128)(2,1)S(1)}, u32[]{:S(2)}, u32[]{:S(2)}) collective-permute-start(bf16[64,256]{1,0:T(8,128)(2,1)S(1)} %get-tuple-element.65), channel_id=1, source_target_pairs={{0,2},{1,3},{2,4},{3,5},{4,6},{5,7},{6,0},{7,1},{8,10},{9,11},{10,... | collective-permute-start | bytes 98312 | tf_op jit(solution)/shard_map/cache_terms/ppermute | solution.py:307

commit v5 on v4

--- a/solution.py
+++ b/solution.py
@@ -70,10 +70,10 @@
 
 def project_kernel(place, *refs):
     pieces, weight_ref, out_ref = refs[:-2], refs[-2], refs[-1]
-    cores, lines, rows, width = pieces[0].shape
+    cores, _, width = pieces[0].shape
     total = None
     for index in range(len(pieces) * cores):
-        piece = pieces[index // cores][index % cores].reshape(lines * rows, width)
+        piece = pieces[index // cores][index % cores]
         term = dot(weight_ref[:, columns(place[BLOCKS + index], width)], piece, ROWS)
         total = term if total is None else total + term
     result = total.T.astype(BF)
@@ -87,14 +87,18 @@
     return jnp.where(swap, second, first), jnp.where(swap, first, second)
 
 
-def score_heads(place, slot, first_row, query_ref, keys, expo_ref, peak_ref, total_ref):
-    heads, span, window = expo_ref.shape
-    query_pos = place[START] + place[LINE] * window + lax.broadcasted_iota(jnp.int32, (1, window), 1)
+def picked(place, route_ref, window, half):
+    tokens = route_ref[:, columns(place[LINE], half)]
+    rows = lax.broadcasted_iota(jnp.int32, (window, half), 0) == tokens
+    return tokens, jnp.where(rows, 1.0, 0.0).astype(BF)
+
+
+def score_heads(place, slot, query_pos, query_ref, keys, expo_ref, peak_ref, total_ref):
+    heads, span, _ = expo_ref.shape
     key_pos = place[FIRST + slot] + lax.broadcasted_iota(jnp.int32, (span, 1), 0)
 
     def one_head(head, _):
-        query = query_ref[pl.ds(first_row, window), columns(head)]
-        scored = dot(keys, query, ROWS) * (SCALE * LOG2E)
+        scored = dot(keys, query_ref[:, columns(head)], ROWS) * (SCALE * LOG2E)
         scored = jnp.where(key_pos <= query_pos, scored, NEG)
         peak = jnp.maximum(jnp.max(scored, axis=0, keepdims=True), FLOOR)
         expo = jnp.exp2(scored - peak)
@@ -108,6 +112,7 @@
 
 def own_kernel(
     place,
+    route_ref,
     query_in,
     key_in,
     weight_in,
@@ -116,35 +121,36 @@
     total_ref,
     weight_out,
     query_ref,
+    all_query_ref,
     key_ref,
     loaded,
 ):
-    window = query_ref.shape[0]
-    rows = pl.ds(pl.multiple_of(place[LINE] * window, window), window)
     copies = [
-        pltpu.make_async_copy(query_in.at[rows], query_ref, loaded.at[0]),
+        pltpu.make_async_copy(query_in, all_query_ref, loaded.at[0]),
         pltpu.make_async_copy(key_in.at[:, columns(place[KV_HEAD])], key_ref, loaded.at[1]),
         pltpu.make_async_copy(weight_in, weight_out, loaded.at[2]),
     ]
     for copy in copies:
         copy.start()
+    tokens, pick = picked(place, route_ref, all_query_ref.shape[0], query_ref.shape[0])
     copies[0].wait()
     copies[1].wait()
-    score_heads(place, 0, 0, query_ref, key_ref[...], expo_ref, peak_ref, total_ref)
+    query_ref[...] = dot(pick, all_query_ref[...], (((0,), (0,)), ((), ()))).astype(BF)
+    score_heads(
+        place, 0, place[START] + tokens, query_ref, key_ref[...], expo_ref, peak_ref, total_ref
+    )
     copies[2].wait()
 
 
-def other_kernel(place, query_ref, straight, crossed, expo_ref, peak_ref, total_ref):
+def other_kernel(place, route_ref, query_ref, straight, crossed, expo_ref, peak_ref, total_ref):
     keys = other_pair(place, straight, crossed)[0]
-    window = expo_ref.shape[2]
-    first_row = pl.multiple_of(place[LINE] * window, window)
-    score_heads(place, 1, first_row, query_ref, keys, expo_ref, peak_ref, total_ref)
+    query_pos = place[START] + route_ref[:, columns(place[LINE], expo_ref.shape[2])]
+    score_heads(place, 1, query_pos, query_ref, keys, expo_ref, peak_ref, total_ref)
 
 
 def delta_kernel(
     place,
-    route_ref,
-    gathered_ref,
+    grad_ref,
     value_ref,
     straight,
     crossed,
@@ -154,16 +160,11 @@
     expo_other,
     peak_other,
     total_other,
-    grad_ref,
     stats_ref,
     probs_grad_ref,
 ):
     heads, span, half = expo_own.shape
-    window = route_ref.shape[1]
-    token = place[LINE] * half + lax.broadcasted_iota(jnp.int32, (half, window), 0)
-    pick = jnp.where(route_ref[...] == token, 1.0, 0.0).astype(BF)
     values = (value_ref[:, columns(place[KV_HEAD])], other_pair(place, straight, crossed)[1])
-    grad_ref[...] = dot(pick, gathered_ref[...].reshape(window, heads * HD)).astype(BF)
     peak = jnp.maximum(peak_own[...], peak_other[...])
     factors = (jnp.exp2(peak_own[...] - peak), jnp.exp2(peak_other[...] - peak))
     stats_ref[0, 0] = peak
@@ -187,6 +188,7 @@
 
 def grads_kernel(
     place,
+    route_ref,
     stats_ref,
     query_ref,
     grad_ref,
@@ -208,6 +210,9 @@
     value_total,
 ):
     heads, span, half = expo_own.shape
+    owners, rows, _ = query_out.shape
+    rows //= 2
+    _, pick = picked(place, route_ref, 2 * half, half)
     peaks = stats_ref[:, 0]
     peak = jnp.max(peaks, axis=0)
     weight = jnp.exp2(peaks - peak[None])
@@ -222,7 +227,7 @@
     value_total[...] = jnp.zeros_like(value_total)
 
     def one_head(head, _):
-        query = query_ref[pl.ds(place[LINE] * half, half), columns(head)]
+        query = query_ref[:, columns(head)]
         grad = grad_ref[:, columns(head)]
         row_delta = delta[pl.ds(head, 1), :]
         turned = jnp.zeros((HD, half), F32)
@@ -233,8 +238,11 @@
             value_total[slot] += dot(probs.astype(BF), grad)
             key_total[slot] += dot(score_grad, query)
             turned += dot(keys_turned[slot], score_grad)
-        result = (SCALE * turned).T.astype(BF)
-        query_out[:, :, columns(head)] = result.reshape(query_out.shape[0], query_out.shape[1], HD)
+        result = dot(pick, (SCALE * turned).astype(BF), ROWS).astype(BF)
+        for line in range(2):
+            query_out[:, line * rows : (line + 1) * rows, columns(head)] = result[
+                line * half : (line + 1) * half
+            ].reshape(owners, rows, HD)
         return 0
 
     lax.fori_loop(0, heads, one_head, 0, unroll=True)
@@ -251,9 +259,17 @@
                 ).astype(BF)
 
 
-def finish_kernel(place, terms_ref, *refs):
+def query_kernel(place, terms_ref, keep_ref, send_ref):
+    rows = keep_ref.shape[0]
+    mine = pl.multiple_of(place[LINE] * rows, rows)
+    theirs = pl.multiple_of((1 - place[LINE]) * rows, rows)
+    keep_ref[...] = jnp.sum(terms_ref[:, pl.ds(mine, rows)].astype(F32), axis=0)
+    send_ref[...] = jnp.sum(terms_ref[:, pl.ds(theirs, rows)].astype(F32), axis=0).astype(BF)
+
+
+def finish_kernel(place, kept_ref, came_ref, *refs):
     pieces, (query_out, key_out, value_out) = refs[:-3], refs[-3:]
-    query_out[...] = jnp.sum(terms_ref[...].astype(F32), axis=0).astype(BF)
+    query_out[...] = (kept_ref[...] + came_ref[...].astype(F32)).astype(BF)
     for step, piece in enumerate(pieces):
         where = columns(place[BLOCKS + 2 * step] // 2)
         key_out[:, where] = piece[:, :HD]
@@ -295,8 +311,8 @@
         + pieces
     ).astype(jnp.int32)
 
-    route = token_route.reshape(lines, groups, rows)
-    route = jnp.where(line == 0, route, route[::-1]).transpose(1, 0, 2).reshape(1, window)
+    route = token_route.reshape(1, window)
+
     def to_pair(value):
         return lax.ppermute(value, "zh", [(0, 1), (1, 0)])
 
@@ -316,25 +332,24 @@
         ((local_heads, half), F32),
         ((local_heads, half), F32),
     ]
-    expo_own, peak_own, total_own, weight = call(
+    expo_own, peak_own, total_own, weight, queries = call(
         own_kernel,
         "own_scores",
-        (place, in_hbm(query_window), in_hbm(key_cache), in_hbm(out_weight)),
-        score_outs + [(out_weight.shape, BF)],
+        (place, route, in_hbm(query_window), in_hbm(key_cache), in_hbm(out_weight)),
+        score_outs + [(out_weight.shape, BF), ((half, local_heads * HD), BF)],
         scratch=[
-            pltpu.VMEM((half, local_heads * HD), BF),
+            pltpu.VMEM(query_window.shape, BF),
             pltpu.VMEM((span, HD), BF),
             pltpu.SemaphoreType.DMA((3,)),
         ],
         cost=score_cost,
-        streamed=(1, 2, 3),
+        streamed=(2, 3, 4),
         held=(0, 3),
     )
     with jax.named_scope("gradient_rows"):
-        other_rows = to_pair(grad_routed)
-        other_rows, weight, route = lax.optimization_barrier((other_rows, weight, route))
-        pair = jnp.stack([grad_routed, other_rows])
-        chip_rows = jnp.stack([pair, to_core(pair)])
+        core_rows = to_core(grad_routed)
+        core_rows, weight = lax.optimization_barrier((core_rows, weight))
+        chip_rows = jnp.stack([grad_routed, core_rows])
         all_rows = [chip_rows] + [to_chip(chip_rows, step) for step in range(1, chips)]
     with jax.named_scope("cache_pair"):
         mine = jnp.where(
@@ -342,12 +357,12 @@
             lax.dynamic_slice_in_dim(key_cache, kv_head * HD, HD, 1),
             lax.dynamic_slice_in_dim(value_cache, kv_head * HD, HD, 1),
         )
-        straight = to_pair(mine)
+        straight, _ = lax.optimization_barrier((to_pair(mine), peak_own))
         crossed = to_core(straight)
     expo_other, peak_other, total_other = call(
         other_kernel,
         "other_scores",
-        (place, query_window, straight, crossed),
+        (place, route, queries, straight, crossed),
         score_outs,
         cost=score_cost,
         held=(0,),
@@ -359,26 +374,25 @@
         project_kernel,
         "project",
         (place, *all_rows, in_vmem(weight)),
-        [((groups, lines * rows, local_heads * HD), BF)],
+        [((groups, rows, local_heads * HD), BF)],
     )
     with jax.named_scope("head_gradients"):
-        gathered = lax.all_to_all(gathered, "xy", 0, 0)
+        grads = lax.all_to_all(gathered, "xy", 0, 0).reshape(half, local_heads * HD)
     own = (in_vmem(expo_own), peak_own)
     other = (in_vmem(expo_other), peak_other)
-    grads, stats, probs_grad = call(
+    stats, probs_grad = call(
         delta_kernel,
         "deltas",
-        (place, route, gathered, value_cache, straight, crossed)
+        (place, grads, value_cache, straight, crossed)
         + own
         + (total_own,)
         + other
         + (total_other,),
         [
-            ((half, local_heads * HD), BF),
             ((groups, 3, local_heads, half), F32),
             ((local_heads, 2, span, half), F32),
         ],
-        held=(2,),
+        held=(1,),
     )
     with jax.named_scope("row_stats"):
         stats = lax.all_to_all(stats, "xy", 0, 0)
@@ -386,9 +400,11 @@
     query_part, keep, send = call(
         grads_kernel,
         "gradients",
-        (place, stats, query_window, grads, key_cache, straight, crossed, in_vmem(probs_grad)) + own + other,
+        (place, route, stats, queries, grads, key_cache, straight, crossed, in_vmem(probs_grad))
+        + own
+        + other,
         [
-            ((groups, half // groups, local_heads * HD), BF),
+            ((groups, lines * rows, local_heads * HD), BF),
             ((2, chips, share, 2 * HD), F32),
             ((2, chips, share, 2 * HD), BF),
         ],
@@ -405,22 +421,23 @@
         chip_sum = keep + to_core(send).astype(F32)
         line_sum = chip_sum[0] + to_pair(chip_sum[1].astype(BF)).astype(F32)
         line_sum = line_sum.astype(BF)
+        row_shape = (rows, local_heads * HD)
+        kept, sent = call(
+            query_kernel, "query_sums", (place, query_terms), [(row_shape, F32), (row_shape, BF)]
+        )
+        line_sum, sent = lax.optimization_barrier((line_sum, sent))
+        came = to_pair(sent)
         own = lax.dynamic_index_in_dim(line_sum, chip, 0, False)
         arrived = [own] + [
             to_chip(lax.dynamic_index_in_dim(line_sum, (chip + step) % chips, 0, False), step)
             for step in range(1, chips)
         ]
-    query_terms, *arrived = lax.optimization_barrier((query_terms, *arrived))
     width = KVH * HD
     return call(
         finish_kernel,
         "finish",
-        (place, query_terms, *arrived),
-        [
-            (query_terms.shape[1:], BF),
-            ((share, width), BF),
-            ((share, width), BF),
-        ],
+        (place, kept, came, *arrived),
+        [(row_shape, BF), ((share, width), BF), ((share, width), BF)],
     )
 
 

time: 97.5 us -> 101 us (1.036); the launches traced: 95.8 us -> 101 us
  blocking collectives: 34.2 us -> 27.3 us
  starting transfers between devices: 26.7 us -> 32.5 us
  waiting for transfers between devices: 14.1 us -> 18.9 us
  Pallas kernels: 17.3 us -> 18.8 us
    all_to_all x1, waiting for transfers between devices: 0.48 us -> 9.94 us  [on_device(): query_terms = lax.all_to_all(query_part, 'xy', 0, 0)]
    ppermute x3, starting transfers between devices: 9.47 us -> 18.6 us  [to_pair(): return lax.ppermute(value, 'zh', [(0, 1), (1, 0)])]
    all_to_all x1, blocking collectives: 22.8 us -> 16.2 us  [on_device(): grads = lax.all_to_all(gathered, 'xy', 0, 0).reshape(half, local_heads * HD)]
    ppermute x6, waiting for transfers between devices: 7.46 us -> 5.24 us  [to_chip(): lax.ppermute(value, 'tp', [(i, (i + 2 * step) % parts) for i in range(par...]
    ppermute x6, starting transfers between devices: 7.22 us -> 5.08 us  [to_chip(): lax.ppermute(value, 'tp', [(i, (i + 2 * step) % parts) for i in range(par...]
    pallas_call x6 -> x7, Pallas kernels: 17.3 us -> 18.8 us  [call(): pl.pallas_call(kernel, in_specs=[SMEM] + [HBM if i in streamed else VMEM...]
    ppermute x3, starting transfers between devices: 6.45 us -> 5.17 us  [to_core(): return lax.ppermute(value, 'tp', [(i, i ^ 1) for i in range(parts)])]
    ppermute x3, waiting for transfers between devices: 4.97 us -> 3.73 us  [to_pair(): return lax.ppermute(value, 'zh', [(0, 1), (1, 0)])]
  transfers between devices with their start and end apart: 13 -> 13, of which waited for: 8 -> 6; matrix products, arithmetic and copies ran while one was open for 2% -> 0% of each run, Pallas kernels for 7% -> 6%
where the time goes in v5:
time: 101 us
  starting transfers between devices  32.5 us (32%)
  blocking collectives  27.3 us (27%)
  waiting for transfers between devices  18.9 us (19%)
  Pallas kernels  18.8 us (19%)
  between operations  1.48 us (1%)
  other arithmetic  1.12 us (1%)
    pallas_call x7, Pallas kernels, call(): pl.pallas_call(kernel, in_specs=[SMEM] + [HBM if i in streamed else VMEM...  18.8 us
    ppermute x3, starting transfers between devices, to_pair(): return lax.ppermute(value, 'zh', [(0, 1), (1, 0)])  18.6 us
    all_to_all x1, blocking collectives, on_device(): grads = lax.all_to_all(gathered, 'xy', 0, 0).reshape(half, local_heads * HD)  16.2 us
    all_to_all x1, blocking collectives, on_device(): stats = lax.all_to_all(stats, 'xy', 0, 0)  11 us
    all_to_all x1, waiting for transfers between devices, on_device(): query_terms = lax.all_to_all(query_part, 'xy', 0, 0)  9.94 us
    ppermute x6, waiting for transfers between devices, to_chip(): lax.ppermute(value, 'tp', [(i, (i + 2 * step) % parts) for i in range(par...  5.24 us
    ppermute x3, starting transfers between devices, to_core(): return lax.ppermute(value, 'tp', [(i, i ^ 1) for i in range(parts)])  5.17 us
    ppermute x6, starting transfers between devices, to_chip(): lax.ppermute(value, 'tp', [(i, (i + 2 * step) % parts) for i in range(par...  5.08 us
  transfers between devices with their start and end apart: 13, of which 6 were waited for; matrix products, arithmetic and copies ran while one was open for 0% of the time, Pallas kernels for 6%

profile of v5, /device:TPU:1, one launch (start us, length us, event | category | flops | bytes accessed | tf_op | source)
XLA Modules:
  0.0 101.0 jit_solution(10898113050144621943)
XLA Ops:
  0.7 1.0 %dynamic-slice_select_fusion = bf16[512,128]{1,0:T(8,128)(2,1)S(1)} fusion(bf16[512,512]{1,0:T(8,128)(2,1)} %value_ref.1, s32[]{:T(128)S(6)} %select_n.99, bf16[512,512]{1,0:T(8,128)(2,1)} %key_ref.1, pred[]{:T(512)S(6)} %eq.24), kind=kLoop, calls=%fused_computation.6 | loop fusion | flops 65536 | bytes 393221 | tf_op jit(solution)/shard_map/cache_pair/jit(_where)/select_n | solution.py:355
  1.7 7.8 %collective-permute-start.4 = (bf16[512,128]{1,0:T(8,128)(2,1)S(1)}, bf16[512,128]{1,0:T(8,128)(2,1)S(1)}, u32[]{:S(2)}, u32[]{:S(2)}) collective-permute-start(bf16[512,128]{1,0:T(8,128)(2,1)S(1)} %dynamic-slice_select_fusion), channel_id=1, source_target_pairs={{0,128},{128,0},{1,129},{129,1},{2,130},{130,2},{3,131},{131,3},{4... | collective-permute-start | bytes 393224 | tf_op jit(solution)/shard_map/cache_pair/ppermute | solution.py:317
  9.5 1.0 collective-permute-start
  11.9 4.3 %own_scores.1 = (f32[8,512,256]{2,1,0:T(8,128)S(1)}, f32[8,256]{1,0:T(8,128)S(1)}, f32[8,256]{1,0:T(8,128)S(1)}, bf16[1024,4096]{1,0:T(8,128)(2,1)S(1)}, bf16[256,1024]{1,0:T(8,128)(2,1)S(1)}) custom-call(s32[14]{0:T(128)S(1)} %stack.64.place, s32[1,512]{1,0:T(1,128)S(1)} %bitcast.35, bf16[512,1024]{1,0:T(8,128)(2,1)} %query_in.1, bf16[512,512]{1,0:T(8,128)(2,1)} %key_ref.1, ...), custom_call_target="tpu_custom_call" | custom-call | flops 268435456 | bytes 4194304 | tf_op jit(solution)/shard_map/own_scores/pallas_call | solution.py:41
  16.4 1.7 %collective-permute-start.3 = (bf16[2,16,512]{2,1,0:T(8,128)(2,1)S(1)}, bf16[2,16,512]{2,1,0:T(8,128)(2,1)S(1)}, u32[]{:S(2)}, u32[]{:S(2)}) collective-permute-start(bf16[2,16,512]{2,1,0:T(8,128)(2,1)S(1)} %pad_maximum_fusion.refs_0_), channel_id=1, source_target_pairs={{0,6},{1,7},{2,0},{3,1},{4,2},{5,3},{6,4},{7,5},{8,14},{9,15},{10,... | collective-permute-start | bytes 98312 | tf_op jit(solution)/shard_map/gradient_rows/ppermute | solution.py:323
  18.8 1.1 %collective-permute-start.1 = (bf16[2,16,512]{2,1,0:T(8,128)(2,1)S(1)}, bf16[2,16,512]{2,1,0:T(8,128)(2,1)S(1)}, u32[]{:S(2)}, u32[]{:S(2)}) collective-permute-start(bf16[2,16,512]{2,1,0:T(8,128)(2,1)S(1)} %pad_maximum_fusion.refs_0_), channel_id=1, source_target_pairs={{0,2},{1,3},{2,4},{3,5},{4,6},{5,7},{6,0},{7,1},{8,10},{9,11},{10,... | collective-permute-start | bytes 98312 | tf_op jit(solution)/shard_map/gradient_rows/ppermute | solution.py:323
  19.9 2.0 %other_scores.1 = (f32[8,512,256]{2,1,0:T(8,128)S(1)}, f32[8,256]{1,0:T(8,128)S(1)}, f32[8,256]{1,0:T(8,128)S(1)}) custom-call(s32[14]{0:T(128)S(1)} %stack.64.place, s32[1,512]{1,0:T(1,128)S(1)} %bitcast.36, bf16[256,1024]{1,0:T(8,128)(2,1)S(1)} %get-tuple-element.36.query_ref, bf16[512,128]{1,0:T(8,128)(2,1)S(1)} %collective-permute-done.4.straight, ...), custom_call_target="tpu_custom_call" | custom-call | flops 268435456 | bytes 4194304 | tf_op jit(solution)/shard_map/other_scores/pallas_call | solution.py:41
  22.0 1.4 %collective-permute-done.1.refs_1_ = bf16[2,16,512]{2,1,0:T(8,128)(2,1)S(1)} collective-permute-done((bf16[2,16,512]{2,1,0:T(8,128)(2,1)S(1)}, bf16[2,16,512]{2,1,0:T(8,128)(2,1)S(1)}, u32[]{:S(2)}, u32[]{:S(2)}) %collective-permute-start.1) | collective-permute-done | bytes 32800 | tf_op jit(solution)/shard_map/gradient_rows/ppermute | solution.py:323
  23.4 2.9 %project.1 = bf16[16,16,1024]{2,1,0:T(8,128)(2,1)S(1)} custom-call(s32[14]{0:T(128)S(1)} %stack.64.place, bf16[2,16,512]{2,1,0:T(8,128)(2,1)S(1)} %pad_maximum_fusion.refs_0_, bf16[2,16,512]{2,1,0:T(8,128)(2,1)S(1)} %collective-permute-done.1.refs_1_, bf16[2,16,512]{2,1,0:T(8,128)(2,1)S(1)} %collective-permute-done.2.refs_2_, ...), custom_call_target="tpu_custom_call" | custom-call | tf_op jit(solution)/shard_map/project/pallas_call | solution.py:41
  26.3 16.2 %all_to_all.15 = bf16[16,16,1024]{2,1,0:T(8,128)(2,1)S(1)} all-to-all(bf16[16,16,1024]{2,1,0:T(8,128)(2,1)S(1)} %project.1), channel_id=1, replica_groups=mesh['zh'=2,'xy'=16,'tp'=8] {'xy'}, dimensions={0} | all-to-all | bytes 1048576 | tf_op jit(solution)/shard_map/head_gradients/all_to_all | solution.py:380
  42.5 1.9 %deltas.1 = (f32[16,3,8,256]{3,2,1,0:T(8,128)S(1)}, f32[8,2,512,256]{3,2,1,0:T(8,128)S(1)}) custom-call(s32[14]{0:T(128)S(1)} %stack.64.place, bf16[256,1024]{1,0:T(8,128)(2,1)S(1)} %bitcast.33, bf16[512,512]{1,0:T(8,128)(2,1)S(1)} %copy-done.1, bf16[512,128]{1,0:T(8,128)(2,1)S(1)} %collective-permute-done.4.straight, ...), custom_call_target="tpu_custom_call" | custom-call | tf_op jit(solution)/shard_map/deltas/pallas_call | solution.py:41
  44.5 11.0 %all_to_all.16.stats_ref = f32[16,3,8,256]{3,2,1,0:T(8,128)S(1)} all-to-all(f32[16,3,8,256]{3,2,1,0:T(8,128)S(1)} %get-tuple-element.52), channel_id=1, replica_groups=mesh['zh'=2,'xy'=16,'tp'=8] {'xy'}, dimensions={0} | all-to-all | bytes 786432 | tf_op jit(solution)/shard_map/row_stats/all_to_all | solution.py:398
  55.5 5.7 %gradients.1 = (bf16[16,32,1024]{2,1,0:T(8,128)(2,1)}, f32[2,4,64,256]{3,2,1,0:T(8,128)S(1)}, bf16[2,4,64,256]{3,2,1,0:T(8,128)(2,1)S(1)}) custom-call(s32[14]{0:T(128)S(1)} %stack.64.place, s32[1,512]{1,0:T(1,128)S(1)} %bitcast.37, f32[16,3,8,256]{3,2,1,0:T(8,128)S(1)} %all_to_all.16.stats_ref, bf16[256,1024]{1,0:T(8,128)(2,1)S(1)} %get-tuple-element.36.query_ref, ...), custom_call_target="tpu_custom_call" | custom-call | tf_op jit(solution)/shard_map/gradients/pallas_call | solution.py:41
  61.2 4.1 %collective-permute-start.6 = (bf16[2,4,64,256]{3,2,1,0:T(8,128)(2,1)S(1)}, bf16[2,4,64,256]{3,2,1,0:T(8,128)(2,1)S(1)}, u32[]{:S(2)}, u32[]{:S(2)}) collective-permute-start(bf16[2,4,64,256]{3,2,1,0:T(8,128)(2,1)S(1)} %get-tuple-element.57), channel_id=1, source_target_pairs={{0,1},{1,0},{2,3},{3,2},{4,5},{5,4},{6,7},{7,6},{8,9},{9,8},{10,11... | collective-permute-start | bytes 786440 | tf_op jit(solution)/shard_map/cache_terms/ppermute | solution.py:320
  65.4 3.7 %all-to-all-start.2 = ((bf16[16,32,1024]{2,1,0:T(8,128)(2,1)}), bf16[16,32,1024]{2,1,0:T(8,128)(2,1)S(1)}, u32[]{:S(2)}, u32[]{:S(2)}) async-start(bf16[16,32,1024]{2,1,0:T(8,128)(2,1)} %get-tuple-element.54), calls=%async_computation.2 | async-start | bytes 2097152 | tf_op jit(solution)/shard_map/all_to_all | solution.py:419
  69.1 5.4 %collective-permute-start.7 = (bf16[4,64,256]{2,1,0:T(8,128)(2,1)S(1)}, bf16[4,64,256]{2,1,0:T(8,128)(2,1)S(1)}, u32[]{:S(2)}, u32[]{:S(2)}) collective-permute-start(bf16[4,64,256]{2,1,0:T(8,128)(2,1)S(1)} %fusion.2), channel_id=1, source_target_pairs={{0,128},{128,0},{1,129},{129,1},{2,130},{130,2},{3,131},{131,3},{4... | collective-permute-start | bytes 393224 | tf_op jit(solution)/shard_map/cache_terms/ppermute | solution.py:317
  74.5 3.7 %collective-permute-done.7 = bf16[4,64,256]{2,1,0:T(8,128)(2,1)S(1)} collective-permute-done((bf16[4,64,256]{2,1,0:T(8,128)(2,1)S(1)}, bf16[4,64,256]{2,1,0:T(8,128)(2,1)S(1)}, u32[]{:S(2)}, u32[]{:S(2)}) %collective-permute-start.7) | collective-permute-done | bytes 131104 | tf_op jit(solution)/shard_map/cache_terms/ppermute | solution.py:317
  78.3 9.9 %all-to-all-done.2.terms_ref = bf16[16,32,1024]{2,1,0:T(8,128)(2,1)S(1)} async-done(((bf16[16,32,1024]{2,1,0:T(8,128)(2,1)}), bf16[16,32,1024]{2,1,0:T(8,128)(2,1)S(1)}, u32[]{:S(2)}, u32[]{:S(2)}) %all-to-all-start.2) | async-done | bytes 1048608 | tf_op jit(solution)/shard_map/all_to_all | solution.py:419
  88.9 5.4 %collective-permute-start.8 = (bf16[16,1024]{1,0:T(8,128)(2,1)S(1)}, bf16[16,1024]{1,0:T(8,128)(2,1)S(1)}, u32[]{:S(2)}, u32[]{:S(2)}) collective-permute-start(bf16[16,1024]{1,0:T(8,128)(2,1)S(1)} %get-tuple-element.59), channel_id=1, source_target_pairs={{0,128},{128,0},{1,129},{129,1},{2,130},{130,2},{3,131},{131,3},{4... | collective-permute-start | bytes 98312 | tf_op jit(solution)/shard_map/cache_terms/ppermute | solution.py:317
  94.3 0.8 collective-permute-start.11
  95.9 1.5 %collective-permute-done.11.refs_3_ = bf16[64,256]{1,0:T(8,128)(2,1)S(1)} collective-permute-done((bf16[64,256]{1,0:T(8,128)(2,1)S(1)}, bf16[64,256]{1,0:T(8,128)(2,1)S(1)}, u32[]{:S(2)}, u32[]{:S(2)}) %collective-permute-start.11) | collective-permute-done | bytes 32800 | tf_op jit(solution)/shard_map/cache_terms/ppermute | solution.py:323
  97.4 1.6 %collective-permute-done.10.refs_2_ = bf16[64,256]{1,0:T(8,128)(2,1)S(1)} collective-permute-done((bf16[64,256]{1,0:T(8,128)(2,1)S(1)}, bf16[64,256]{1,0:T(8,128)(2,1)S(1)}, u32[]{:S(2)}, u32[]{:S(2)}) %collective-permute-start.10) | collective-permute-done | bytes 32800 | tf_op jit(solution)/shard_map/cache_terms/ppermute | solution.py:323
  98.9 0.8 collective-permute-done.9.refs_1_
  99.7 1.2 %finish.1 = (bf16[16,1024]{1,0:T(8,128)(2,1)}, bf16[64,512]{1,0:T(8,128)(2,1)}, bf16[64,512]{1,0:T(8,128)(2,1)}) custom-call(s32[14]{0:T(128)S(1)} %stack.64.place, f32[16,1024]{1,0:T(8,128)S(1)} %get-tuple-element.55.kept_ref, bf16[16,1024]{1,0:T(8,128)(2,1)S(1)} %collective-permute-done.8.came_ref, bf16[64,256]{1,0:T(8,128)(2,1)S(1)} %get-tuple-element.64.refs_0_, ...), custom_call_target="tpu_custom_call" | custom-call | tf_op jit(solution)/shard_map/finish/pallas_call | solution.py:41
  (26 shorter events, 3.2 us)
Async XLA Ops:
  0.6 15.7 %copy-start.3 = (bf16[16,512]{1,0:T(8,128)(2,1)S(1)}, bf16[16,512]{1,0:T(8,128)(2,1)}, u32[]{:S(2)}) copy-start(bf16[16,512]{1,0:T(8,128)(2,1)} %param.11) | copy-start | bytes 49156
  1.7 14.6 %collective-permute-start.4 = (bf16[512,128]{1,0:T(8,128)(2,1)S(1)}, bf16[512,128]{1,0:T(8,128)(2,1)S(1)}, u32[]{:S(2)}, u32[]{:S(2)}) collective-permute-start(bf16[512,128]{1,0:T(8,128)(2,1)S(1)} %dynamic-slice_select_fusion), channel_id=1, source_target_pairs={{0,128},{128,0},{1,129},{129,1},{2,130},{130,2},{3,131},{131,3},{4... | collective-permute-start | bytes 393224 | tf_op jit(solution)/shard_map/cache_pair/ppermute | solution.py:317
  9.5 6.8 %collective-permute-start = (bf16[16,512]{1,0:T(8,128)(2,1)}, bf16[16,512]{1,0:T(8,128)(2,1)S(1)}, u32[]{:S(2)}, u32[]{:S(2)}) collective-permute-start(bf16[16,512]{1,0:T(8,128)(2,1)} %param.11), channel_id=1, source_target_pairs={{0,1},{1,0},{2,3},{3,2},{4,5},{5,4},{6,7},{7,6},{8,9},{9,8},{10,11... | collective-permute-start | bytes 49160 | tf_op jit(solution)/shard_map/gradient_rows/ppermute | solution.py:320
  11.2 0.7 copy-start.2
  16.2 26.3 %copy-start.1 = (bf16[512,512]{1,0:T(8,128)(2,1)S(1)}, bf16[512,512]{1,0:T(8,128)(2,1)}, u32[]{:S(2)}) copy-start(bf16[512,512]{1,0:T(8,128)(2,1)} %value_ref.1) | copy-start | bytes 1572868
  16.3 3.7 %collective-permute-start.5 = (bf16[512,128]{1,0:T(8,128)(2,1)S(1)}, bf16[512,128]{1,0:T(8,128)(2,1)S(1)}, u32[]{:S(2)}, u32[]{:S(2)}) collective-permute-start(bf16[512,128]{1,0:T(8,128)(2,1)S(1)} %collective-permute-done.4.straight), channel_id=1, source_target_pairs={{0,1},{1,0},{2,3},{3,2},{4,5},{5,4},{6,7},{7,6},{8,9},{9,8},{10,11... | collective-permute-start | bytes 393224 | tf_op jit(solution)/shard_map/cache_pair/ppermute | solution.py:320
  16.4 5.6 %collective-permute-start.3 = (bf16[2,16,512]{2,1,0:T(8,128)(2,1)S(1)}, bf16[2,16,512]{2,1,0:T(8,128)(2,1)S(1)}, u32[]{:S(2)}, u32[]{:S(2)}) collective-permute-start(bf16[2,16,512]{2,1,0:T(8,128)(2,1)S(1)} %pad_maximum_fusion.refs_0_), channel_id=1, source_target_pairs={{0,6},{1,7},{2,0},{3,1},{4,2},{5,3},{6,4},{7,5},{8,14},{9,15},{10,... | collective-permute-start | bytes 98312 | tf_op jit(solution)/shard_map/gradient_rows/ppermute | solution.py:323
  18.1 3.9 %collective-permute-start.2 = (bf16[2,16,512]{2,1,0:T(8,128)(2,1)S(1)}, bf16[2,16,512]{2,1,0:T(8,128)(2,1)S(1)}, u32[]{:S(2)}, u32[]{:S(2)}) collective-permute-start(bf16[2,16,512]{2,1,0:T(8,128)(2,1)S(1)} %pad_maximum_fusion.refs_0_), channel_id=1, source_target_pairs={{0,4},{1,5},{2,6},{3,7},{4,0},{5,1},{6,2},{7,3},{8,12},{9,13},{10,... | collective-permute-start | bytes 98312 | tf_op jit(solution)/shard_map/gradient_rows/ppermute | solution.py:323
  18.8 4.6 %collective-permute-start.1 = (bf16[2,16,512]{2,1,0:T(8,128)(2,1)S(1)}, bf16[2,16,512]{2,1,0:T(8,128)(2,1)S(1)}, u32[]{:S(2)}, u32[]{:S(2)}) collective-permute-start(bf16[2,16,512]{2,1,0:T(8,128)(2,1)S(1)} %pad_maximum_fusion.refs_0_), channel_id=1, source_target_pairs={{0,2},{1,3},{2,4},{3,5},{4,6},{5,7},{6,0},{7,1},{8,10},{9,11},{10,... | collective-permute-start | bytes 98312 | tf_op jit(solution)/shard_map/gradient_rows/ppermute | solution.py:323
  23.4 32.1 %copy-start = (bf16[512,512]{1,0:T(8,128)(2,1)S(1)}, bf16[512,512]{1,0:T(8,128)(2,1)}, u32[]{:S(2)}) copy-start(bf16[512,512]{1,0:T(8,128)(2,1)} %key_ref.1) | copy-start | bytes 1572868
  61.2 7.8 %collective-permute-start.6 = (bf16[2,4,64,256]{3,2,1,0:T(8,128)(2,1)S(1)}, bf16[2,4,64,256]{3,2,1,0:T(8,128)(2,1)S(1)}, u32[]{:S(2)}, u32[]{:S(2)}) collective-permute-start(bf16[2,4,64,256]{3,2,1,0:T(8,128)(2,1)S(1)} %get-tuple-element.57), channel_id=1, source_target_pairs={{0,1},{1,0},{2,3},{3,2},{4,5},{5,4},{6,7},{7,6},{8,9},{9,8},{10,11... | collective-permute-start | bytes 786440 | tf_op jit(solution)/shard_map/cache_terms/ppermute | solution.py:320
  65.4 22.9 %all-to-all-start.2 = ((bf16[16,32,1024]{2,1,0:T(8,128)(2,1)}), bf16[16,32,1024]{2,1,0:T(8,128)(2,1)S(1)}, u32[]{:S(2)}, u32[]{:S(2)}) async-start(bf16[16,32,1024]{2,1,0:T(8,128)(2,1)} %get-tuple-element.54), calls=%async_computation.2 | async-start | bytes 2097152 | tf_op jit(solution)/shard_map/all_to_all | solution.py:419
  69.1 9.1 %collective-permute-start.7 = (bf16[4,64,256]{2,1,0:T(8,128)(2,1)S(1)}, bf16[4,64,256]{2,1,0:T(8,128)(2,1)S(1)}, u32[]{:S(2)}, u32[]{:S(2)}) collective-permute-start(bf16[4,64,256]{2,1,0:T(8,128)(2,1)S(1)} %fusion.2), channel_id=1, source_target_pairs={{0,128},{128,0},{1,129},{129,1},{2,130},{130,2},{3,131},{131,3},{4... | collective-permute-start | bytes 393224 | tf_op jit(solution)/shard_map/cache_terms/ppermute | solution.py:317
  88.9 7.0 %collective-permute-start.8 = (bf16[16,1024]{1,0:T(8,128)(2,1)S(1)}, bf16[16,1024]{1,0:T(8,128)(2,1)S(1)}, u32[]{:S(2)}, u32[]{:S(2)}) collective-permute-start(bf16[16,1024]{1,0:T(8,128)(2,1)S(1)} %get-tuple-element.59), channel_id=1, source_target_pairs={{0,128},{128,0},{1,129},{129,1},{2,130},{130,2},{3,131},{131,3},{4... | collective-permute-start | bytes 98312 | tf_op jit(solution)/shard_map/cache_terms/ppermute | solution.py:317
  94.3 3.0 %collective-permute-start.11 = (bf16[64,256]{1,0:T(8,128)(2,1)S(1)}, bf16[64,256]{1,0:T(8,128)(2,1)S(1)}, u32[]{:S(2)}, u32[]{:S(2)}) collective-permute-start(bf16[64,256]{1,0:T(8,128)(2,1)S(1)} %get-tuple-element.61), channel_id=1, source_target_pairs={{0,6},{1,7},{2,0},{3,1},{4,2},{5,3},{6,4},{7,5},{8,14},{9,15},{10,... | collective-permute-start | bytes 98312 | tf_op jit(solution)/shard_map/cache_terms/ppermute | solution.py:323
  95.2 3.8 %collective-permute-start.10 = (bf16[64,256]{1,0:T(8,128)(2,1)S(1)}, bf16[64,256]{1,0:T(8,128)(2,1)S(1)}, u32[]{:S(2)}, u32[]{:S(2)}) collective-permute-start(bf16[64,256]{1,0:T(8,128)(2,1)S(1)} %get-tuple-element.62), channel_id=1, source_target_pairs={{0,4},{1,5},{2,6},{3,7},{4,0},{5,1},{6,2},{7,3},{8,12},{9,13},{10,... | collective-permute-start | bytes 98312 | tf_op jit(solution)/shard_map/cache_terms/ppermute | solution.py:323
  95.2 4.6 %collective-permute-start.9 = (bf16[64,256]{1,0:T(8,128)(2,1)S(1)}, bf16[64,256]{1,0:T(8,128)(2,1)S(1)}, u32[]{:S(2)}, u32[]{:S(2)}) collective-permute-start(bf16[64,256]{1,0:T(8,128)(2,1)S(1)} %get-tuple-element.63), channel_id=1, source_target_pairs={{0,2},{1,3},{2,4},{3,5},{4,6},{5,7},{6,0},{7,1},{8,10},{9,11},{10,... | collective-permute-start | bytes 98312 | tf_op jit(solution)/shard_map/cache_terms/ppermute | solution.py:323

commit v6 on v4

--- a/solution.py
+++ b/solution.py
@@ -159,11 +159,17 @@
     probs_grad_ref,
 ):
     heads, span, half = expo_own.shape
-    window = route_ref.shape[1]
-    token = place[LINE] * half + lax.broadcasted_iota(jnp.int32, (half, window), 0)
-    pick = jnp.where(route_ref[...] == token, 1.0, 0.0).astype(BF)
+    groups, rows, width = gathered_ref.shape
+    rows //= 2
     values = (value_ref[:, columns(place[KV_HEAD])], other_pair(place, straight, crossed)[1])
-    grad_ref[...] = dot(pick, gathered_ref[...].reshape(window, heads * HD)).astype(BF)
+    token = place[LINE] * half + lax.broadcasted_iota(jnp.int32, (half, groups * rows), 0)
+    grad = None
+    for part, line in enumerate((place[LINE], 1 - place[LINE])):
+        pick = route_ref[:, columns(line, groups * rows)] == token
+        routed = gathered_ref[:, part * rows : (part + 1) * rows].reshape(groups * rows, width)
+        term = dot(jnp.where(pick, 1.0, 0.0).astype(BF), routed)
+        grad = term if grad is None else grad + term
+    grad_ref[...] = grad.astype(BF)
     peak = jnp.maximum(peak_own[...], peak_other[...])
     factors = (jnp.exp2(peak_own[...] - peak), jnp.exp2(peak_other[...] - peak))
     stats_ref[0, 0] = peak
@@ -295,8 +301,8 @@
         + pieces
     ).astype(jnp.int32)
 
-    route = token_route.reshape(lines, groups, rows)
-    route = jnp.where(line == 0, route, route[::-1]).transpose(1, 0, 2).reshape(1, window)
+    route = token_route.reshape(1, window)
+
     def to_pair(value):
         return lax.ppermute(value, "zh", [(0, 1), (1, 0)])
 
@@ -330,12 +336,6 @@
         streamed=(1, 2, 3),
         held=(0, 3),
     )
-    with jax.named_scope("gradient_rows"):
-        other_rows = to_pair(grad_routed)
-        other_rows, weight, route = lax.optimization_barrier((other_rows, weight, route))
-        pair = jnp.stack([grad_routed, other_rows])
-        chip_rows = jnp.stack([pair, to_core(pair)])
-        all_rows = [chip_rows] + [to_chip(chip_rows, step) for step in range(1, chips)]
     with jax.named_scope("cache_pair"):
         mine = jnp.where(
             core == 0,
@@ -343,7 +343,13 @@
             lax.dynamic_slice_in_dim(value_cache, kv_head * HD, HD, 1),
         )
         straight = to_pair(mine)
+    with jax.named_scope("gradient_rows"):
+        other_rows = to_pair(grad_routed)
+        other_rows, straight, weight = lax.optimization_barrier((other_rows, straight, weight))
         crossed = to_core(straight)
+        pair = jnp.stack([grad_routed, other_rows])
+        chip_rows = jnp.stack([pair, to_core(pair)])
+        all_rows = [chip_rows] + [to_chip(chip_rows, step) for step in range(1, chips)]
     expo_other, peak_other, total_other = call(
         other_kernel,
         "other_scores",

time: 97.5 us -> 96.5 us (0.990); the launches traced: 95.8 us -> 96.2 us
  starting transfers between devices: 26.7 us -> 28.4 us
    ppermute x3, starting transfers between devices: 9.47 us -> 11.2 us  [to_pair(): return lax.ppermute(value, 'zh', [(0, 1), (1, 0)])]
    ppermute x3, waiting for transfers between devices: 4.97 us -> 3.5 us  [to_pair(): return lax.ppermute(value, 'zh', [(0, 1), (1, 0)])]
    ppermute x6, starting transfers between devices: 7.22 us -> 8.62 us  [to_chip(): lax.ppermute(value, 'tp', [(i, (i + 2 * step) % parts) for i in range(par...]
    ppermute x3, starting transfers between devices: 6.45 us -> 5.06 us  [to_core(): return lax.ppermute(value, 'tp', [(i, i ^ 1) for i in range(parts)])]
  transfers between devices with their start and end apart: 13 -> 13, of which waited for: 8 -> 7; matrix products, arithmetic and copies ran while one was open for 2% -> 0% of each run, Pallas kernels for 7% -> 6%
where the time goes in v6:
time: 96.5 us; the launch traced here: 96.2 us
  blocking collectives  34.4 us (36%)
  starting transfers between devices  28.4 us (29%)
  Pallas kernels  17.3 us (18%)
  waiting for transfers between devices  13.3 us (14%)
  between operations  1.47 us (2%)
  other arithmetic  1.19 us (1%)
    all_to_all x1, blocking collectives, on_device(): gathered = lax.all_to_all(gathered, 'xy', 0, 0)  22.8 us
    pallas_call x6, Pallas kernels, call(): pl.pallas_call(kernel, in_specs=[SMEM] + [HBM if i in streamed else VMEM...  17.3 us
    all_to_all x1, blocking collectives, on_device(): stats = lax.all_to_all(stats, 'xy', 0, 0)  11.6 us
    ppermute x3, starting transfers between devices, to_pair(): return lax.ppermute(value, 'zh', [(0, 1), (1, 0)])  11.2 us
    ppermute x6, starting transfers between devices, to_chip(): lax.ppermute(value, 'tp', [(i, (i + 2 * step) % parts) for i in range(par...  8.62 us
    ppermute x6, waiting for transfers between devices, to_chip(): lax.ppermute(value, 'tp', [(i, (i + 2 * step) % parts) for i in range(par...  7.83 us
    ppermute x3, starting transfers between devices, to_core(): return lax.ppermute(value, 'tp', [(i, i ^ 1) for i in range(parts)])  5.06 us
    all_to_all x1, starting transfers between devices, on_device(): query_terms = lax.all_to_all(query_part, 'xy', 0, 0)  3.57 us
  transfers between devices with their start and end apart: 13, of which 7 were waited for; matrix products, arithmetic and copies ran while one was open for 0% of the time, Pallas kernels for 6%

profile of v6, /device:TPU:1, one launch (start us, length us, event | category | flops | bytes accessed | tf_op | source)
XLA Modules:
  0.0 96.2 jit_solution(11043248702389258603)
XLA Ops:
  0.7 1.1 %dynamic-slice_select_fusion = bf16[512,128]{1,0:T(8,128)(2,1)S(1)} fusion(bf16[512,512]{1,0:T(8,128)(2,1)} %value_ref.1, s32[]{:T(128)S(6)} %select_n.99, bf16[512,512]{1,0:T(8,128)(2,1)} %key_ref.1, pred[]{:T(512)S(6)} %eq.24), kind=kLoop, calls=%fused_computation.6 | loop fusion | flops 65536 | bytes 393221 | tf_op jit(solution)/shard_map/cache_pair/jit(_where)/select_n | solution.py:340
  1.8 7.8 %collective-permute-start.1 = (bf16[512,128]{1,0:T(8,128)(2,1)S(1)}, bf16[512,128]{1,0:T(8,128)(2,1)S(1)}, u32[]{:S(2)}, u32[]{:S(2)}) collective-permute-start(bf16[512,128]{1,0:T(8,128)(2,1)S(1)} %dynamic-slice_select_fusion), channel_id=1, source_target_pairs={{0,128},{128,0},{1,129},{129,1},{2,130},{130,2},{3,131},{131,3},{4... | collective-permute-start | bytes 393224 | tf_op jit(solution)/shard_map/cache_pair/ppermute | solution.py:307
  10.5 4.2 %own_scores.1 = (f32[8,512,256]{2,1,0:T(8,128)S(1)}, f32[8,256]{1,0:T(8,128)S(1)}, f32[8,256]{1,0:T(8,128)S(1)}, bf16[1024,4096]{1,0:T(8,128)(2,1)S(1)}) custom-call(s32[14]{0:T(128)S(1)} %stack.73.place, bf16[512,1024]{1,0:T(8,128)(2,1)} %query_ref.3, bf16[512,512]{1,0:T(8,128)(2,1)} %key_ref.1, bf16[1024,4096]{1,0:T(8,128)(2,1)} %weight_in.1), custom_call_target="tpu_custom_call" | custom-call | flops 268435456 | bytes 4194304 | tf_op jit(solution)/shard_map/own_scores/pallas_call | solution.py:41
  14.7 1.6 %collective-permute-done = bf16[16,512]{1,0:T(8,128)(2,1)S(1)} collective-permute-done((bf16[16,512]{1,0:T(8,128)(2,1)}, bf16[16,512]{1,0:T(8,128)(2,1)S(1)}, u32[]{:S(2)}, u32[]{:S(2)}) %collective-permute-start) | collective-permute-done | bytes 16416 | tf_op jit(solution)/shard_map/gradient_rows/ppermute | solution.py:307
  16.3 2.2 %collective-permute-start.2 = (bf16[2,16,512]{2,1,0:T(8,128)(2,1)S(1)}, bf16[2,16,512]{2,1,0:T(8,128)(2,1)S(1)}, u32[]{:S(2)}, u32[]{:S(2)}) collective-permute-start(bf16[2,16,512]{2,1,0:T(8,128)(2,1)S(1)} %get-tuple-element.68), channel_id=1, source_target_pairs={{0,1},{1,0},{2,3},{3,2},{4,5},{5,4},{6,7},{7,6},{8,9},{9,8},{10,11... | collective-permute-start | bytes 98312 | tf_op jit(solution)/shard_map/gradient_rows/ppermute | solution.py:310
  18.6 0.8 collective-permute-done.2
  19.4 1.7 %collective-permute-start.5 = (bf16[2,2,16,512]{3,2,1,0:T(8,128)(2,1)S(1)}, bf16[2,2,16,512]{3,2,1,0:T(8,128)(2,1)S(1)}, u32[]{:S(2)}, u32[]{:S(2)}) collective-permute-start(bf16[2,2,16,512]{3,2,1,0:T(8,128)(2,1)S(1)} %pad_maximum_fusion.refs_0_), channel_id=1, source_target_pairs={{0,6},{1,7},{2,0},{3,1},{4,2},{5,3},{6,4},{7,5},{8,14},{9,15},{10,... | collective-permute-start | bytes 196616 | tf_op jit(solution)/shard_map/gradient_rows/ppermute | solution.py:313
  22.1 2.0 %other_scores.1 = (f32[8,512,256]{2,1,0:T(8,128)S(1)}, f32[8,256]{1,0:T(8,128)S(1)}, f32[8,256]{1,0:T(8,128)S(1)}) custom-call(s32[14]{0:T(128)S(1)} %stack.73.place, bf16[512,1024]{1,0:T(8,128)(2,1)S(1)} %copy-done, bf16[512,128]{1,0:T(8,128)(2,1)S(1)} %collective-permute-done.1.straight, bf16[512,128]{1,0:T(8,128)(2,1)S(1)} %collective-permute-done.6.crossed), custom_call_target="tpu_custom_call" | custom-call | flops 268435456 | bytes 4194304 | tf_op jit(solution)/shard_map/other_scores/pallas_call | solution.py:41
  24.1 4.3 %collective-permute-done.4.refs_2_ = bf16[2,2,16,512]{3,2,1,0:T(8,128)(2,1)S(1)} collective-permute-done((bf16[2,2,16,512]{3,2,1,0:T(8,128)(2,1)S(1)}, bf16[2,2,16,512]{3,2,1,0:T(8,128)(2,1)S(1)}, u32[]{:S(2)}, u32[]{:S(2)}) %collective-permute-start.4) | collective-permute-done | bytes 65568 | tf_op jit(solution)/shard_map/gradient_rows/ppermute | solution.py:313
  28.4 2.9 %project.1 = bf16[16,32,1024]{2,1,0:T(8,128)(2,1)S(1)} custom-call(s32[14]{0:T(128)S(1)} %stack.73.place, bf16[2,2,16,512]{3,2,1,0:T(8,128)(2,1)S(1)} %pad_maximum_fusion.refs_0_, bf16[2,2,16,512]{3,2,1,0:T(8,128)(2,1)S(1)} %collective-permute-done.3.refs_1_, bf16[2,2,16,512]{3,2,1,0:T(8,128)(2,1)S(1)} %collective-permute-done.4.refs_2_, ...), custom_call_target="tpu_custom_call" | custom-call | tf_op jit(solution)/shard_map/project/pallas_call | solution.py:41
  31.4 22.8 %all_to_all.15.gathered_ref = bf16[16,32,1024]{2,1,0:T(8,128)(2,1)S(1)} all-to-all(bf16[16,32,1024]{2,1,0:T(8,128)(2,1)S(1)} %project.1), channel_id=1, replica_groups=mesh['zh'=2,'xy'=16,'tp'=8] {'xy'}, dimensions={0} | all-to-all | bytes 2097152 | tf_op jit(solution)/shard_map/head_gradients/all_to_all | solution.py:371
  54.1 2.2 %deltas.1 = (bf16[256,1024]{1,0:T(8,128)(2,1)S(1)}, f32[16,3,8,256]{3,2,1,0:T(8,128)S(1)}, f32[8,2,512,256]{3,2,1,0:T(8,128)S(1)}) custom-call(s32[14]{0:T(128)S(1)} %stack.73.place, s32[1,512]{1,0:T(1,128)S(1)} %bitcast.35, bf16[16,32,1024]{2,1,0:T(8,128)(2,1)S(1)} %all_to_all.15.gathered_ref, bf16[512,512]{1,0:T(8,128)(2,1)S(1)} %copy-done.2, ...), custom_call_target="tpu_custom_call" | custom-call | tf_op jit(solution)/shard_map/deltas/pallas_call | solution.py:41
  56.3 11.6 %all_to_all.16.stats_ref = f32[16,3,8,256]{3,2,1,0:T(8,128)S(1)} all-to-all(f32[16,3,8,256]{3,2,1,0:T(8,128)S(1)} %get-tuple-element.52), channel_id=1, replica_groups=mesh['zh'=2,'xy'=16,'tp'=8] {'xy'}, dimensions={0} | all-to-all | bytes 786432 | tf_op jit(solution)/shard_map/row_stats/all_to_all | solution.py:390
  68.0 4.8 %gradients.1 = (bf16[16,16,1024]{2,1,0:T(8,128)(2,1)}, f32[2,4,64,256]{3,2,1,0:T(8,128)S(1)}, bf16[2,4,64,256]{3,2,1,0:T(8,128)(2,1)S(1)}) custom-call(s32[14]{0:T(128)S(1)} %stack.73.place, f32[16,3,8,256]{3,2,1,0:T(8,128)S(1)} %all_to_all.16.stats_ref, bf16[512,1024]{1,0:T(8,128)(2,1)S(1)} %copy-done, bf16[256,1024]{1,0:T(8,128)(2,1)S(1)} %get-tuple-element.53.grad_ref, ...), custom_call_target="tpu_custom_call" | custom-call | tf_op jit(solution)/shard_map/gradients/pallas_call | solution.py:41
  72.7 2.8 %collective-permute-start.7 = (bf16[2,4,64,256]{3,2,1,0:T(8,128)(2,1)S(1)}, bf16[2,4,64,256]{3,2,1,0:T(8,128)(2,1)S(1)}, u32[]{:S(2)}, u32[]{:S(2)}) collective-permute-start(bf16[2,4,64,256]{3,2,1,0:T(8,128)(2,1)S(1)} %get-tuple-element.57), channel_id=1, source_target_pairs={{0,1},{1,0},{2,3},{3,2},{4,5},{5,4},{6,7},{7,6},{8,9},{9,8},{10,11... | collective-permute-start | bytes 786440 | tf_op jit(solution)/shard_map/cache_terms/ppermute | solution.py:310
  75.5 1.2 %collective-permute-done.7 = bf16[2,4,64,256]{3,2,1,0:T(8,128)(2,1)S(1)} collective-permute-done((bf16[2,4,64,256]{3,2,1,0:T(8,128)(2,1)S(1)}, bf16[2,4,64,256]{3,2,1,0:T(8,128)(2,1)S(1)}, u32[]{:S(2)}, u32[]{:S(2)}) %collective-permute-start.7) | collective-permute-done | bytes 262176 | tf_op jit(solution)/shard_map/cache_terms/ppermute | solution.py:310
  76.7 3.2 %collective-permute-start.8 = (bf16[4,64,256]{2,1,0:T(8,128)(2,1)S(1)}, bf16[4,64,256]{2,1,0:T(8,128)(2,1)S(1)}, u32[]{:S(2)}, u32[]{:S(2)}) collective-permute-start(bf16[4,64,256]{2,1,0:T(8,128)(2,1)S(1)} %fusion.2), channel_id=1, source_target_pairs={{0,128},{128,0},{1,129},{129,1},{2,130},{130,2},{3,131},{131,3},{4... | collective-permute-start | bytes 393224 | tf_op jit(solution)/shard_map/cache_terms/ppermute | solution.py:307
  80.0 3.6 %all-to-all-start.2 = ((bf16[16,16,1024]{2,1,0:T(8,128)(2,1)}), bf16[16,16,1024]{2,1,0:T(8,128)(2,1)S(1)}, u32[]{:S(2)}, u32[]{:S(2)}) async-start(bf16[16,16,1024]{2,1,0:T(8,128)(2,1)} %get-tuple-element.55), calls=%async_computation.2 | async-start | bytes 1048576 | tf_op jit(solution)/shard_map/all_to_all | solution.py:409
  83.6 1.9 %collective-permute-done.8 = bf16[4,64,256]{2,1,0:T(8,128)(2,1)S(1)} collective-permute-done((bf16[4,64,256]{2,1,0:T(8,128)(2,1)S(1)}, bf16[4,64,256]{2,1,0:T(8,128)(2,1)S(1)}, u32[]{:S(2)}, u32[]{:S(2)}) %collective-permute-start.8) | collective-permute-done | bytes 131104 | tf_op jit(solution)/shard_map/cache_terms/ppermute | solution.py:307
  85.5 2.6 %collective-permute-start.11 = (bf16[64,256]{1,0:T(8,128)(2,1)S(1)}, bf16[64,256]{1,0:T(8,128)(2,1)S(1)}, u32[]{:S(2)}, u32[]{:S(2)}) collective-permute-start(bf16[64,256]{1,0:T(8,128)(2,1)S(1)} %get-tuple-element.63), channel_id=1, source_target_pairs={{0,6},{1,7},{2,0},{3,1},{4,2},{5,3},{6,4},{7,5},{8,14},{9,15},{10,... | collective-permute-start | bytes 98312 | tf_op jit(solution)/shard_map/cache_terms/ppermute | solution.py:313
  88.1 2.0 %collective-permute-start.10 = (bf16[64,256]{1,0:T(8,128)(2,1)S(1)}, bf16[64,256]{1,0:T(8,128)(2,1)S(1)}, u32[]{:S(2)}, u32[]{:S(2)}) collective-permute-start(bf16[64,256]{1,0:T(8,128)(2,1)S(1)} %get-tuple-element.64), channel_id=1, source_target_pairs={{0,4},{1,5},{2,6},{3,7},{4,0},{5,1},{6,2},{7,3},{8,12},{9,13},{10,... | collective-permute-start | bytes 98312 | tf_op jit(solution)/shard_map/cache_terms/ppermute | solution.py:313
  90.1 1.4 %collective-permute-start.9 = (bf16[64,256]{1,0:T(8,128)(2,1)S(1)}, bf16[64,256]{1,0:T(8,128)(2,1)S(1)}, u32[]{:S(2)}, u32[]{:S(2)}) collective-permute-start(bf16[64,256]{1,0:T(8,128)(2,1)S(1)} %get-tuple-element.65), channel_id=1, source_target_pairs={{0,2},{1,3},{2,4},{3,5},{4,6},{5,7},{6,0},{7,1},{8,10},{9,11},{10,... | collective-permute-start | bytes 98312 | tf_op jit(solution)/shard_map/cache_terms/ppermute | solution.py:313
  92.0 2.9 %collective-permute-done.9.refs_1_ = bf16[64,256]{1,0:T(8,128)(2,1)S(1)} collective-permute-done((bf16[64,256]{1,0:T(8,128)(2,1)S(1)}, bf16[64,256]{1,0:T(8,128)(2,1)S(1)}, u32[]{:S(2)}, u32[]{:S(2)}) %collective-permute-start.9) | collective-permute-done | bytes 32800 | tf_op jit(solution)/shard_map/cache_terms/ppermute | solution.py:313
  95.0 1.2 %finish.1 = (bf16[16,1024]{1,0:T(8,128)(2,1)}, bf16[64,512]{1,0:T(8,128)(2,1)}, bf16[64,512]{1,0:T(8,128)(2,1)}) custom-call(s32[14]{0:T(128)S(1)} %stack.73.place, bf16[16,16,1024]{2,1,0:T(8,128)(2,1)S(1)} %all-to-all-done.2.terms_ref, bf16[64,256]{1,0:T(8,128)(2,1)S(1)} %get-tuple-element.59.refs_0_, bf16[64,256]{1,0:T(8,128)(2,1)S(1)} %collective-permute-done.9.refs_1_, ...), custom_call_target="tpu_custom_call" | custom-call | tf_op jit(solution)/shard_map/finish/pallas_call | solution.py:41
  (28 shorter events, 2.1 us)
Async XLA Ops:
  0.6 15.7 %copy-start.4 = (bf16[16,512]{1,0:T(8,128)(2,1)S(1)}, bf16[16,512]{1,0:T(8,128)(2,1)}, u32[]{:S(2)}) copy-start(bf16[16,512]{1,0:T(8,128)(2,1)} %param.11) | copy-start | bytes 49156
  0.6 21.5 %copy-start = (bf16[512,1024]{1,0:T(8,128)(2,1)S(1)}, bf16[512,1024]{1,0:T(8,128)(2,1)}, u32[]{:S(2)}) copy-start(bf16[512,1024]{1,0:T(8,128)(2,1)} %query_ref.3) | copy-start | bytes 3145732
  1.8 14.5 %collective-permute-start.1 = (bf16[512,128]{1,0:T(8,128)(2,1)S(1)}, bf16[512,128]{1,0:T(8,128)(2,1)S(1)}, u32[]{:S(2)}, u32[]{:S(2)}) collective-permute-start(bf16[512,128]{1,0:T(8,128)(2,1)S(1)} %dynamic-slice_select_fusion), channel_id=1, source_target_pairs={{0,128},{128,0},{1,129},{129,1},{2,130},{130,2},{3,131},{131,3},{4... | collective-permute-start | bytes 393224 | tf_op jit(solution)/shard_map/cache_pair/ppermute | solution.py:307
  9.6 6.7 %collective-permute-start = (bf16[16,512]{1,0:T(8,128)(2,1)}, bf16[16,512]{1,0:T(8,128)(2,1)S(1)}, u32[]{:S(2)}, u32[]{:S(2)}) collective-permute-start(bf16[16,512]{1,0:T(8,128)(2,1)} %param.11), channel_id=1, source_target_pairs={{0,128},{128,0},{1,129},{129,1},{2,130},{130,2},{3,131},{131,3},{4... | collective-permute-start | bytes 49160 | tf_op jit(solution)/shard_map/gradient_rows/ppermute | solution.py:307
  14.6 39.5 %copy-start.2 = (bf16[512,512]{1,0:T(8,128)(2,1)S(1)}, bf16[512,512]{1,0:T(8,128)(2,1)}, u32[]{:S(2)}) copy-start(bf16[512,512]{1,0:T(8,128)(2,1)} %value_ref.1) | copy-start | bytes 1572868
  14.7 39.5 %copy-start.3 = (s32[512]{0:T(512)S(1)}, s32[512]{0:T(512)}, u32[]{:S(2)}) copy-start(s32[512]{0:T(512)} %param.12) | copy-start | bytes 6148
  16.3 3.1 %collective-permute-start.2 = (bf16[2,16,512]{2,1,0:T(8,128)(2,1)S(1)}, bf16[2,16,512]{2,1,0:T(8,128)(2,1)S(1)}, u32[]{:S(2)}, u32[]{:S(2)}) collective-permute-start(bf16[2,16,512]{2,1,0:T(8,128)(2,1)S(1)} %get-tuple-element.68), channel_id=1, source_target_pairs={{0,1},{1,0},{2,3},{3,2},{4,5},{5,4},{6,7},{7,6},{8,9},{9,8},{10,11... | collective-permute-start | bytes 98312 | tf_op jit(solution)/shard_map/gradient_rows/ppermute | solution.py:310
  18.5 3.6 %collective-permute-start.6 = (bf16[512,128]{1,0:T(8,128)(2,1)S(1)}, bf16[512,128]{1,0:T(8,128)(2,1)S(1)}, u32[]{:S(2)}, u32[]{:S(2)}) collective-permute-start(bf16[512,128]{1,0:T(8,128)(2,1)S(1)} %collective-permute-done.1.straight), channel_id=1, source_target_pairs={{0,1},{1,0},{2,3},{3,2},{4,5},{5,4},{6,7},{7,6},{8,9},{9,8},{10,11... | collective-permute-start | bytes 393224 | tf_op jit(solution)/shard_map/gradient_rows/ppermute | solution.py:310
  19.4 4.7 %collective-permute-start.5 = (bf16[2,2,16,512]{3,2,1,0:T(8,128)(2,1)S(1)}, bf16[2,2,16,512]{3,2,1,0:T(8,128)(2,1)S(1)}, u32[]{:S(2)}, u32[]{:S(2)}) collective-permute-start(bf16[2,2,16,512]{3,2,1,0:T(8,128)(2,1)S(1)} %pad_maximum_fusion.refs_0_), channel_id=1, source_target_pairs={{0,6},{1,7},{2,0},{3,1},{4,2},{5,3},{6,4},{7,5},{8,14},{9,15},{10,... | collective-permute-start | bytes 196616 | tf_op jit(solution)/shard_map/gradient_rows/ppermute | solution.py:313
  21.1 7.3 %collective-permute-start.4 = (bf16[2,2,16,512]{3,2,1,0:T(8,128)(2,1)S(1)}, bf16[2,2,16,512]{3,2,1,0:T(8,128)(2,1)S(1)}, u32[]{:S(2)}, u32[]{:S(2)}) collective-permute-start(bf16[2,2,16,512]{3,2,1,0:T(8,128)(2,1)S(1)} %pad_maximum_fusion.refs_0_), channel_id=1, source_target_pairs={{0,4},{1,5},{2,6},{3,7},{4,0},{5,1},{6,2},{7,3},{8,12},{9,13},{10,... | collective-permute-start | bytes 196616 | tf_op jit(solution)/shard_map/gradient_rows/ppermute | solution.py:313
  21.3 7.1 %collective-permute-start.3 = (bf16[2,2,16,512]{3,2,1,0:T(8,128)(2,1)S(1)}, bf16[2,2,16,512]{3,2,1,0:T(8,128)(2,1)S(1)}, u32[]{:S(2)}, u32[]{:S(2)}) collective-permute-start(bf16[2,2,16,512]{3,2,1,0:T(8,128)(2,1)S(1)} %pad_maximum_fusion.refs_0_), channel_id=1, source_target_pairs={{0,2},{1,3},{2,4},{3,5},{4,6},{5,7},{6,0},{7,1},{8,10},{9,11},{10,... | collective-permute-start | bytes 196616 | tf_op jit(solution)/shard_map/gradient_rows/ppermute | solution.py:313
  31.4 36.6 %copy-start.1 = (bf16[512,512]{1,0:T(8,128)(2,1)S(1)}, bf16[512,512]{1,0:T(8,128)(2,1)}, u32[]{:S(2)}) copy-start(bf16[512,512]{1,0:T(8,128)(2,1)} %key_ref.1) | copy-start | bytes 1572868
  72.7 3.9 %collective-permute-start.7 = (bf16[2,4,64,256]{3,2,1,0:T(8,128)(2,1)S(1)}, bf16[2,4,64,256]{3,2,1,0:T(8,128)(2,1)S(1)}, u32[]{:S(2)}, u32[]{:S(2)}) collective-permute-start(bf16[2,4,64,256]{3,2,1,0:T(8,128)(2,1)S(1)} %get-tuple-element.57), channel_id=1, source_target_pairs={{0,1},{1,0},{2,3},{3,2},{4,5},{5,4},{6,7},{7,6},{8,9},{9,8},{10,11... | collective-permute-start | bytes 786440 | tf_op jit(solution)/shard_map/cache_terms/ppermute | solution.py:310
  76.7 8.7 %collective-permute-start.8 = (bf16[4,64,256]{2,1,0:T(8,128)(2,1)S(1)}, bf16[4,64,256]{2,1,0:T(8,128)(2,1)S(1)}, u32[]{:S(2)}, u32[]{:S(2)}) collective-permute-start(bf16[4,64,256]{2,1,0:T(8,128)(2,1)S(1)} %fusion.2), channel_id=1, source_target_pairs={{0,128},{128,0},{1,129},{129,1},{2,130},{130,2},{3,131},{131,3},{4... | collective-permute-start | bytes 393224 | tf_op jit(solution)/shard_map/cache_terms/ppermute | solution.py:307
  80.0 15.0 %all-to-all-start.2 = ((bf16[16,16,1024]{2,1,0:T(8,128)(2,1)}), bf16[16,16,1024]{2,1,0:T(8,128)(2,1)S(1)}, u32[]{:S(2)}, u32[]{:S(2)}) async-start(bf16[16,16,1024]{2,1,0:T(8,128)(2,1)} %get-tuple-element.55), calls=%async_computation.2 | async-start | bytes 1048576 | tf_op jit(solution)/shard_map/all_to_all | solution.py:409
  85.5 5.9 %collective-permute-start.11 = (bf16[64,256]{1,0:T(8,128)(2,1)S(1)}, bf16[64,256]{1,0:T(8,128)(2,1)S(1)}, u32[]{:S(2)}, u32[]{:S(2)}) collective-permute-start(bf16[64,256]{1,0:T(8,128)(2,1)S(1)} %get-tuple-element.63), channel_id=1, source_target_pairs={{0,6},{1,7},{2,0},{3,1},{4,2},{5,3},{6,4},{7,5},{8,14},{9,15},{10,... | collective-permute-start | bytes 98312 | tf_op jit(solution)/shard_map/cache_terms/ppermute | solution.py:313
  88.1 4.0 %collective-permute-start.10 = (bf16[64,256]{1,0:T(8,128)(2,1)S(1)}, bf16[64,256]{1,0:T(8,128)(2,1)S(1)}, u32[]{:S(2)}, u32[]{:S(2)}) collective-permute-start(bf16[64,256]{1,0:T(8,128)(2,1)S(1)} %get-tuple-element.64), channel_id=1, source_target_pairs={{0,4},{1,5},{2,6},{3,7},{4,0},{5,1},{6,2},{7,3},{8,12},{9,13},{10,... | collective-permute-start | bytes 98312 | tf_op jit(solution)/shard_map/cache_terms/ppermute | solution.py:313
  90.1 4.9 %collective-permute-start.9 = (bf16[64,256]{1,0:T(8,128)(2,1)S(1)}, bf16[64,256]{1,0:T(8,128)(2,1)S(1)}, u32[]{:S(2)}, u32[]{:S(2)}) collective-permute-start(bf16[64,256]{1,0:T(8,128)(2,1)S(1)} %get-tuple-element.65), channel_id=1, source_target_pairs={{0,2},{1,3},{2,4},{3,5},{4,6},{5,7},{6,0},{7,1},{8,10},{9,11},{10,... | collective-permute-start | bytes 98312 | tf_op jit(solution)/shard_map/cache_terms/ppermute | solution.py:313

commit v7 on v6

--- a/solution.py
+++ b/solution.py
@@ -68,14 +68,26 @@
     return pl.ds(pl.multiple_of(index * width, width), width)
 
 
-def project_kernel(place, *refs):
-    pieces, weight_ref, out_ref = refs[:-2], refs[-2], refs[-1]
-    cores, lines, rows, width = pieces[0].shape
+def project_pieces(steps, place, pieces, weight_ref):
     total = None
-    for index in range(len(pieces) * cores):
-        piece = pieces[index // cores][index % cores].reshape(lines * rows, width)
-        term = dot(weight_ref[:, columns(place[BLOCKS + index], width)], piece, ROWS)
-        total = term if total is None else total + term
+    for step, piece in zip(steps, pieces):
+        cores, lines, rows, width = piece.shape
+        for core in range(cores):
+            block = place[BLOCKS + step * cores + core]
+            rows_here = piece[core].reshape(lines * rows, width)
+            term = dot(weight_ref[:, columns(block, width)], rows_here, ROWS)
+            total = term if total is None else total + term
+    return total
+
+
+def project_first_kernel(steps, place, *refs):
+    pieces, weight_ref, partial_ref = refs[:-2], refs[-2], refs[-1]
+    partial_ref[...] = project_pieces(steps, place, pieces, weight_ref)
+
+
+def project_kernel(steps, place, *refs):
+    pieces, weight_ref, partial_ref, out_ref = refs[:-3], refs[-3], refs[-2], refs[-1]
+    total = partial_ref[...] + project_pieces(steps, place, pieces, weight_ref)
     result = total.T.astype(BF)
     for copy in range(out_ref.shape[0]):
         out_ref[copy] = result
@@ -358,13 +370,24 @@
         cost=score_cost,
         held=(0,),
     )
-    all_rows, straight, crossed, expo_other, peak_other, total_other = lax.optimization_barrier(
-        (all_rows, straight, crossed, expo_other, peak_other, total_other)
+    early, late = (0, chips - 1), tuple(range(1, chips - 1))
+    (partial,) = call(
+        functools.partial(project_first_kernel, early),
+        "project_first",
+        (place, *[all_rows[step] for step in early], in_vmem(weight)),
+        [((local_heads * HD, lines * rows), F32)],
+        cost=score_cost,
+    )
+    late_rows = [all_rows[step] for step in late]
+    late_rows, partial, straight, crossed, expo_other, peak_other, total_other = (
+        lax.optimization_barrier(
+            (late_rows, partial, straight, crossed, expo_other, peak_other, total_other)
+        )
     )
     (gathered,) = call(
-        project_kernel,
+        functools.partial(project_kernel, late),
         "project",
-        (place, *all_rows, in_vmem(weight)),
+        (place, *late_rows, in_vmem(weight), partial),
         [((groups, lines * rows, local_heads * HD), BF)],
     )
     with jax.named_scope("head_gradients"):

time: 96.5 us -> 95.4 us (0.989)
  waiting for transfers between devices: 13.3 us -> 11.5 us
    ppermute x6, waiting for transfers between devices: 7.83 us -> 6.05 us  [to_chip(): lax.ppermute(value, 'tp', [(i, (i + 2 * step) % parts) for i in range(par...]
    pallas_call x6 -> x7, Pallas kernels: 17.3 us -> 18.1 us  [call(): pl.pallas_call(kernel, in_specs=[SMEM] + [HBM if i in streamed else VMEM...]
  transfers between devices with their start and end apart: 13 -> 13, of which waited for: 7 -> 8; matrix products, arithmetic and copies ran while one was open for 0% -> 0% of each run, Pallas kernels for 6% -> 8%
where the time goes in v7:
time: 95.4 us; the launch traced here: 95.1 us
  blocking collectives  34.3 us (36%)
  starting transfers between devices  28.5 us (30%)
  Pallas kernels  18.1 us (19%)
  waiting for transfers between devices  11.5 us (12%)
  between operations  1.49 us (2%)
  other arithmetic  1.12 us (1%)
    all_to_all x1, blocking collectives, on_device(): gathered = lax.all_to_all(gathered, 'xy', 0, 0)  22.8 us
    pallas_call x7, Pallas kernels, call(): pl.pallas_call(kernel, in_specs=[SMEM] + [HBM if i in streamed else VMEM...  18.1 us
    all_to_all x1, blocking collectives, on_device(): stats = lax.all_to_all(stats, 'xy', 0, 0)  11.6 us
    ppermute x3, starting transfers between devices, to_pair(): return lax.ppermute(value, 'zh', [(0, 1), (1, 0)])  11.2 us
    ppermute x6, starting transfers between devices, to_chip(): lax.ppermute(value, 'tp', [(i, (i + 2 * step) % parts) for i in range(par...  8.64 us
    ppermute x6, waiting for transfers between devices, to_chip(): lax.ppermute(value, 'tp', [(i, (i + 2 * step) % parts) for i in range(par...  6.05 us
    ppermute x3, starting transfers between devices, to_core(): return lax.ppermute(value, 'tp', [(i, i ^ 1) for i in range(parts)])  5.09 us
    all_to_all x1, starting transfers between devices, on_device(): query_terms = lax.all_to_all(query_part, 'xy', 0, 0)  3.57 us
  transfers between devices with their start and end apart: 13, of which 8 were waited for; matrix products, arithmetic and copies ran while one was open for 0% of the time, Pallas kernels for 8%

profile of v7, /device:TPU:1, one launch (start us, length us, event | category | flops | bytes accessed | tf_op | source)
XLA Modules:
  0.0 95.1 jit_solution(15980661748162361289)
XLA Ops:
  0.7 1.0 %dynamic-slice_select_fusion = bf16[512,128]{1,0:T(8,128)(2,1)S(1)} fusion(bf16[512,512]{1,0:T(8,128)(2,1)} %value_ref.1, s32[]{:T(128)S(6)} %select_n.99, bf16[512,512]{1,0:T(8,128)(2,1)} %key_ref.1, pred[]{:T(512)S(6)} %eq.24), kind=kLoop, calls=%fused_computation.6 | loop fusion | flops 65536 | bytes 393221 | tf_op jit(solution)/shard_map/cache_pair/jit(_where)/select_n | solution.py:352
  1.7 7.8 %collective-permute-start.1 = (bf16[512,128]{1,0:T(8,128)(2,1)S(1)}, bf16[512,128]{1,0:T(8,128)(2,1)S(1)}, u32[]{:S(2)}, u32[]{:S(2)}) collective-permute-start(bf16[512,128]{1,0:T(8,128)(2,1)S(1)} %dynamic-slice_select_fusion), channel_id=1, source_target_pairs={{0,128},{128,0},{1,129},{129,1},{2,130},{130,2},{3,131},{131,3},{4... | collective-permute-start | bytes 393224 | tf_op jit(solution)/shard_map/cache_pair/ppermute | solution.py:319
  10.4 4.2 %own_scores.1 = (f32[8,512,256]{2,1,0:T(8,128)S(1)}, f32[8,256]{1,0:T(8,128)S(1)}, f32[8,256]{1,0:T(8,128)S(1)}, bf16[1024,4096]{1,0:T(8,128)(2,1)S(1)}) custom-call(s32[14]{0:T(128)S(1)} %stack.73.place, bf16[512,1024]{1,0:T(8,128)(2,1)} %query_ref.3, bf16[512,512]{1,0:T(8,128)(2,1)} %key_ref.1, bf16[1024,4096]{1,0:T(8,128)(2,1)} %weight_in.1), custom_call_target="tpu_custom_call" | custom-call | flops 268435456 | bytes 4194304 | tf_op jit(solution)/shard_map/own_scores/pallas_call | solution.py:41
  14.6 1.7 %collective-permute-done = bf16[16,512]{1,0:T(8,128)(2,1)S(1)} collective-permute-done((bf16[16,512]{1,0:T(8,128)(2,1)}, bf16[16,512]{1,0:T(8,128)(2,1)S(1)}, u32[]{:S(2)}, u32[]{:S(2)}) %collective-permute-start) | collective-permute-done | bytes 16416 | tf_op jit(solution)/shard_map/gradient_rows/ppermute | solution.py:319
  16.2 2.2 %collective-permute-start.2 = (bf16[2,16,512]{2,1,0:T(8,128)(2,1)S(1)}, bf16[2,16,512]{2,1,0:T(8,128)(2,1)S(1)}, u32[]{:S(2)}, u32[]{:S(2)}) collective-permute-start(bf16[2,16,512]{2,1,0:T(8,128)(2,1)S(1)} %get-tuple-element.66), channel_id=1, source_target_pairs={{0,1},{1,0},{2,3},{3,2},{4,5},{5,4},{6,7},{7,6},{8,9},{9,8},{10,11... | collective-permute-start | bytes 98312 | tf_op jit(solution)/shard_map/gradient_rows/ppermute | solution.py:322
  19.3 1.7 %collective-permute-start.5 = (bf16[2,2,16,512]{3,2,1,0:T(8,128)(2,1)S(1)}, bf16[2,2,16,512]{3,2,1,0:T(8,128)(2,1)S(1)}, u32[]{:S(2)}, u32[]{:S(2)}) collective-permute-start(bf16[2,2,16,512]{3,2,1,0:T(8,128)(2,1)S(1)} %pad_maximum_fusion.refs_0_), channel_id=1, source_target_pairs={{0,6},{1,7},{2,0},{3,1},{4,2},{5,3},{6,4},{7,5},{8,14},{9,15},{10,... | collective-permute-start | bytes 196616 | tf_op jit(solution)/shard_map/gradient_rows/ppermute | solution.py:325
  22.5 1.8 %project_first.1.refs_3_ = f32[1024,32]{1,0:T(8,128)S(1)} custom-call(s32[14]{0:T(128)S(1)} %stack.73.place, bf16[2,2,16,512]{3,2,1,0:T(8,128)(2,1)S(1)} %pad_maximum_fusion.refs_0_, bf16[2,2,16,512]{3,2,1,0:T(8,128)(2,1)S(1)} %collective-permute-done.5.refs_1_, bf16[1024,4096]{1,0:T(8,128)(2,1)S(1)} %get-tuple-element.34.refs_2_), custom_call_target="tpu_custom_call" | custom-call | flops 268435456 | bytes 4194304 | tf_op jit(solution)/shard_map/project_first/pallas_call | solution.py:41
  24.3 2.1 %other_scores.1 = (f32[8,512,256]{2,1,0:T(8,128)S(1)}, f32[8,256]{1,0:T(8,128)S(1)}, f32[8,256]{1,0:T(8,128)S(1)}) custom-call(s32[14]{0:T(128)S(1)} %stack.73.place, bf16[512,1024]{1,0:T(8,128)(2,1)S(1)} %copy-done, bf16[512,128]{1,0:T(8,128)(2,1)S(1)} %collective-permute-done.1.straight, bf16[512,128]{1,0:T(8,128)(2,1)S(1)} %collective-permute-done.6.crossed), custom_call_target="tpu_custom_call" | custom-call | flops 268435456 | bytes 4194304 | tf_op jit(solution)/shard_map/other_scores/pallas_call | solution.py:41
  26.3 2.0 %collective-permute-done.4.refs_1_ = bf16[2,2,16,512]{3,2,1,0:T(8,128)(2,1)S(1)} collective-permute-done((bf16[2,2,16,512]{3,2,1,0:T(8,128)(2,1)S(1)}, bf16[2,2,16,512]{3,2,1,0:T(8,128)(2,1)S(1)}, u32[]{:S(2)}, u32[]{:S(2)}) %collective-permute-start.4) | collective-permute-done | bytes 65568 | tf_op jit(solution)/shard_map/gradient_rows/ppermute | solution.py:325
  28.3 1.9 %project.1 = bf16[16,32,1024]{2,1,0:T(8,128)(2,1)S(1)} custom-call(s32[14]{0:T(128)S(1)} %stack.73.place, bf16[2,2,16,512]{3,2,1,0:T(8,128)(2,1)S(1)} %collective-permute-done.3.refs_0_, bf16[2,2,16,512]{3,2,1,0:T(8,128)(2,1)S(1)} %collective-permute-done.4.refs_1_, bf16[1024,4096]{1,0:T(8,128)(2,1)S(1)} %get-tuple-element.34.refs_2_, ...), custom_call_target="tpu_custom_call" | custom-call | tf_op jit(solution)/shard_map/project/pallas_call | solution.py:41
  30.2 22.8 %all_to_all.15.gathered_ref = bf16[16,32,1024]{2,1,0:T(8,128)(2,1)S(1)} all-to-all(bf16[16,32,1024]{2,1,0:T(8,128)(2,1)S(1)} %project.1), channel_id=1, replica_groups=mesh['zh'=2,'xy'=16,'tp'=8] {'xy'}, dimensions={0} | all-to-all | bytes 2097152 | tf_op jit(solution)/shard_map/head_gradients/all_to_all | solution.py:394
  53.0 2.2 %deltas.1 = (bf16[256,1024]{1,0:T(8,128)(2,1)S(1)}, f32[16,3,8,256]{3,2,1,0:T(8,128)S(1)}, f32[8,2,512,256]{3,2,1,0:T(8,128)S(1)}) custom-call(s32[14]{0:T(128)S(1)} %stack.73.place, s32[1,512]{1,0:T(1,128)S(1)} %bitcast.35, bf16[16,32,1024]{2,1,0:T(8,128)(2,1)S(1)} %all_to_all.15.gathered_ref, bf16[512,512]{1,0:T(8,128)(2,1)S(1)} %copy-done.2, ...), custom_call_target="tpu_custom_call" | custom-call | tf_op jit(solution)/shard_map/deltas/pallas_call | solution.py:41
  55.2 11.6 %all_to_all.16.stats_ref = f32[16,3,8,256]{3,2,1,0:T(8,128)S(1)} all-to-all(f32[16,3,8,256]{3,2,1,0:T(8,128)S(1)} %get-tuple-element.50), channel_id=1, replica_groups=mesh['zh'=2,'xy'=16,'tp'=8] {'xy'}, dimensions={0} | all-to-all | bytes 786432 | tf_op jit(solution)/shard_map/row_stats/all_to_all | solution.py:413
  66.8 4.8 %gradients.1 = (bf16[16,16,1024]{2,1,0:T(8,128)(2,1)}, f32[2,4,64,256]{3,2,1,0:T(8,128)S(1)}, bf16[2,4,64,256]{3,2,1,0:T(8,128)(2,1)S(1)}) custom-call(s32[14]{0:T(128)S(1)} %stack.73.place, f32[16,3,8,256]{3,2,1,0:T(8,128)S(1)} %all_to_all.16.stats_ref, bf16[512,1024]{1,0:T(8,128)(2,1)S(1)} %copy-done, bf16[256,1024]{1,0:T(8,128)(2,1)S(1)} %get-tuple-element.51.grad_ref, ...), custom_call_target="tpu_custom_call" | custom-call | tf_op jit(solution)/shard_map/gradients/pallas_call | solution.py:41
  71.5 2.8 %collective-permute-start.7 = (bf16[2,4,64,256]{3,2,1,0:T(8,128)(2,1)S(1)}, bf16[2,4,64,256]{3,2,1,0:T(8,128)(2,1)S(1)}, u32[]{:S(2)}, u32[]{:S(2)}) collective-permute-start(bf16[2,4,64,256]{3,2,1,0:T(8,128)(2,1)S(1)} %get-tuple-element.55), channel_id=1, source_target_pairs={{0,1},{1,0},{2,3},{3,2},{4,5},{5,4},{6,7},{7,6},{8,9},{9,8},{10,11... | collective-permute-start | bytes 786440 | tf_op jit(solution)/shard_map/cache_terms/ppermute | solution.py:322
  74.3 1.2 %collective-permute-done.7 = bf16[2,4,64,256]{3,2,1,0:T(8,128)(2,1)S(1)} collective-permute-done((bf16[2,4,64,256]{3,2,1,0:T(8,128)(2,1)S(1)}, bf16[2,4,64,256]{3,2,1,0:T(8,128)(2,1)S(1)}, u32[]{:S(2)}, u32[]{:S(2)}) %collective-permute-start.7) | collective-permute-done | bytes 262176 | tf_op jit(solution)/shard_map/cache_terms/ppermute | solution.py:322
  75.6 3.3 %collective-permute-start.8 = (bf16[4,64,256]{2,1,0:T(8,128)(2,1)S(1)}, bf16[4,64,256]{2,1,0:T(8,128)(2,1)S(1)}, u32[]{:S(2)}, u32[]{:S(2)}) collective-permute-start(bf16[4,64,256]{2,1,0:T(8,128)(2,1)S(1)} %fusion.2), channel_id=1, source_target_pairs={{0,128},{128,0},{1,129},{129,1},{2,130},{130,2},{3,131},{131,3},{4... | collective-permute-start | bytes 393224 | tf_op jit(solution)/shard_map/cache_terms/ppermute | solution.py:319
  78.8 3.6 %all-to-all-start.2 = ((bf16[16,16,1024]{2,1,0:T(8,128)(2,1)}), bf16[16,16,1024]{2,1,0:T(8,128)(2,1)S(1)}, u32[]{:S(2)}, u32[]{:S(2)}) async-start(bf16[16,16,1024]{2,1,0:T(8,128)(2,1)} %get-tuple-element.53), calls=%async_computation.2 | async-start | bytes 1048576 | tf_op jit(solution)/shard_map/all_to_all | solution.py:432
  82.4 1.8 %collective-permute-done.8 = bf16[4,64,256]{2,1,0:T(8,128)(2,1)S(1)} collective-permute-done((bf16[4,64,256]{2,1,0:T(8,128)(2,1)S(1)}, bf16[4,64,256]{2,1,0:T(8,128)(2,1)S(1)}, u32[]{:S(2)}, u32[]{:S(2)}) %collective-permute-start.8) | collective-permute-done | bytes 131104 | tf_op jit(solution)/shard_map/cache_terms/ppermute | solution.py:319
  84.4 4.7 %collective-permute-start.11 = (bf16[64,256]{1,0:T(8,128)(2,1)S(1)}, bf16[64,256]{1,0:T(8,128)(2,1)S(1)}, u32[]{:S(2)}, u32[]{:S(2)}) collective-permute-start(bf16[64,256]{1,0:T(8,128)(2,1)S(1)} %get-tuple-element.61), channel_id=1, source_target_pairs={{0,6},{1,7},{2,0},{3,1},{4,2},{5,3},{6,4},{7,5},{8,14},{9,15},{10,... | collective-permute-start | bytes 98312 | tf_op jit(solution)/shard_map/cache_terms/ppermute | solution.py:325
  89.0 1.3 %collective-permute-start.9 = (bf16[64,256]{1,0:T(8,128)(2,1)S(1)}, bf16[64,256]{1,0:T(8,128)(2,1)S(1)}, u32[]{:S(2)}, u32[]{:S(2)}) collective-permute-start(bf16[64,256]{1,0:T(8,128)(2,1)S(1)} %get-tuple-element.63), channel_id=1, source_target_pairs={{0,2},{1,3},{2,4},{3,5},{4,6},{5,7},{6,0},{7,1},{8,10},{9,11},{10,... | collective-permute-start | bytes 98312 | tf_op jit(solution)/shard_map/cache_terms/ppermute | solution.py:325
  90.3 2.7 %collective-permute-done.10.refs_2_ = bf16[64,256]{1,0:T(8,128)(2,1)S(1)} collective-permute-done((bf16[64,256]{1,0:T(8,128)(2,1)S(1)}, bf16[64,256]{1,0:T(8,128)(2,1)S(1)}, u32[]{:S(2)}, u32[]{:S(2)}) %collective-permute-start.10) | collective-permute-done | bytes 32800 | tf_op jit(solution)/shard_map/cache_terms/ppermute | solution.py:325
  93.0 0.9 collective-permute-done.9.refs_1_
  93.9 1.2 %finish.1 = (bf16[16,1024]{1,0:T(8,128)(2,1)}, bf16[64,512]{1,0:T(8,128)(2,1)}, bf16[64,512]{1,0:T(8,128)(2,1)}) custom-call(s32[14]{0:T(128)S(1)} %stack.73.place, bf16[16,16,1024]{2,1,0:T(8,128)(2,1)S(1)} %all-to-all-done.2.terms_ref, bf16[64,256]{1,0:T(8,128)(2,1)S(1)} %get-tuple-element.57.refs_0_, bf16[64,256]{1,0:T(8,128)(2,1)S(1)} %collective-permute-done.9.refs_1_, ...), custom_call_target="tpu_custom_call" | custom-call | tf_op jit(solution)/shard_map/finish/pallas_call | solution.py:41
  (29 shorter events, 2.7 us)
Async XLA Ops:
  0.6 15.6 %copy-start.4 = (bf16[16,512]{1,0:T(8,128)(2,1)S(1)}, bf16[16,512]{1,0:T(8,128)(2,1)}, u32[]{:S(2)}) copy-start(bf16[16,512]{1,0:T(8,128)(2,1)} %param.11) | copy-start | bytes 49156
  1.7 14.5 %collective-permute-start.1 = (bf16[512,128]{1,0:T(8,128)(2,1)S(1)}, bf16[512,128]{1,0:T(8,128)(2,1)S(1)}, u32[]{:S(2)}, u32[]{:S(2)}) collective-permute-start(bf16[512,128]{1,0:T(8,128)(2,1)S(1)} %dynamic-slice_select_fusion), channel_id=1, source_target_pairs={{0,128},{128,0},{1,129},{129,1},{2,130},{130,2},{3,131},{131,3},{4... | collective-permute-start | bytes 393224 | tf_op jit(solution)/shard_map/cache_pair/ppermute | solution.py:319
  9.5 6.7 %collective-permute-start = (bf16[16,512]{1,0:T(8,128)(2,1)}, bf16[16,512]{1,0:T(8,128)(2,1)S(1)}, u32[]{:S(2)}, u32[]{:S(2)}) collective-permute-start(bf16[16,512]{1,0:T(8,128)(2,1)} %param.11), channel_id=1, source_target_pairs={{0,128},{128,0},{1,129},{129,1},{2,130},{130,2},{3,131},{131,3},{4... | collective-permute-start | bytes 49160 | tf_op jit(solution)/shard_map/gradient_rows/ppermute | solution.py:319
  10.4 13.9 %copy-start = (bf16[512,1024]{1,0:T(8,128)(2,1)S(1)}, bf16[512,1024]{1,0:T(8,128)(2,1)}, u32[]{:S(2)}) copy-start(bf16[512,1024]{1,0:T(8,128)(2,1)} %query_ref.3) | copy-start | bytes 3145732
  16.2 3.1 %collective-permute-start.2 = (bf16[2,16,512]{2,1,0:T(8,128)(2,1)S(1)}, bf16[2,16,512]{2,1,0:T(8,128)(2,1)S(1)}, u32[]{:S(2)}, u32[]{:S(2)}) collective-permute-start(bf16[2,16,512]{2,1,0:T(8,128)(2,1)S(1)} %get-tuple-element.66), channel_id=1, source_target_pairs={{0,1},{1,0},{2,3},{3,2},{4,5},{5,4},{6,7},{7,6},{8,9},{9,8},{10,11... | collective-permute-start | bytes 98312 | tf_op jit(solution)/shard_map/gradient_rows/ppermute | solution.py:322
  18.4 5.8 %collective-permute-start.6 = (bf16[512,128]{1,0:T(8,128)(2,1)S(1)}, bf16[512,128]{1,0:T(8,128)(2,1)S(1)}, u32[]{:S(2)}, u32[]{:S(2)}) collective-permute-start(bf16[512,128]{1,0:T(8,128)(2,1)S(1)} %collective-permute-done.1.straight), channel_id=1, source_target_pairs={{0,1},{1,0},{2,3},{3,2},{4,5},{5,4},{6,7},{7,6},{8,9},{9,8},{10,11... | collective-permute-start | bytes 393224 | tf_op jit(solution)/shard_map/gradient_rows/ppermute | solution.py:322
  19.3 3.2 %collective-permute-start.5 = (bf16[2,2,16,512]{3,2,1,0:T(8,128)(2,1)S(1)}, bf16[2,2,16,512]{3,2,1,0:T(8,128)(2,1)S(1)}, u32[]{:S(2)}, u32[]{:S(2)}) collective-permute-start(bf16[2,2,16,512]{3,2,1,0:T(8,128)(2,1)S(1)} %pad_maximum_fusion.refs_0_), channel_id=1, source_target_pairs={{0,6},{1,7},{2,0},{3,1},{4,2},{5,3},{6,4},{7,5},{8,14},{9,15},{10,... | collective-permute-start | bytes 196616 | tf_op jit(solution)/shard_map/gradient_rows/ppermute | solution.py:325
  21.0 7.3 %collective-permute-start.4 = (bf16[2,2,16,512]{3,2,1,0:T(8,128)(2,1)S(1)}, bf16[2,2,16,512]{3,2,1,0:T(8,128)(2,1)S(1)}, u32[]{:S(2)}, u32[]{:S(2)}) collective-permute-start(bf16[2,2,16,512]{3,2,1,0:T(8,128)(2,1)S(1)} %pad_maximum_fusion.refs_0_), channel_id=1, source_target_pairs={{0,4},{1,5},{2,6},{3,7},{4,0},{5,1},{6,2},{7,3},{8,12},{9,13},{10,... | collective-permute-start | bytes 196616 | tf_op jit(solution)/shard_map/gradient_rows/ppermute | solution.py:325
  21.3 7.1 %collective-permute-start.3 = (bf16[2,2,16,512]{3,2,1,0:T(8,128)(2,1)S(1)}, bf16[2,2,16,512]{3,2,1,0:T(8,128)(2,1)S(1)}, u32[]{:S(2)}, u32[]{:S(2)}) collective-permute-start(bf16[2,2,16,512]{3,2,1,0:T(8,128)(2,1)S(1)} %pad_maximum_fusion.refs_0_), channel_id=1, source_target_pairs={{0,2},{1,3},{2,4},{3,5},{4,6},{5,7},{6,0},{7,1},{8,10},{9,11},{10,... | collective-permute-start | bytes 196616 | tf_op jit(solution)/shard_map/gradient_rows/ppermute | solution.py:325
  24.2 28.8 %copy-start.2 = (bf16[512,512]{1,0:T(8,128)(2,1)S(1)}, bf16[512,512]{1,0:T(8,128)(2,1)}, u32[]{:S(2)}) copy-start(bf16[512,512]{1,0:T(8,128)(2,1)} %value_ref.1) | copy-start | bytes 1572868
  24.2 28.8 %copy-start.3 = (s32[512]{0:T(512)S(1)}, s32[512]{0:T(512)}, u32[]{:S(2)}) copy-start(s32[512]{0:T(512)} %param.12) | copy-start | bytes 6148
  30.2 36.6 %copy-start.1 = (bf16[512,512]{1,0:T(8,128)(2,1)S(1)}, bf16[512,512]{1,0:T(8,128)(2,1)}, u32[]{:S(2)}) copy-start(bf16[512,512]{1,0:T(8,128)(2,1)} %key_ref.1) | copy-start | bytes 1572868
  71.5 4.0 %collective-permute-start.7 = (bf16[2,4,64,256]{3,2,1,0:T(8,128)(2,1)S(1)}, bf16[2,4,64,256]{3,2,1,0:T(8,128)(2,1)S(1)}, u32[]{:S(2)}, u32[]{:S(2)}) collective-permute-start(bf16[2,4,64,256]{3,2,1,0:T(8,128)(2,1)S(1)} %get-tuple-element.55), channel_id=1, source_target_pairs={{0,1},{1,0},{2,3},{3,2},{4,5},{5,4},{6,7},{7,6},{8,9},{9,8},{10,11... | collective-permute-start | bytes 786440 | tf_op jit(solution)/shard_map/cache_terms/ppermute | solution.py:322
  75.6 8.7 %collective-permute-start.8 = (bf16[4,64,256]{2,1,0:T(8,128)(2,1)S(1)}, bf16[4,64,256]{2,1,0:T(8,128)(2,1)S(1)}, u32[]{:S(2)}, u32[]{:S(2)}) collective-permute-start(bf16[4,64,256]{2,1,0:T(8,128)(2,1)S(1)} %fusion.2), channel_id=1, source_target_pairs={{0,128},{128,0},{1,129},{129,1},{2,130},{130,2},{3,131},{131,3},{4... | collective-permute-start | bytes 393224 | tf_op jit(solution)/shard_map/cache_terms/ppermute | solution.py:319
  78.8 15.1 %all-to-all-start.2 = ((bf16[16,16,1024]{2,1,0:T(8,128)(2,1)}), bf16[16,16,1024]{2,1,0:T(8,128)(2,1)S(1)}, u32[]{:S(2)}, u32[]{:S(2)}) async-start(bf16[16,16,1024]{2,1,0:T(8,128)(2,1)} %get-tuple-element.53), calls=%async_computation.2 | async-start | bytes 1048576 | tf_op jit(solution)/shard_map/all_to_all | solution.py:432
  84.4 5.9 %collective-permute-start.11 = (bf16[64,256]{1,0:T(8,128)(2,1)S(1)}, bf16[64,256]{1,0:T(8,128)(2,1)S(1)}, u32[]{:S(2)}, u32[]{:S(2)}) collective-permute-start(bf16[64,256]{1,0:T(8,128)(2,1)S(1)} %get-tuple-element.61), channel_id=1, source_target_pairs={{0,6},{1,7},{2,0},{3,1},{4,2},{5,3},{6,4},{7,5},{8,14},{9,15},{10,... | collective-permute-start | bytes 98312 | tf_op jit(solution)/shard_map/cache_terms/ppermute | solution.py:325
  89.0 4.0 %collective-permute-start.10 = (bf16[64,256]{1,0:T(8,128)(2,1)S(1)}, bf16[64,256]{1,0:T(8,128)(2,1)S(1)}, u32[]{:S(2)}, u32[]{:S(2)}) collective-permute-start(bf16[64,256]{1,0:T(8,128)(2,1)S(1)} %get-tuple-element.62), channel_id=1, source_target_pairs={{0,4},{1,5},{2,6},{3,7},{4,0},{5,1},{6,2},{7,3},{8,12},{9,13},{10,... | collective-permute-start | bytes 98312 | tf_op jit(solution)/shard_map/cache_terms/ppermute | solution.py:325
  89.0 4.9 %collective-permute-start.9 = (bf16[64,256]{1,0:T(8,128)(2,1)S(1)}, bf16[64,256]{1,0:T(8,128)(2,1)S(1)}, u32[]{:S(2)}, u32[]{:S(2)}) collective-permute-start(bf16[64,256]{1,0:T(8,128)(2,1)S(1)} %get-tuple-element.63), channel_id=1, source_target_pairs={{0,2},{1,3},{2,4},{3,5},{4,6},{5,7},{6,0},{7,1},{8,10},{9,11},{10,... | collective-permute-start | bytes 98312 | tf_op jit(solution)/shard_map/cache_terms/ppermute | solution.py:325
